TPU v7x, 256 devices: a whole 4x4x8 slice. The times are simulated.
256 devices in a mesh: frame: 8 (over z), height: 16 (over x, y), head: 2 (over core).
Axes of the slice: x: 4, y: 4, z: 8, core: 2. Of those that a mesh axis runs over, the one named last changes fastest.
Arguments:
- q_raw: bfloat16 [16, 48, 80, 5120], P('frame', 'height', None, 'head'), may hold values from -8 to 8
- k_raw: bfloat16 [16, 48, 80, 5120], P('frame', 'height', None, 'head'), may hold values from -8 to 8
- v_in: bfloat16 [16, 48, 80, 5120], P('frame', 'height', None, 'head'), may hold values from -6 to 6
- q_gain: float32 [5120], P('head'), may hold values from 0.8 to 2
- k_gain: float32 [5120], P('head'), may hold values from 0.8 to 2
- window: int32 [40, 3], P('head'), may hold values from 0 to 9, as said below
Outputs:
- attended: bfloat16 [16, 48, 80, 5120], P('frame', 'height', None, 'head')
Inputs may be any that keep to these rules, and one draw needn't show every extreme that they name: window[h, 0] and window[h, 1] are 0 or 1, window[h, 2] lies in 0 to 9; some head has (1, 1, 9).
All inputs are finite; a program needn't handle non-finite values.
Results may differ from a plain program's by a relative error of at most 0.012.
Values may be sent and summed in bfloat16 or wider, within the bound.
No kernel may reach another device: no remote copies, remote signals or barrier semaphores. Data moves between devices by JAX's collectives and lax.ppermute only.
A program may use at most 128 MiB of HBM per device.

v0:
```python
import jax
import jax.numpy as jnp
from jax import lax
from jax.sharding import PartitionSpec as P

HD = 128
TILE_W = 8


epsilon_norm = 1e-06


def with_halo(block, sides, width):
    for axis, dim in sides:
        count = lax.axis_size(axis)
        forward = [(i, i + 1) for i in range(count - 1)]
        backward = [(target, source) for source, target in forward]
        low = lax.ppermute(
            lax.slice_in_dim(block, block.shape[dim] - width, None, axis=dim), axis, forward
        )
        high = lax.ppermute(lax.slice_in_dim(block, 0, width, axis=dim), axis, backward)
        block = jnp.concatenate([low, block, high], axis=dim)
    return block


def normalized(raw, square_sum, gain, width_total):
    inverse = lax.rsqrt(square_sum / width_total + epsilon_norm)
    return (raw.astype(jnp.float32) * inverse[..., None] * gain).astype(jnp.bfloat16)


def squares_of(raw):
    values = raw.astype(jnp.float32)
    return jnp.sum(values * values, axis=-1)


def body(q_raw, k_raw, v_in, q_gain, k_gain, window):
    frames_dev, rows_local, width_cols, channels = q_raw.shape
    width_total = channels * lax.axis_size("head")
    query_squares = squares_of(q_raw)
    key_squares = squares_of(k_raw)
    query_sum, key_sum = lax.psum((query_squares, key_squares), "head")
    key_normed = normalized(k_raw, key_sum, k_gain, width_total)
    stacked = jnp.stack((key_normed, v_in))
    extended = with_halo(stacked, (("frame", 1), ("height", 2)), 1)
    key_ext = extended[0]
    value_ext = extended[1]
    query_normed = normalized(q_raw, query_sum, q_gain, width_total)
    query_count = frames_dev * rows_local * width_cols
    key_count = (frames_dev + 2) * (rows_local + 2) * width_cols
    query_flat = query_normed.reshape(query_count, channels)
    key_flat = key_ext.reshape(key_count, channels)
    value_flat = value_ext.reshape(key_count, channels)
    frame_start = lax.axis_index("frame") * frames_dev
    row_start = lax.axis_index("height") * rows_local
    frame_total = frames_dev * lax.axis_size("frame")
    row_total = rows_local * lax.axis_size("height")
    query_ids = jnp.arange(query_count, dtype=jnp.int32)
    query_frame = frame_start + query_ids // (rows_local * width_cols)
    query_row = row_start + query_ids // width_cols % rows_local
    query_tile = query_ids % width_cols // TILE_W
    key_ids = jnp.arange(key_count, dtype=jnp.int32)
    key_frame = frame_start - 1 + key_ids // ((rows_local + 2) * width_cols)
    key_row = row_start - 1 + key_ids // width_cols % (rows_local + 2)
    key_tile = key_ids % width_cols // TILE_W
    key_valid = (
        (key_frame >= 0) & (key_frame < frame_total) & (key_row >= 0) & (key_row < row_total)
    )
    frame_gap = jnp.abs(query_frame[:, None] - key_frame[None, :])
    row_gap = jnp.abs(query_row[:, None] - key_row[None, :])
    tile_gap = jnp.abs(query_tile[:, None] - key_tile[None, :])
    pair_width = 2 * HD
    score_scale = HD ** (-0.5)

    def attend_group(group_index, output_buffer):
        start_col = group_index * pair_width
        query_block = lax.dynamic_slice_in_dim(query_flat, start_col, pair_width, 1).reshape(
            query_count, 2, HD
        )
        key_block = lax.dynamic_slice_in_dim(key_flat, start_col, pair_width, 1).reshape(
            key_count, 2, HD
        )
        value_block = lax.dynamic_slice_in_dim(value_flat, start_col, pair_width, 1).reshape(
            key_count, 2, HD
        )
        window_block = lax.dynamic_slice_in_dim(window, group_index * 2, 2, 0)
        visible = frame_gap[None, :, :] <= window_block[:, 0][:, None, None]
        visible = visible & (row_gap[None, :, :] <= window_block[:, 1][:, None, None])
        visible = visible & (tile_gap[None, :, :] <= window_block[:, 2][:, None, None])
        visible = visible & key_valid[None, None, :]
        scores = (
            jnp.einsum("qhd,khd->hqk", query_block, key_block, preferred_element_type=jnp.float32)
            * score_scale
        )
        scores = jnp.where(visible, scores, -jnp.inf)
        row_max = jnp.max(scores, axis=-1, keepdims=True)
        weights = jnp.exp(scores - row_max)
        denominator = jnp.sum(weights, axis=-1, keepdims=True)
        mixed = jnp.einsum(
            "hqk,khd->qhd",
            weights.astype(jnp.bfloat16),
            value_block,
            preferred_element_type=jnp.float32,
        )
        mixed = mixed / jnp.transpose(denominator, (1, 0, 2))
        mixed = mixed.astype(jnp.bfloat16).reshape(query_count, pair_width)
        return lax.dynamic_update_slice_in_dim(output_buffer, mixed, start_col, 1)

    initial = jnp.zeros((query_count, channels), jnp.bfloat16)
    result = lax.fori_loop(0, channels // pair_width, attend_group, initial)
    return result.reshape(frames_dev, rows_local, width_cols, channels)


def solution(mesh):
    placed = (
        P("frame", "height", None, "head"),
        P("frame", "height", None, "head"),
        P("frame", "height", None, "head"),
        P("head"),
        P("head"),
        P("head", None),
    )
    return jax.shard_map(
        body,
        mesh=mesh,
        in_specs=placed,
        out_specs=P("frame", "height", None, "head"),
        check_vma=False,
    )
```

profile of v0, /device:TPU:38, one launch (start us, length us, event | category | flops | bytes accessed | tf_op | source)
XLA Modules:
  0.0 332.0 jit_solution(4900768550472440863)
XLA Ops:
  9.9 3.8 %collective-permute-start = (bf16[2,1,3,80,2560]{4,3,2,1,0:T(8,128)(2,1)S(1)}, bf16[2,1,3,80,2560]{4,3,2,1,0:T(8,128)(2,1)S(1)}, u32[]{:S(2)}, u32[]{:S(2)}) collective-permute-start(bf16[2,1,3,80,2560]{4,3,2,1,0:T(8,128)(2,1)S(1)} %get-tuple-element.273), channel_id=1, source_target_pairs={{0,32},{32,64},{64,96},{96,128},{128,160},{160,192},{192,224},{1,3... | collective-permute-start | bytes 7372808 | tf_op jit(solution)/shard_map/ppermute | solution.py:18
  15.9 51.3 %collective-permute-done = bf16[2,1,3,80,2560]{4,3,2,1,0:T(8,128)(2,1)S(1)} collective-permute-done((bf16[2,1,3,80,2560]{4,3,2,1,0:T(8,128)(2,1)S(1)}, bf16[2,1,3,80,2560]{4,3,2,1,0:T(8,128)(2,1)S(1)}, u32[]{:S(2)}, u32[]{:S(2)}) %collective-permute-start) | collective-permute-done | bytes 2457632 | tf_op jit(solution)/shard_map/ppermute | solution.py:18
  67.2 3.7 %collective-permute-done.1 = bf16[2,1,3,80,2560]{4,3,2,1,0:T(8,128)(2,1)S(1)} collective-permute-done((bf16[2,1,3,80,2560]{4,3,2,1,0:T(8,128)(2,1)S(1)}, bf16[2,1,3,80,2560]{4,3,2,1,0:T(8,128)(2,1)S(1)}, u32[]{:S(2)}, u32[]{:S(2)}) %collective-permute-start.1) | collective-permute-done | bytes 2457632 | tf_op jit(solution)/shard_map/ppermute | solution.py:21
  71.0 3.4 %pad_maximum_fusion.4 = (bf16[2,4,1,80,2560]{4,3,2,1,0:T(8,128)(2,1)}, bf16[2,4,1,80,2560]{4,3,2,1,0:T(8,128)(2,1)}) fusion(bf16[2,1,3,80,2560]{4,3,2,1,0:T(8,128)(2,1)S(1)} %collective-permute-done.1, bf16[2,1,3,80,2560]{4,3,2,1,0:T(8,128)(2,1)S(1)} %collective-permute-done, bf16[1,2,3,80,2560]{4,3,2,1,0:T(8,128)(2,1)S(1)} %bitcast.67, ...), kind=kLoop, calls=%fused_computation.60 | loop fusion | flops 9830400 | bytes 16384000 | tf_op jit(solution)/shard_map/slice | solution.py:19
  74.5 3.5 %collective-permute-start.2 = (bf16[2,4,1,80,2560]{4,3,2,1,0:T(8,128)(2,1)}, bf16[2,4,1,80,2560]{4,3,2,1,0:T(8,128)(2,1)}, u32[]{:S(2)}, u32[]{:S(2)}) collective-permute-start(bf16[2,4,1,80,2560]{4,3,2,1,0:T(8,128)(2,1)} %get-tuple-element.271), channel_id=1, source_target_pairs={{0,2},{2,4},{4,6},{6,8},{8,10},{10,12},{12,14},{14,16},{16,18},{18... | collective-permute-start | bytes 9830408 | tf_op jit(solution)/shard_map/ppermute | solution.py:18
  78.0 4.6 %collective-permute-start.3 = (bf16[2,4,1,80,2560]{4,3,2,1,0:T(8,128)(2,1)}, bf16[2,4,1,80,2560]{4,3,2,1,0:T(8,128)(2,1)}, u32[]{:S(2)}, u32[]{:S(2)}) collective-permute-start(bf16[2,4,1,80,2560]{4,3,2,1,0:T(8,128)(2,1)} %get-tuple-element.272), channel_id=1, source_target_pairs={{2,0},{4,2},{6,4},{8,6},{10,8},{12,10},{14,12},{16,14},{18,16},{20... | collective-permute-start | bytes 9830408 | tf_op jit(solution)/shard_map/ppermute | solution.py:21
  82.7 3.9 %fusion.40 = bf16[2,3,80,2560]{3,2,1,0:T(8,128)(2,1)} fusion(bf16[2,3,80,2560]{3,2,1,0:T(8,128)(2,1)} %param.8, f32[2560]{0:T(1024)S(1)} %copy-done.9, f32[2,3,80]{2,1,0:T(4,128)S(1)} %get-tuple-element.275), kind=kLoop, calls=%fused_computation.54 | loop fusion | flops 4915200 | bytes 4927360 | tf_op jit(solution)/shard_map/convert_element_type | solution.py:28
  86.7 64.1 %collective-permute-done.2 = bf16[2,4,1,80,2560]{4,3,2,1,0:T(8,128)(2,1)} collective-permute-done((bf16[2,4,1,80,2560]{4,3,2,1,0:T(8,128)(2,1)}, bf16[2,4,1,80,2560]{4,3,2,1,0:T(8,128)(2,1)}, u32[]{:S(2)}, u32[]{:S(2)}) %collective-permute-start.2) | collective-permute-done | bytes 3276832 | tf_op jit(solution)/shard_map/ppermute | solution.py:18
  152.0 7.1 %pad_maximum_fusion = bf16[2,4,5,80,2560]{4,3,2,1,0:T(8,128)(2,1)S(1)} fusion(bf16[2,4,1,80,2560]{4,3,2,1,0:T(8,128)(2,1)} %collective-permute-done.3, bf16[2,1,3,80,2560]{4,3,2,1,0:T(8,128)(2,1)} %copy-done.6, bf16[1,2,3,80,2560]{4,3,2,1,0:T(8,128)(2,1)S(1)} %bitcast.68, bf16[1,2,3,80,2560]{4,3,2,1,0:T(8,128)(2,1)S(1)} %fusion.42, ...), kind=kLoop, calls=%fused_computation.44 | loop fusion | flops 40960000 | bytes 32768000 | tf_op jit(solution)/shard_map/concatenate | solution.py:22
  159.1 5.9 %fusion.73 = (bf16[1,4,5,80,2560]{4,3,2,1,0:T(8,128)(2,1)}, bf16[1,4,5,80,2560]{4,3,2,1,0:T(8,128)(2,1)}) fusion(bf16[2,4,5,80,2560]{4,3,2,1,0:T(8,128)(2,1)S(1)} %pad_maximum_fusion), kind=kLoop, calls=%fused_computation.122 | loop fusion | bytes 32768000 | tf_op jit(solution)/shard_map/slice | solution.py:45
  166.6 165.4 %while.14 = (s32[]{:T(128)}, bf16[480,2560]{1,0:T(8,128)(2,1)}, bf16[1600,2560]{1,0:T(8,128)(2,1)}, s32[20,3]{0,1:T(4,128)S(1)}, bf16[480,2560]{1,0:T(8,128)(2,1...) while((s32[]{:T(128)}, bf16[480,2560]{1,0:T(8,128)(2,1)}, ...), condition=%wide.region_7.8_spmd.clone, body=%wide.region_4.7_spmd.clone.sunk | while | flops 811298240 | bytes 70662840 | solution.py:109
  170.3 3.9 %fusion.85 = (f32[2,480]{1,0:T(2,128)S(1)}, f32[2,480,1600]{2,1,0:T(8,128)S(1)}) fusion(bf16[1600,2,128]{0,2,1:T(8,128)(2,1)S(1)} %bitcast.65, pred[1600]{0:T(1024)(128)(4,1)S(1)} %compare_and_fusion.2, s32[2]{0:T(128)S(1)} %get-tuple-element.377, s32[480,1600]{1,0:T(8,128)S(1)} %get-tuple-element.378, s32[2]{0:T(128)S(1)} %get-tuple-element.379, ...), kind=kOutput, calls=%fused_computation.121.clone.1 | convolution fusion | flops 407039040 | bytes 16430428 | tf_op jit(solution)/shard_map/while/body/eval_jaxpr/qhd,khd->hqk/dot_general | solution.py:91
  174.2 2.7 copy-done
  178.5 3.9 %fusion.87 = bf16[2,60,8,128]{3,2,1,0:T(8,128)(2,1)S(1)} fusion(bf16[1600,2,128]{0,2,1:T(8,128)(2,1)S(1)} %bitcast.69, f32[2,480,1600]{2,1,0:T(8,128)} %copy-done, f32[2,480]{1,0:T(2,128)S(1)} %get-tuple-element.383, f32[480,2]{0,1:T(2,128)S(1)} %bitcast.73), kind=kOutput, calls=%fused_computation.16.clone.1 | convolution fusion | flops 396533760 | bytes 7216640 | tf_op jit(solution)/shard_map/while/body/eval_jaxpr/hqk,khd->qhd/dot_general | solution.py:98
  186.8 3.9 %fusion.85 = (f32[2,480]{1,0:T(2,128)S(1)}, f32[2,480,1600]{2,1,0:T(8,128)S(1)}) fusion(bf16[1600,2,128]{0,2,1:T(8,128)(2,1)S(1)} %bitcast.65, pred[1600]{0:T(1024)(128)(4,1)S(1)} %compare_and_fusion.2, s32[2]{0:T(128)S(1)} %get-tuple-element.377, s32[480,1600]{1,0:T(8,128)S(1)} %get-tuple-element.378, s32[2]{0:T(128)S(1)} %get-tuple-element.379, ...), kind=kOutput, calls=%fused_computation.121.clone.1 | convolution fusion | flops 407039040 | bytes 16430428 | tf_op jit(solution)/shard_map/while/body/eval_jaxpr/qhd,khd->hqk/dot_general | solution.py:91
  195.1 3.9 %fusion.87 = bf16[2,60,8,128]{3,2,1,0:T(8,128)(2,1)S(1)} fusion(bf16[1600,2,128]{0,2,1:T(8,128)(2,1)S(1)} %bitcast.69, f32[2,480,1600]{2,1,0:T(8,128)} %copy-done, f32[2,480]{1,0:T(2,128)S(1)} %get-tuple-element.383, f32[480,2]{0,1:T(2,128)S(1)} %bitcast.73), kind=kOutput, calls=%fused_computation.16.clone.1 | convolution fusion | flops 396533760 | bytes 7216640 | tf_op jit(solution)/shard_map/while/body/eval_jaxpr/hqk,khd->qhd/dot_general | solution.py:98
  203.4 3.9 %fusion.85 = (f32[2,480]{1,0:T(2,128)S(1)}, f32[2,480,1600]{2,1,0:T(8,128)S(1)}) fusion(bf16[1600,2,128]{0,2,1:T(8,128)(2,1)S(1)} %bitcast.65, pred[1600]{0:T(1024)(128)(4,1)S(1)} %compare_and_fusion.2, s32[2]{0:T(128)S(1)} %get-tuple-element.377, s32[480,1600]{1,0:T(8,128)S(1)} %get-tuple-element.378, s32[2]{0:T(128)S(1)} %get-tuple-element.379, ...), kind=kOutput, calls=%fused_computation.121.clone.1 | convolution fusion | flops 407039040 | bytes 16430428 | tf_op jit(solution)/shard_map/while/body/eval_jaxpr/qhd,khd->hqk/dot_general | solution.py:91
  211.6 3.9 %fusion.87 = bf16[2,60,8,128]{3,2,1,0:T(8,128)(2,1)S(1)} fusion(bf16[1600,2,128]{0,2,1:T(8,128)(2,1)S(1)} %bitcast.69, f32[2,480,1600]{2,1,0:T(8,128)} %copy-done, f32[2,480]{1,0:T(2,128)S(1)} %get-tuple-element.383, f32[480,2]{0,1:T(2,128)S(1)} %bitcast.73), kind=kOutput, calls=%fused_computation.16.clone.1 | convolution fusion | flops 396533760 | bytes 7216640 | tf_op jit(solution)/shard_map/while/body/eval_jaxpr/hqk,khd->qhd/dot_general | solution.py:98
  219.9 3.9 %fusion.85 = (f32[2,480]{1,0:T(2,128)S(1)}, f32[2,480,1600]{2,1,0:T(8,128)S(1)}) fusion(bf16[1600,2,128]{0,2,1:T(8,128)(2,1)S(1)} %bitcast.65, pred[1600]{0:T(1024)(128)(4,1)S(1)} %compare_and_fusion.2, s32[2]{0:T(128)S(1)} %get-tuple-element.377, s32[480,1600]{1,0:T(8,128)S(1)} %get-tuple-element.378, s32[2]{0:T(128)S(1)} %get-tuple-element.379, ...), kind=kOutput, calls=%fused_computation.121.clone.1 | convolution fusion | flops 407039040 | bytes 16430428 | tf_op jit(solution)/shard_map/while/body/eval_jaxpr/qhd,khd->hqk/dot_general | solution.py:91
  228.1 3.9 %fusion.87 = bf16[2,60,8,128]{3,2,1,0:T(8,128)(2,1)S(1)} fusion(bf16[1600,2,128]{0,2,1:T(8,128)(2,1)S(1)} %bitcast.69, f32[2,480,1600]{2,1,0:T(8,128)} %copy-done, f32[2,480]{1,0:T(2,128)S(1)} %get-tuple-element.383, f32[480,2]{0,1:T(2,128)S(1)} %bitcast.73), kind=kOutput, calls=%fused_computation.16.clone.1 | convolution fusion | flops 396533760 | bytes 7216640 | tf_op jit(solution)/shard_map/while/body/eval_jaxpr/hqk,khd->qhd/dot_general | solution.py:98
  236.5 3.9 %fusion.85 = (f32[2,480]{1,0:T(2,128)S(1)}, f32[2,480,1600]{2,1,0:T(8,128)S(1)}) fusion(bf16[1600,2,128]{0,2,1:T(8,128)(2,1)S(1)} %bitcast.65, pred[1600]{0:T(1024)(128)(4,1)S(1)} %compare_and_fusion.2, s32[2]{0:T(128)S(1)} %get-tuple-element.377, s32[480,1600]{1,0:T(8,128)S(1)} %get-tuple-element.378, s32[2]{0:T(128)S(1)} %get-tuple-element.379, ...), kind=kOutput, calls=%fused_computation.121.clone.1 | convolution fusion | flops 407039040 | bytes 16430428 | tf_op jit(solution)/shard_map/while/body/eval_jaxpr/qhd,khd->hqk/dot_general | solution.py:91
  244.7 3.9 %fusion.87 = bf16[2,60,8,128]{3,2,1,0:T(8,128)(2,1)S(1)} fusion(bf16[1600,2,128]{0,2,1:T(8,128)(2,1)S(1)} %bitcast.69, f32[2,480,1600]{2,1,0:T(8,128)} %copy-done, f32[2,480]{1,0:T(2,128)S(1)} %get-tuple-element.383, f32[480,2]{0,1:T(2,128)S(1)} %bitcast.73), kind=kOutput, calls=%fused_computation.16.clone.1 | convolution fusion | flops 396533760 | bytes 7216640 | tf_op jit(solution)/shard_map/while/body/eval_jaxpr/hqk,khd->qhd/dot_general | solution.py:98
  253.0 3.9 %fusion.85 = (f32[2,480]{1,0:T(2,128)S(1)}, f32[2,480,1600]{2,1,0:T(8,128)S(1)}) fusion(bf16[1600,2,128]{0,2,1:T(8,128)(2,1)S(1)} %bitcast.65, pred[1600]{0:T(1024)(128)(4,1)S(1)} %compare_and_fusion.2, s32[2]{0:T(128)S(1)} %get-tuple-element.377, s32[480,1600]{1,0:T(8,128)S(1)} %get-tuple-element.378, s32[2]{0:T(128)S(1)} %get-tuple-element.379, ...), kind=kOutput, calls=%fused_computation.121.clone.1 | convolution fusion | flops 407039040 | bytes 16430428 | tf_op jit(solution)/shard_map/while/body/eval_jaxpr/qhd,khd->hqk/dot_general | solution.py:91
  261.2 3.9 %fusion.87 = bf16[2,60,8,128]{3,2,1,0:T(8,128)(2,1)S(1)} fusion(bf16[1600,2,128]{0,2,1:T(8,128)(2,1)S(1)} %bitcast.69, f32[2,480,1600]{2,1,0:T(8,128)} %copy-done, f32[2,480]{1,0:T(2,128)S(1)} %get-tuple-element.383, f32[480,2]{0,1:T(2,128)S(1)} %bitcast.73), kind=kOutput, calls=%fused_computation.16.clone.1 | convolution fusion | flops 396533760 | bytes 7216640 | tf_op jit(solution)/shard_map/while/body/eval_jaxpr/hqk,khd->qhd/dot_general | solution.py:98
  269.5 3.9 %fusion.85 = (f32[2,480]{1,0:T(2,128)S(1)}, f32[2,480,1600]{2,1,0:T(8,128)S(1)}) fusion(bf16[1600,2,128]{0,2,1:T(8,128)(2,1)S(1)} %bitcast.65, pred[1600]{0:T(1024)(128)(4,1)S(1)} %compare_and_fusion.2, s32[2]{0:T(128)S(1)} %get-tuple-element.377, s32[480,1600]{1,0:T(8,128)S(1)} %get-tuple-element.378, s32[2]{0:T(128)S(1)} %get-tuple-element.379, ...), kind=kOutput, calls=%fused_computation.121.clone.1 | convolution fusion | flops 407039040 | bytes 16430428 | tf_op jit(solution)/shard_map/while/body/eval_jaxpr/qhd,khd->hqk/dot_general | solution.py:91
  277.8 3.9 %fusion.87 = bf16[2,60,8,128]{3,2,1,0:T(8,128)(2,1)S(1)} fusion(bf16[1600,2,128]{0,2,1:T(8,128)(2,1)S(1)} %bitcast.69, f32[2,480,1600]{2,1,0:T(8,128)} %copy-done, f32[2,480]{1,0:T(2,128)S(1)} %get-tuple-element.383, f32[480,2]{0,1:T(2,128)S(1)} %bitcast.73), kind=kOutput, calls=%fused_computation.16.clone.1 | convolution fusion | flops 396533760 | bytes 7216640 | tf_op jit(solution)/shard_map/while/body/eval_jaxpr/hqk,khd->qhd/dot_general | solution.py:98
  286.1 3.9 %fusion.85 = (f32[2,480]{1,0:T(2,128)S(1)}, f32[2,480,1600]{2,1,0:T(8,128)S(1)}) fusion(bf16[1600,2,128]{0,2,1:T(8,128)(2,1)S(1)} %bitcast.65, pred[1600]{0:T(1024)(128)(4,1)S(1)} %compare_and_fusion.2, s32[2]{0:T(128)S(1)} %get-tuple-element.377, s32[480,1600]{1,0:T(8,128)S(1)} %get-tuple-element.378, s32[2]{0:T(128)S(1)} %get-tuple-element.379, ...), kind=kOutput, calls=%fused_computation.121.clone.1 | convolution fusion | flops 407039040 | bytes 16430428 | tf_op jit(solution)/shard_map/while/body/eval_jaxpr/qhd,khd->hqk/dot_general | solution.py:91
  294.3 3.9 %fusion.87 = bf16[2,60,8,128]{3,2,1,0:T(8,128)(2,1)S(1)} fusion(bf16[1600,2,128]{0,2,1:T(8,128)(2,1)S(1)} %bitcast.69, f32[2,480,1600]{2,1,0:T(8,128)} %copy-done, f32[2,480]{1,0:T(2,128)S(1)} %get-tuple-element.383, f32[480,2]{0,1:T(2,128)S(1)} %bitcast.73), kind=kOutput, calls=%fused_computation.16.clone.1 | convolution fusion | flops 396533760 | bytes 7216640 | tf_op jit(solution)/shard_map/while/body/eval_jaxpr/hqk,khd->qhd/dot_general | solution.py:98
  302.6 3.9 %fusion.85 = (f32[2,480]{1,0:T(2,128)S(1)}, f32[2,480,1600]{2,1,0:T(8,128)S(1)}) fusion(bf16[1600,2,128]{0,2,1:T(8,128)(2,1)S(1)} %bitcast.65, pred[1600]{0:T(1024)(128)(4,1)S(1)} %compare_and_fusion.2, s32[2]{0:T(128)S(1)} %get-tuple-element.377, s32[480,1600]{1,0:T(8,128)S(1)} %get-tuple-element.378, s32[2]{0:T(128)S(1)} %get-tuple-element.379, ...), kind=kOutput, calls=%fused_computation.121.clone.1 | convolution fusion | flops 407039040 | bytes 16430428 | tf_op jit(solution)/shard_map/while/body/eval_jaxpr/qhd,khd->hqk/dot_general | solution.py:91
  310.8 3.9 %fusion.87 = bf16[2,60,8,128]{3,2,1,0:T(8,128)(2,1)S(1)} fusion(bf16[1600,2,128]{0,2,1:T(8,128)(2,1)S(1)} %bitcast.69, f32[2,480,1600]{2,1,0:T(8,128)} %copy-done, f32[2,480]{1,0:T(2,128)S(1)} %get-tuple-element.383, f32[480,2]{0,1:T(2,128)S(1)} %bitcast.73), kind=kOutput, calls=%fused_computation.16.clone.1 | convolution fusion | flops 396533760 | bytes 7216640 | tf_op jit(solution)/shard_map/while/body/eval_jaxpr/hqk,khd->qhd/dot_general | solution.py:98
  319.2 3.9 %fusion.85 = (f32[2,480]{1,0:T(2,128)S(1)}, f32[2,480,1600]{2,1,0:T(8,128)S(1)}) fusion(bf16[1600,2,128]{0,2,1:T(8,128)(2,1)S(1)} %bitcast.65, pred[1600]{0:T(1024)(128)(4,1)S(1)} %compare_and_fusion.2, s32[2]{0:T(128)S(1)} %get-tuple-element.377, s32[480,1600]{1,0:T(8,128)S(1)} %get-tuple-element.378, s32[2]{0:T(128)S(1)} %get-tuple-element.379, ...), kind=kOutput, calls=%fused_computation.121.clone.1 | convolution fusion | flops 407039040 | bytes 16430428 | tf_op jit(solution)/shard_map/while/body/eval_jaxpr/qhd,khd->hqk/dot_general | solution.py:91
  327.4 3.9 %fusion.87 = bf16[2,60,8,128]{3,2,1,0:T(8,128)(2,1)S(1)} fusion(bf16[1600,2,128]{0,2,1:T(8,128)(2,1)S(1)} %bitcast.69, f32[2,480,1600]{2,1,0:T(8,128)} %copy-done, f32[2,480]{1,0:T(2,128)S(1)} %get-tuple-element.383, f32[480,2]{0,1:T(2,128)S(1)} %bitcast.73), kind=kOutput, calls=%fused_computation.16.clone.1 | convolution fusion | flops 396533760 | bytes 7216640 | tf_op jit(solution)/shard_map/while/body/eval_jaxpr/hqk,khd->qhd/dot_general | solution.py:98
  (150 shorter events, 99.5 us)
Async XLA Ops:
  0.0 2.4 copy-start.3
  0.0 5.5 %copy-start.8 = (f32[2560]{0:T(1024)S(1)}, f32[2560]{0:T(1024)}, u32[]{:S(2)}) copy-start(f32[2560]{0:T(1024)} %param.12) | copy-start | bytes 30724
  7.8 63.1 %copy-start.1 = (bf16[2,3,80,2560]{3,2,1,0:T(8,128)(2,1)S(1)}, bf16[2,3,80,2560]{3,2,1,0:T(8,128)(2,1)}, u32[]{:S(2)}) copy-start(bf16[2,3,80,2560]{3,2,1,0:T(8,128)(2,1)} %param.10) | copy-start | bytes 7372804
  9.9 57.3 %collective-permute-start = (bf16[2,1,3,80,2560]{4,3,2,1,0:T(8,128)(2,1)S(1)}, bf16[2,1,3,80,2560]{4,3,2,1,0:T(8,128)(2,1)S(1)}, u32[]{:S(2)}, u32[]{:S(2)}) collective-permute-start(bf16[2,1,3,80,2560]{4,3,2,1,0:T(8,128)(2,1)S(1)} %get-tuple-element.273), channel_id=1, source_target_pairs={{0,32},{32,64},{64,96},{96,128},{128,160},{160,192},{192,224},{1,3... | collective-permute-start | bytes 7372808 | tf_op jit(solution)/shard_map/ppermute | solution.py:18
  13.7 69.0 %copy-start.9 = (f32[2560]{0:T(1024)S(1)}, f32[2560]{0:T(1024)}, u32[]{:S(2)}) copy-start(f32[2560]{0:T(1024)} %param.11) | copy-start | bytes 30724
  13.7 57.2 %collective-permute-start.1 = (bf16[2,1,3,80,2560]{4,3,2,1,0:T(8,128)(2,1)S(1)}, bf16[2,1,3,80,2560]{4,3,2,1,0:T(8,128)(2,1)S(1)}, u32[]{:S(2)}, u32[]{:S(2)}) collective-permute-start(bf16[2,1,3,80,2560]{4,3,2,1,0:T(8,128)(2,1)S(1)} %get-tuple-element.274), channel_id=1, source_target_pairs={{32,0},{64,32},{96,64},{128,96},{160,128},{192,160},{224,192},{33,... | collective-permute-start | bytes 7372808 | tf_op jit(solution)/shard_map/ppermute | solution.py:21
  67.2 7.1 %copy-start.4 = (bf16[2,1,3,80,2560]{4,3,2,1,0:T(8,128)(2,1)}, bf16[2,1,3,80,2560]{4,3,2,1,0:T(8,128)(2,1)S(1)}, u32[]{:S(2)}) copy-start(bf16[2,1,3,80,2560]{4,3,2,1,0:T(8,128)(2,1)S(1)} %collective-permute-done) | copy-start | bytes 7372804
  71.0 3.5 %copy-start.6 = (bf16[2,1,3,80,2560]{4,3,2,1,0:T(8,128)(2,1)}, bf16[2,1,3,80,2560]{4,3,2,1,0:T(8,128)(2,1)S(1)}, u32[]{:S(2)}) copy-start(bf16[2,1,3,80,2560]{4,3,2,1,0:T(8,128)(2,1)S(1)} %collective-permute-done.1) | copy-start | bytes 7372804
  74.5 76.3 %collective-permute-start.2 = (bf16[2,4,1,80,2560]{4,3,2,1,0:T(8,128)(2,1)}, bf16[2,4,1,80,2560]{4,3,2,1,0:T(8,128)(2,1)}, u32[]{:S(2)}, u32[]{:S(2)}) collective-permute-start(bf16[2,4,1,80,2560]{4,3,2,1,0:T(8,128)(2,1)} %get-tuple-element.271), channel_id=1, source_target_pairs={{0,2},{2,4},{4,6},{6,8},{8,10},{10,12},{12,14},{14,16},{16,18},{18... | collective-permute-start | bytes 9830408 | tf_op jit(solution)/shard_map/ppermute | solution.py:18
  78.0 74.0 %collective-permute-start.3 = (bf16[2,4,1,80,2560]{4,3,2,1,0:T(8,128)(2,1)}, bf16[2,4,1,80,2560]{4,3,2,1,0:T(8,128)(2,1)}, u32[]{:S(2)}, u32[]{:S(2)}) collective-permute-start(bf16[2,4,1,80,2560]{4,3,2,1,0:T(8,128)(2,1)} %get-tuple-element.272), channel_id=1, source_target_pairs={{2,0},{4,2},{6,4},{8,6},{10,8},{12,10},{14,12},{16,14},{18,16},{20... | collective-permute-start | bytes 9830408 | tf_op jit(solution)/shard_map/ppermute | solution.py:21
  82.6 69.4 %copy-start.2 = (bf16[2,3,80,2560]{3,2,1,0:T(8,128)(2,1)S(1)}, bf16[2,3,80,2560]{3,2,1,0:T(8,128)(2,1)}, u32[]{:S(2)}) copy-start(bf16[2,3,80,2560]{3,2,1,0:T(8,128)(2,1)} %param.10) | copy-start | bytes 7372804
  82.6 69.4 %copy-start.5 = (bf16[2,1,3,80,2560]{4,3,2,1,0:T(8,128)(2,1)S(1)}, bf16[2,1,3,80,2560]{4,3,2,1,0:T(8,128)(2,1)}, u32[]{:S(2)}) copy-start(bf16[2,1,3,80,2560]{4,3,2,1,0:T(8,128)(2,1)} %copy-done.4) | copy-start | bytes 7372804
  159.1 7.5 %copy-start.7 = (s32[20,3]{0,1:T(4,128)S(1)}, s32[20,3]{0,1:T(4,128)}, u32[]{:S(2)}) copy-start(s32[20,3]{0,1:T(4,128)} %param.13) | copy-start | bytes 724
  174.2 2.7 copy-start
  190.7 2.7 copy-start
  207.3 2.7 copy-start
  223.8 2.7 copy-start
  240.3 2.7 copy-start
  256.9 2.7 copy-start
  273.4 2.7 copy-start
  290.0 2.7 copy-start
  306.5 2.7 copy-start
  323.0 2.7 copy-start
where the time goes:
time: 337 us; the launch traced here: 332 us
  waiting for transfers between devices  120 us (36%)
  matrix products  77.7 us (23%)
  local copies, waits for them, and re-layouts  70.7 us (21%)
  other arithmetic  45.8 us (14%)
  starting transfers between devices  14.1 us (4%)
    ppermute x2, waiting for transfers between devices, with_halo(): lax.ppermute(lax.slice_in_dim(block, block.shape[dim] - width, None, axis...  115 us
    dot_general x10, matrix products, attend_group(): jnp.einsum('hqk,khd->qhd', weights.astype(jnp.bfloat16), value_block, pre...  38.8 us
    dot_general x10, matrix products, attend_group(): jnp.einsum('qhd,khd->hqk', query_block, key_block, preferred_element_type...  38.8 us
    while x20, local copies, waits for them, and re-layouts  26.6 us
    dynamic_slice x20, local copies, waits for them, and re-layouts, attend_group(): lax.dynamic_slice_in_dim(key_flat, start_col, pair_width, 1)  21.8 us
    reduce_sum x10, other arithmetic, attend_group(): denominator = jnp.sum(weights, axis=-1, keepdims=True)  10 us
    abs x10, other arithmetic, body(): tile_gap = jnp.abs(query_tile[:, None] - key_tile[None, :])  8.87 us
    ppermute x2, starting transfers between devices, with_halo(): lax.ppermute(lax.slice_in_dim(block, block.shape[dim] - width, None, axis...  7.3 us
  transfers between devices with their start and end apart: 4, of which 4 were waited for; matrix products, arithmetic and copies ran while one was open for 1% of the time, Pallas kernels for 0%

commit v1 on v0

v1 whole, which is shorter than its diff:
```python
import functools
import math

import jax
import jax.numpy as jnp
from jax import lax
from jax.experimental import pallas as pl
from jax.experimental.pallas import tpu as pltpu
from jax.sharding import PartitionSpec as P

HD = 128
W = 80
EPS = 1e-06
NEG = -1e30
LOG2E = math.log2(math.e)
SCALE2 = LOG2E / math.sqrt(HD)
F32 = jnp.float32
BF16 = jnp.bfloat16

NH = 20
AT_P = 0
AT_Y = NH
AT_PLACE = 2 * NH
AT_WIN = 3 * NH
AT_ROW_LO = 6 * NH
AT_ROW_HI = 6 * NH + 1
AT_FRAME_LO = 6 * NH + 2
AT_FRAME_HI = 6 * NH + 3
AT_NF = 6 * NH + 4


def params(mib=12):
    return pltpu.CompilerParams(vmem_limit_bytes=mib * 1024 * 1024)


def estimate(heads, pairs):
    flops = heads * pairs * HD * 4
    return pl.CostEstimate(flops=flops * 3, bytes_accessed=heads * 1_000_000, transcendentals=heads * pairs)


def normed(raw, inverse, gain):
    return (raw.astype(F32) * inverse * gain).astype(BF16)


def pack_queries_kernel(group, meta, *refs):
    raws = refs[:group]
    gains = refs[group : 2 * group]
    inverse, up, down = refs[2 * group :]
    for j in range(group):
        q = normed(raws[j][...], inverse[...], gains[j][...].reshape(1, 1, 1, HD))
        up[j] = q[1].reshape(3 * W, HD)
        down[j] = q[0].reshape(3 * W, HD)


def pack_rows_kernel(group, meta, *refs):
    keys = refs[:group]
    values = refs[group : 2 * group]
    gains = refs[2 * group : 3 * group]
    inverse, up, down = refs[3 * group :]
    for j in range(group):
        gain = gains[j][...].reshape(1, 1, HD)
        up[j, 0] = normed(keys[j][:, 2], inverse[:, 2], gain)
        up[j, 1] = values[j][:, 2]
        down[j, 0] = normed(keys[j][:, 0], inverse[:, 0], gain)
        down[j, 1] = values[j][:, 0]


def head_spec(at, start, group, j):
    return pl.BlockSpec((2, 3, W, HD), lambda s, meta: (0, 0, 0, meta[at + start + s * group + j]))


def gain_spec(at, start, group, j):
    return pl.BlockSpec((1, HD), lambda s, meta: (0, meta[at + start + s * group + j]))


def whole(shape):
    return pl.BlockSpec(shape, lambda s, meta: (0,) * len(shape))


def group_of(count):
    return 4 if count % 4 == 0 else 2


def pack_queries(meta, q, gain, inverse, count):
    group = group_of(count)
    out = jax.ShapeDtypeStruct((count, 3 * W, HD), BF16)
    out_spec = pl.BlockSpec((group, 3 * W, HD), lambda s, meta: (s, 0, 0))
    return pl.pallas_call(
        functools.partial(pack_queries_kernel, group),
        grid_spec=pltpu.PrefetchScalarGridSpec(
            num_scalar_prefetch=1,
            grid=(count // group,),
            in_specs=[head_spec(AT_P, 0, group, j) for j in range(group)]
            + [gain_spec(AT_P, 0, group, j) for j in range(group)]
            + [whole((2, 3, W, HD))],
            out_specs=[out_spec, out_spec],
        ),
        out_shape=[out, out],
        compiler_params=params(),
        cost_estimate=pl.CostEstimate(flops=count * 200_000, bytes_accessed=count * 250_000, transcendentals=0),
        name="pack_queries",
    )(meta, *([q] * group), *([gain] * group), inverse)


def pack_rows(meta, k, v, gain, inverse, start, count):
    group = group_of(count)
    out = jax.ShapeDtypeStruct((count, 2, 2, W, HD), BF16)
    out_spec = pl.BlockSpec((group, 2, 2, W, HD), lambda s, meta: (s, 0, 0, 0, 0))
    return pl.pallas_call(
        functools.partial(pack_rows_kernel, group),
        grid_spec=pltpu.PrefetchScalarGridSpec(
            num_scalar_prefetch=1,
            grid=(count // group,),
            in_specs=[head_spec(AT_Y, start, group, j) for j in range(group)] * 2
            + [gain_spec(AT_Y, start, group, j) for j in range(group)]
            + [whole((2, 3, W, HD))],
            out_specs=[out_spec, out_spec],
        ),
        out_shape=[out, out],
        compiler_params=params(),
        cost_estimate=pl.CostEstimate(flops=count * 200_000, bytes_accessed=count * 400_000, transcendentals=0),
        name="pack_rows",
    )(meta, *([k] * group), *([v] * group), *([gain] * group), inverse)


def fill_lines(kx, vx, k, v, inverse, gain, low, high):
    kn = normed(k[...], inverse[...], gain[...].reshape(1, 1, 1, HD))
    for j in range(2):
        kx[j, 0:W] = low[0, 0, j]
        kx[j, W : 4 * W] = kn[j].reshape(3 * W, HD)
        kx[j, 4 * W : 5 * W] = high[0, 0, j]
        vx[j, 0:W, 0:HD] = low[0, 1, j]
        vx[j, W : 4 * W, 0:HD] = v[j].reshape(3 * W, HD)
        vx[j, 4 * W : 5 * W, 0:HD] = high[0, 1, j]


def line_scratch(group):
    return [pltpu.VMEM((2, 5 * W, HD), BF16)] * group + [pltpu.VMEM((2, 5 * W, 2 * HD), BF16)] * group


def fill_ones(values):
    for vx in values:
        vx[:, :, HD:] = jnp.ones((2, 5 * W, HD), BF16)


def biases(meta, head):
    lane = lax.broadcasted_iota(jnp.int32, (W, 3 * W), 1)
    line = (lane >= W).astype(jnp.int32) + (lane >= 2 * W).astype(jnp.int32)
    key_tile = (lane - W * line) >> 3
    query_tile = lax.broadcasted_iota(jnp.int32, (W, 3 * W), 0) >> 3
    gap = jnp.abs(key_tile - query_tile)
    reach_row = meta[AT_WIN + 3 * head + 1]
    reach_tile = meta[AT_WIN + 3 * head + 2]
    inner = jnp.where(reach_row > 0, reach_tile, -1)
    first = jnp.where(meta[AT_ROW_LO] > 0, inner, -1)
    last = jnp.where(meta[AT_ROW_HI] > 0, inner, -1)
    out = []
    for low, high in ((first, inner), (inner, inner), (inner, last)):
        limit = jnp.where(line == 0, low, jnp.where(line == 2, high, reach_tile))
        out.append(jnp.where(gap <= limit, 0.0, NEG).astype(F32))
    return out


def dot_t(q, k):
    return lax.dot_general(q, k, (((1,), (1,)), ((), ())), preferred_element_type=F32)


def lines_of(i):
    return slice(i * W, (i + 3) * W)


def softmax_parts(scores):
    top = functools.reduce(jnp.maximum, [jnp.max(s, axis=-1, keepdims=True) for s in scores])
    return [jnp.exp2((s - top) * SCALE2).astype(BF16) for s in scores], top


def closing(mixed, top):
    total = mixed[:, HD:]
    return (mixed[:, :HD] / total).astype(BF16), top * SCALE2 + jnp.log(total) * LOG2E


def remote_kernel(start, group, steps, meta, *refs):
    ob, oa = refs[3 * group + 5 : 3 * group + 7]
    sb, sa = refs[-2:]
    step = pl.program_id(0)

    @pl.when(step < steps)
    def _():
        remote_step(start, group, step, meta, *refs)

    @pl.when(step == steps)
    def _():
        ob[0] = sb[...].astype(BF16)
        oa[0] = sa[...].astype(BF16)


def remote_step(start, group, step, meta, *refs):
    qb, qa, inverse = refs[:3]
    refs = refs[3:]
    ks, vs, gains = refs[:group], refs[group : 2 * group], refs[2 * group : 3 * group]
    low, high, ob, oa = refs[3 * group : 3 * group + 4]
    kxs, vxs = refs[3 * group + 4 : 4 * group + 4], refs[4 * group + 4 : 5 * group + 4]
    sb, sa = refs[-2:]

    @pl.when(step == 0)
    def _():
        sb[...] = jnp.zeros_like(sb)
        sa[...] = jnp.zeros_like(sa)
        fill_ones(vxs)

    for g in range(group):
        fill_lines(kxs[g], vxs[g], ks[g], vs[g], inverse, gains[g], low.at[pl.ds(g, 1)], high.at[pl.ds(g, 1)])
    scores = []
    for g in range(group):
        head = meta[AT_P + start + step * group + g]
        masks = biases(meta, head)
        parts = [
            dot_t(q[g, i * W : (i + 1) * W], kxs[g][j, lines_of(i)]) + masks[i]
            for j, q in ((0, qb), (1, qa))
            for i in range(3)
        ]
        scores.append(jnp.concatenate(parts, axis=0))
    lane = lax.broadcasted_iota(jnp.int32, (3 * W, HD), 1)
    for g in range(group):
        (weights,), top = softmax_parts([scores[g]])
        mixed = jnp.concatenate(
            [
                jnp.dot(
                    weights[(3 * j + i) * W : (3 * j + i + 1) * W],
                    vxs[g][j, lines_of(i)],
                    preferred_element_type=F32,
                )
                for j in range(2)
                for i in range(3)
            ],
            axis=0,
        )
        mixed, lse = closing(mixed, top)
        ob[g] = mixed[: 3 * W]
        oa[g] = mixed[3 * W :]
        for j, st in ((0, sb), (1, sa)):
            full = lse[3 * W * j : 3 * W * (j + 1)]
            piece = full.astype(BF16).astype(F32)
            rest = full - piece
            middle = rest.astype(BF16).astype(F32)
            both = jnp.where(lane < 32, piece, jnp.where(lane < 64, middle, rest - middle))
            both = jnp.where(lane < 96, both, 0.0)
            st[...] = jnp.where((lane & 31) == step * group + g, both, st[...])


def remote_partial(meta, qb, qa, k, v, gain, inverse, low, high, start, count):
    group = 2
    rows = low.shape[0]
    steps = count // group
    last = min(rows // group, steps) - 1

    def at(j):
        return lambda s, meta: (0, 0, 0, meta[AT_P + start + jnp.minimum(s, steps - 1) * group + j])

    heads = [pl.BlockSpec((2, 3, W, HD), at(j)) for j in range(group)]
    gains = [pl.BlockSpec((1, HD), lambda s, meta, at=at(j): at(s, meta)[2:]) for j in range(group)]
    q_spec = pl.BlockSpec(
        (group, 3 * W, HD), lambda s, meta: (start // group + jnp.minimum(s, steps - 1), 0, 0)
    )
    o_spec = pl.BlockSpec((group, 3 * W, HD), lambda s, meta: (s, 0, 0))
    row_spec = pl.BlockSpec((group, 2, 2, W, HD), lambda s, meta: (jnp.minimum(s, last), 0, 0, 0, 0))
    out = jax.ShapeDtypeStruct((count + 1, 3 * W, HD), BF16)
    return pl.pallas_call(
        functools.partial(remote_kernel, start, group, steps),
        grid_spec=pltpu.PrefetchScalarGridSpec(
            num_scalar_prefetch=1,
            grid=(steps + 1,),
            in_specs=[q_spec, q_spec, whole((2, 3, W, HD))]
            + heads * 2
            + gains
            + [row_spec, row_spec],
            out_specs=[o_spec, o_spec],
            scratch_shapes=line_scratch(group) + [pltpu.VMEM((3 * W, HD), F32)] * 2,
        ),
        out_shape=[out, out],
        compiler_params=params(),
        cost_estimate=estimate(count, 480 * 240),
        name="remote_partial",
    )(meta, qb, qa, inverse, *([k] * group), *([v] * group), *([gain] * group), low, high)


def own_kernel(group, split, meta, *refs):
    qinverse, kinverse = refs[:2]
    refs = refs[2:]
    qs, ks, vs, qgains, kgains = (refs[group * n : group * (n + 1)] for n in range(5))
    refs = refs[5 * group :]
    chunks = 1 if split is None else 2
    lows, highs = (refs[group * chunks * n : group * chunks * (n + 1)] for n in range(2))
    out, lse_out = refs[2 * group * chunks : 2 * group * chunks + 2]
    refs = refs[2 * group * chunks + 2 :]
    kxs, vxs = refs[:group], refs[group:]
    step = pl.program_id(0)
    start = 0

    @pl.when(step == 0)
    def _():
        lse_out[...] = jnp.zeros_like(lse_out)
        fill_ones(vxs)

    def line_of(blocks, g):
        if split is None:
            return blocks[g]
        early = meta[AT_PLACE + start + step * group + g] < split
        return jnp.where(early, blocks[g][...], blocks[group + g][...])

    for g in range(group):
        fill_lines(
            kxs[g], vxs[g], ks[g], vs[g], kinverse, kgains[g], line_of(lows, g), line_of(highs, g)
        )
    scores = []
    for g in range(group):
        head = meta[AT_P + start + step * group + g]
        masks = biases(meta, head)
        cross = jnp.where(meta[AT_WIN + 3 * head] > 0, 0.0, NEG)
        both = ([], [])
        qn = normed(qs[g][...], qinverse[...], qgains[g][...].reshape(1, 1, 1, HD))
        for i in range(3):
            qi = qn[:, i].reshape(2 * W, HD)
            far = masks[i] + cross
            for j in range(2):
                mask = jnp.concatenate([masks[i], far] if j == 0 else [far, masks[i]], axis=0)
                both[j].append(dot_t(qi, kxs[g][j, lines_of(i)]) + mask)
        scores.append([jnp.concatenate(part, axis=0) for part in both])
    lane = lax.broadcasted_iota(jnp.int32, (2 * W, HD), 1)
    for g in range(group):
        weights, top = softmax_parts(scores[g])
        for i in range(3):
            at = slice(2 * W * i, 2 * W * (i + 1))
            mixed = sum(
                jnp.dot(weights[j][at], vxs[g][j, lines_of(i)], preferred_element_type=F32) for j in range(2)
            )
            mixed, lse = closing(mixed, top[at])
            out[g, :, i] = mixed.reshape(2, W, HD)
            old = lse_out[:, i].reshape(2 * W, HD)
            lse_out[:, i] = jnp.where(lane == start + step * group + g, lse, old).reshape(2, W, HD)


def own_partial(meta, q, k, v, qgain, kgain, qinverse, kinverse, lows, highs, split, count):
    group = 2
    start = 0
    heads = [head_spec(AT_P, start, group, j) for j in range(group)]
    gains = [gain_spec(AT_P, start, group, j) for j in range(group)]

    def row_spec(first, rows, j):
        def at(s, meta):
            place = meta[AT_PLACE + start + s * group + j] - first
            return (jnp.clip(place, 0, rows - 1), 0, 0, 0, 0)

        return pl.BlockSpec((1, 2, 2, W, HD), at)

    rows = [
        row_spec(first, chunk.shape[0], j)
        for first, chunk in zip((0, split), lows)
        for j in range(group)
    ]
    return pl.pallas_call(
        functools.partial(own_kernel, group, split),
        grid_spec=pltpu.PrefetchScalarGridSpec(
            num_scalar_prefetch=1,
            grid=(count // group,),
            in_specs=[whole((2, 3, W, HD))] * 2 + heads * 3 + gains * 2 + rows * 2,
            out_specs=[
                pl.BlockSpec((group, 2, 3, W, HD), lambda s, meta: (s, 0, 0, 0, 0)),
                whole((2, 3, W, HD)),
            ],
            scratch_shapes=line_scratch(group),
        ),
        out_shape=[
            jax.ShapeDtypeStruct((count, 2, 3, W, HD), BF16),
            jax.ShapeDtypeStruct((2, 3, W, HD), F32),
        ],
        compiler_params=params(),
        cost_estimate=estimate(count, 480 * 480),
        name="own_partial",
    )(
        meta,
        qinverse,
        kinverse,
        *([q] * group),
        *([k] * group),
        *([v] * group),
        *([qgain] * group),
        *([kgain] * group),
        *[chunk for chunk in lows for _ in range(group)],
        *[chunk for chunk in highs for _ in range(group)],
    )


def merge_kernel(group, starts, meta, part, lse, ob, oa, sb, sa, *refs):
    out, buffer, sems = refs[-3:]
    step = pl.program_id(0)
    steps = pl.num_programs(0)
    slot = slot_at(step, group, starts)
    at = lax.rem(step, 2)

    def copy(step, buffer_at, g):
        head = meta[AT_P + slot_at(step, group, starts) + g]
        return pltpu.make_async_copy(
            buffer.at[buffer_at, g],
            out.at[:, :, :, pl.ds(pl.multiple_of(head * HD, HD), HD)],
            sems.at[buffer_at, g],
        )

    @pl.when(step >= 2)
    def _():
        for g in range(group):
            copy(step - 2, at, g).wait()

    lane = lax.broadcasted_iota(jnp.int32, (3 * W, HD), 1)
    for g in range(group):
        merged = slot + g < meta[AT_NF]
        for j, o, st, flag in ((0, ob, sb, AT_FRAME_LO), (1, oa, sa, AT_FRAME_HI)):
            mine = jnp.where(lane == slot + g, lse[j].reshape(3 * W, HD), 0.0)
            own = jnp.sum(mine, axis=1, keepdims=True)
            pieces = jnp.where(((lane & 31) == step * group + g) & (lane < 96), st[0].astype(F32), 0.0)
            other = jnp.sum(pieces, axis=1, keepdims=True)
            use = merged & (meta[flag] > 0)
            other = jnp.where(use, other, NEG)
            top = jnp.maximum(own, other)
            own_weight = jnp.exp2(own - top)
            other_weight = jnp.exp2(other - top)
            scale = 1.0 / (own_weight + other_weight)
            far = jnp.where(use, o[g].astype(F32), 0.0)
            mixed = part[g, j].reshape(3 * W, HD).astype(F32) * (own_weight * scale)
            mixed = mixed + far * (other_weight * scale)
            buffer[at, g, j] = mixed.astype(BF16).reshape(3, W, HD)
    for g in range(group):
        copy(step, at, g).start()

    @pl.when(step == steps - 1)
    def _():
        for g in range(group):
            if starts[2] > 1:
                copy(step - 1, 1 - at, g).wait()
            copy(step, at, g).wait()


def slot_at(step, group, starts):
    base, tail, _, turn = starts
    return jnp.where(step < turn, base + step * group, tail + (step - turn) * group)


def merge(meta, out, part, lse, o_below, o_above, base, tail, chunk):
    group = 2
    turn = chunk // group
    steps = turn + (0 if tail is None else (NH - tail) // group)
    starts = (base, NH if tail is None else tail, steps, turn)
    stop = o_below.shape[0] - 1
    o_spec = pl.BlockSpec((group, 3 * W, HD), lambda s, meta: (jnp.minimum(s, turn - 1), 0, 0))
    stat_spec = pl.BlockSpec((1, 3 * W, HD), lambda s, meta: (stop, 0, 0))
    return pl.pallas_call(
        functools.partial(merge_kernel, group, starts),
        grid_spec=pltpu.PrefetchScalarGridSpec(
            num_scalar_prefetch=1,
            grid=(steps,),
            in_specs=[
                pl.BlockSpec(
                    (group, 2, 3, W, HD), lambda s, meta: (slot_at(s, group, starts) // group, 0, 0, 0, 0)
                ),
                whole((2, 3, W, HD)),
                o_spec,
                o_spec,
                stat_spec,
                stat_spec,
            ]
            + ([] if out is None else [pl.BlockSpec(memory_space=pl.ANY)]),
            out_specs=pl.BlockSpec(memory_space=pl.ANY),
            scratch_shapes=[
                pltpu.VMEM((2, group, 2, 3, W, HD), BF16),
                pltpu.SemaphoreType.DMA((2, group)),
            ],
        ),
        out_shape=jax.ShapeDtypeStruct((2, 3, W, NH * HD), BF16),
        input_output_aliases={} if out is None else {7: 0},
        compiler_params=params(),
        cost_estimate=pl.CostEstimate(flops=steps * 2_000_000, bytes_accessed=steps * 800_000, transcendentals=0),
        name="merge",
    )(meta, part, lse, o_below, o_above, o_below, o_above, *([] if out is None else [out]))


def order_of(keys):
    ids = jnp.arange(NH, dtype=jnp.int32)
    unique = keys * NH + ids
    rank = jnp.sum((unique[None, :] < unique[:, None]).astype(jnp.int32), axis=1)
    return jnp.sum(jnp.where(rank[:, None] == ids[None, :], ids[:, None], 0), axis=0), rank


def shifts(axis):
    count = lax.axis_size(axis)
    forward = [(i, i + 1) for i in range(count - 1)]
    return forward, [(b, a) for a, b in forward]


def attention(frame_slots, row_slots, first, meta, q, k, v, q_gain, k_gain, q_inverse, k_inverse):
    up_frame, down_frame = shifts("frame")
    up_row, down_row = shifts("height")
    q_up, q_down = pack_queries(meta, q, q_gain, q_inverse, frame_slots)
    qb = lax.ppermute(q_up, "frame", up_frame)
    qa = lax.ppermute(q_down, "frame", down_frame)
    lows, highs = [], []
    for start, count in ((0, first), (first, row_slots - first)):
        up, down = pack_rows(meta, k, v, k_gain, k_inverse, start, count)
        lows.append(lax.ppermute(up, "height", up_row))
        highs.append(lax.ppermute(down, "height", down_row))
    remote = []
    for part, (start, count) in enumerate(((0, first), (first, frame_slots - first))):
        ob, oa = remote_partial(
            meta, qb, qa, k, v, k_gain, k_inverse, lows[part], highs[part], start, count
        )
        remote.append((lax.ppermute(oa, "frame", up_frame), lax.ppermute(ob, "frame", down_frame)))
    part, lse = own_partial(
        meta, q, k, v, q_gain, k_gain, q_inverse, k_inverse, lows, highs, first, NH
    )
    out = merge(meta, None, part, lse, *remote[0], 0, frame_slots, first)
    return merge(meta, out, part, lse, *remote[1], first, None, frame_slots - first)


def squares_of(raw):
    values = raw.astype(F32)
    return jnp.sum(values * values, axis=-1)


def body(q, k, v, q_gain, k_gain, window):
    width_total = q.shape[3] * lax.axis_size("head")
    query_sum, key_sum = lax.psum((squares_of(q), squares_of(k)), "head")

    def inverse_of(total):
        return jnp.broadcast_to(lax.rsqrt(total / width_total + EPS)[..., None], (2, 3, W, HD))

    frame_reach, row_reach = window[:, 0], window[:, 1]
    frame_at, row_at = lax.axis_index("frame"), lax.axis_index("height")
    flags = jnp.stack(
        [
            row_at > 0,
            row_at < lax.axis_size("height") - 1,
            frame_at > 0,
            frame_at < lax.axis_size("frame") - 1,
        ]
    ).astype(jnp.int32)
    frame_list, frame_rank = order_of((1 - frame_reach) * 2 + (1 - row_reach))
    row_list, row_rank = order_of((1 - row_reach) * 2 + (1 - frame_reach))
    ids = jnp.arange(NH, dtype=jnp.int32)
    place = jnp.sum(jnp.where(frame_rank[:, None] == ids[None, :], row_rank[:, None], 0), axis=0)
    meta = jnp.concatenate(
        [
            frame_list,
            row_list,
            place,
            window.reshape(-1),
            flags,
            jnp.sum(frame_reach, keepdims=True),
        ]
    ).astype(jnp.int32)
    return attention(
        NH,
        NH,
        8,
        meta,
        q,
        k,
        v,
        q_gain[None],
        k_gain[None],
        inverse_of(query_sum),
        inverse_of(key_sum),
    )


def solution(mesh):
    placed = (
        P("frame", "height", None, "head"),
        P("frame", "height", None, "head"),
        P("frame", "height", None, "head"),
        P("head"),
        P("head"),
        P("head", None),
    )
    return jax.shard_map(
        body,
        mesh=mesh,
        in_specs=placed,
        out_specs=P("frame", "height", None, "head"),
        check_vma=False,
    )
```

time: 337 us -> 109 us (0.32); the launches traced: 332 us -> 108 us
  waiting for transfers between devices: 120 us -> 21.1 us
  matrix products: 77.7 us -> 0 us
  local copies, waits for them, and re-layouts: 70.7 us -> 3.55 us
  Pallas kernels: 0 us -> 42 us
  other arithmetic: 45.8 us -> 6.16 us
  starting transfers between devices: 14.1 us -> 32.6 us
    ppermute x4 -> x10, waiting for transfers between devices: 120 us -> 21.1 us  [the longest x2 9.39 us: attention(): lows.append(lax.ppermute(up, 'height', up_row))]
    dot_general x20 -> x0, matrix products: 77.7 us -> none  [the longest x10 38.8 us: attend_group(): jnp.einsum('hqk,khd->qhd', weights.astype(jnp.bfloat16), value_block, pre...]
    pallas_call x0 -> x8, Pallas kernels: none -> 42 us  [the longest x1 14.8 us: own_partial(): pl.pallas_call(functools.partial(own_kernel, group, split), grid_spec=plt...]
    dynamic_slice x40 -> x0, local copies, waits for them, and re-layouts: 29.2 us -> none  [the longest x20 21.8 us: attend_group(): lax.dynamic_slice_in_dim(key_flat, start_col, pair_width, 1)]
    while x20 -> x0, local copies, waits for them, and re-layouts: 26.6 us -> none
    ppermute x4 -> x10, starting transfers between devices: 14.1 us -> 32.6 us  [the longest x2 9.89 us: attention(): lax.ppermute(oa, 'frame', up_frame)]
    abs x20 -> x0, other arithmetic: 13.6 us -> none  [the longest x10 8.87 us: body(): tile_gap = jnp.abs(query_tile[:, None] - key_tile[None, :])]
    reduce_sum x10 -> x3, other arithmetic: 10 us -> 1.67 us  [the longest x1 1.39 us: body(): jnp.sum(frame_reach, keepdims=True)]
  transfers between devices with their start and end apart: 4 -> 10, of which waited for: 4 -> 4; matrix products, arithmetic and copies ran while one was open for 1% -> 0% of each run, Pallas kernels for 0% -> 33%
where the time goes in v1:
time: 109 us; the launch traced here: 108 us
  Pallas kernels  42 us (39%)
  starting transfers between devices  32.6 us (30%)
  waiting for transfers between devices  21.1 us (19%)
  other arithmetic  6.16 us (6%)
  local copies, waits for them, and re-layouts  3.55 us (3%)
  blocking collectives  2.5 us (2%)
    pallas_call x1, Pallas kernels, own_partial(): pl.pallas_call(functools.partial(own_kernel, group, split), grid_spec=plt...  14.8 us
    pallas_call x2, Pallas kernels, remote_partial(): pl.pallas_call(functools.partial(remote_kernel, start, group, steps), gri...  14.8 us
    ppermute x2, starting transfers between devices, attention(): lax.ppermute(oa, 'frame', up_frame)  9.89 us
    ppermute x2, waiting for transfers between devices, attention(): lows.append(lax.ppermute(up, 'height', up_row))  9.39 us
    pallas_call x2, Pallas kernels, merge(): pl.pallas_call(functools.partial(merge_kernel, group, starts), grid_spec=...  7.59 us
    ppermute x2, starting transfers between devices, attention(): highs.append(lax.ppermute(down, 'height', down_row))  7.53 us
    ppermute x2, waiting for transfers between devices, attention(): highs.append(lax.ppermute(down, 'height', down_row))  6.45 us
    ppermute x2, starting transfers between devices, attention(): lows.append(lax.ppermute(up, 'height', up_row))  5.41 us
  transfers between devices with their start and end apart: 10, of which 4 were waited for; matrix products, arithmetic and copies ran while one was open for 0% of the time, Pallas kernels for 33%

profile of v1, /device:TPU:38, one launch (start us, length us, event | category | flops | bytes accessed | tf_op | source)
XLA Modules:
  0.0 108.2 jit_solution(2873682093529716173)
XLA Ops:
  0.0 0.8 fusion.1
  0.8 1.4 %slice_reduce_fusion = (s32[]{:T(128)}, s32[20]{0:T(128)S(1)}, s32[20]{0:T(128)S(1)}) fusion(s32[20,3]{0,1:T(4,128)} %param.11), kind=kLoop, calls=%fused_computation.23 | loop fusion | flops 219 | bytes 324 | tf_op jit(solution)/shard_map/reduce_sum | solution.py:556
  2.2 0.8 copy.10
  2.9 3.6 %multiply_reduce_fusion = (f32[2,3,80]{2,1,0:T(4,128)S(1)}, f32[2,3,80]{2,1,0:T(4,128)S(1)}) fusion(bf16[2,3,80,2560]{3,2,1,0:T(8,128)(2,1)} %refs_4_.9, bf16[2,3,80,2560]{3,2,1,0:T(8,128)(2,1)} %refs_3_.9), kind=kLoop, calls=%fused_computation | loop fusion | flops 7371840 | bytes 4919040 | tf_op jit(solution)/shard_map/reduce_sum | solution.py:525
  6.6 2.5 %all-reduce = (f32[2,3,80]{2,1,0:T(4,128)S(1)}, f32[2,3,80]{2,1,0:T(4,128)S(1)}) all-reduce(f32[2,3,80]{2,1,0:T(4,128)S(1)} %get-tuple-element.42, f32[2,3,80]{2,1,0:T(4,128)S(1)} %get-tuple-element.41), channel_id=1, replica_groups=mesh['frame'=8,'height'=16,'head'=2] {'head'}, use_global_device_ids=true, to_apply=%region_7.8 | all-reduce | flops 960 | bytes 7680 | tf_op jit(solution)/shard_map/psum | solution.py:530
  9.2 0.2 convert_reduce_fusion
  9.6 0.7 concatenate.3.meta
  10.3 0.1 broadcast_in_dim.61.refs_12_.refs_1_.refs_2_
  10.4 1.7 %copy-done.1 = bf16[2,3,80,2560]{3,2,1,0:T(8,128)(2,1)S(1)} copy-done((bf16[2,3,80,2560]{3,2,1,0:T(8,128)(2,1)S(1)}, bf16[2,3,80,2560]{3,2,1,0:T(8,128)(2,1)}, u32[]{:S(2)}) %copy-start.1) | copy-done | bytes 2457624
  12.1 1.7 %pack_rows.3 = (bf16[12,2,2,80,128]{4,3,2,1,0:T(8,128)(2,1)S(1)}, bf16[12,2,2,80,128]{4,3,2,1,0:T(8,128)(2,1)S(1)}) custom-call(s32[125]{0:T(128)S(1)} %concatenate.3.meta, bf16[2,3,80,2560]{3,2,1,0:T(8,128)(2,1)S(1)} %copy-done, bf16[2,3,80,2560]{3,2,1,0:T(8,128)(2,1)S(1)} %copy-done, bf16[2,3,80,2560]{3,2,1,0:T(8,128)(2,1)S(1)} %copy-done, ...), custom_call_target="tpu_custom_call" | custom-call | flops 2400000 | bytes 4800000 | tf_op jit(solution)/shard_map/pack_rows/pallas_call | solution.py:109
  13.8 3.5 %collective-permute-start.1 = (bf16[12,2,2,80,128]{4,3,2,1,0:T(8,128)(2,1)S(1)}, bf16[12,2,2,80,128]{4,3,2,1,0:T(8,128)(2,1)S(1)}, u32[]{:S(2)}, u32[]{:S(2)}) collective-permute-start(bf16[12,2,2,80,128]{4,3,2,1,0:T(8,128)(2,1)S(1)} %get-tuple-element.18), channel_id=1, source_target_pairs={{0,2},{2,4},{4,6},{6,8},{8,10},{10,12},{12,14},{14,16},{16,18},{18... | collective-permute-start | bytes 2949128 | tf_op jit(solution)/shard_map/ppermute | solution.py:508
  17.3 0.1 broadcast_in_dim.60.refs_0_.refs_8_
  17.5 1.8 %pack_queries.1 = (bf16[20,240,128]{2,1,0:T(8,128)(2,1)S(1)}, bf16[20,240,128]{2,1,0:T(8,128)(2,1)S(1)}) custom-call(s32[125]{0:T(128)S(1)} %concatenate.3.meta, bf16[2,3,80,2560]{3,2,1,0:T(8,128)(2,1)S(1)} %copy-done.3, bf16[2,3,80,2560]{3,2,1,0:T(8,128)(2,1)S(1)} %copy-done.3, bf16[2,3,80,2560]{3,2,1,0:T(8,128)(2,1)S(1)} %copy-done.3, ...), custom_call_target="tpu_custom_call" | custom-call | flops 4000000 | bytes 5000000 | tf_op jit(solution)/shard_map/pack_queries/pallas_call | solution.py:88
  19.3 3.8 %collective-permute-start.4 = (bf16[20,240,128]{2,1,0:T(8,128)(2,1)S(1)}, bf16[20,240,128]{2,1,0:T(8,128)(2,1)S(1)}, u32[]{:S(2)}, u32[]{:S(2)}) collective-permute-start(bf16[20,240,128]{2,1,0:T(8,128)(2,1)S(1)} %get-tuple-element.23), channel_id=1, source_target_pairs={{0,32},{32,64},{64,96},{96,128},{128,160},{160,192},{192,224},{1,3... | collective-permute-start | bytes 3686408 | tf_op jit(solution)/shard_map/ppermute | solution.py:503
  23.2 2.1 %collective-permute-start.5 = (bf16[20,240,128]{2,1,0:T(8,128)(2,1)S(1)}, bf16[20,240,128]{2,1,0:T(8,128)(2,1)S(1)}, u32[]{:S(2)}, u32[]{:S(2)}) collective-permute-start(bf16[20,240,128]{2,1,0:T(8,128)(2,1)S(1)} %get-tuple-element.24), channel_id=1, source_target_pairs={{32,0},{64,32},{96,64},{128,96},{160,128},{192,160},{224,192},{33,... | collective-permute-start | bytes 3686408 | tf_op jit(solution)/shard_map/ppermute | solution.py:504
  25.3 4.5 %collective-permute-start.3 = (bf16[12,2,2,80,128]{4,3,2,1,0:T(8,128)(2,1)S(1)}, bf16[12,2,2,80,128]{4,3,2,1,0:T(8,128)(2,1)S(1)}, u32[]{:S(2)}, u32[]{:S(2)}) collective-permute-start(bf16[12,2,2,80,128]{4,3,2,1,0:T(8,128)(2,1)S(1)} %get-tuple-element.20), channel_id=1, source_target_pairs={{2,0},{4,2},{6,4},{8,6},{10,8},{12,10},{14,12},{16,14},{18,16},{20... | collective-permute-start | bytes 2949128 | tf_op jit(solution)/shard_map/ppermute | solution.py:509
  29.7 1.3 %pack_rows.2 = (bf16[8,2,2,80,128]{4,3,2,1,0:T(8,128)(2,1)S(1)}, bf16[8,2,2,80,128]{4,3,2,1,0:T(8,128)(2,1)S(1)}) custom-call(s32[125]{0:T(128)S(1)} %concatenate.3.meta, bf16[2,3,80,2560]{3,2,1,0:T(8,128)(2,1)S(1)} %copy-done, bf16[2,3,80,2560]{3,2,1,0:T(8,128)(2,1)S(1)} %copy-done, bf16[2,3,80,2560]{3,2,1,0:T(8,128)(2,1)S(1)} %copy-done, ...), custom_call_target="tpu_custom_call" | custom-call | flops 1600000 | bytes 3200000 | tf_op jit(solution)/shard_map/pack_rows/pallas_call | solution.py:109
  31.1 1.9 %collective-permute-start = (bf16[8,2,2,80,128]{4,3,2,1,0:T(8,128)(2,1)S(1)}, bf16[8,2,2,80,128]{4,3,2,1,0:T(8,128)(2,1)S(1)}, u32[]{:S(2)}, u32[]{:S(2)}) collective-permute-start(bf16[8,2,2,80,128]{4,3,2,1,0:T(8,128)(2,1)S(1)} %get-tuple-element.17), channel_id=1, source_target_pairs={{0,2},{2,4},{4,6},{6,8},{8,10},{10,12},{12,14},{14,16},{16,18},{18... | collective-permute-start | bytes 1966088 | tf_op jit(solution)/shard_map/ppermute | solution.py:508
  33.0 9.4 %collective-permute-done.1.refs_14_.refs_15_.refs_9_ = bf16[12,2,2,80,128]{4,3,2,1,0:T(8,128)(2,1)S(1)} collective-permute-done((bf16[12,2,2,80,128]{4,3,2,1,0:T(8,128)(2,1)S(1)}, bf16[12,2,2,80,128]{4,3,2,1,0:T(8,128)(2,1)S(1)}, u32[]{:S(2)}, u32[]{:S(2)}) %collective-permute-start.1) | collective-permute-done | bytes 983072 | tf_op jit(solution)/shard_map/ppermute | solution.py:508
  42.4 3.1 %collective-permute-start.2 = (bf16[8,2,2,80,128]{4,3,2,1,0:T(8,128)(2,1)S(1)}, bf16[8,2,2,80,128]{4,3,2,1,0:T(8,128)(2,1)S(1)}, u32[]{:S(2)}, u32[]{:S(2)}) collective-permute-start(bf16[8,2,2,80,128]{4,3,2,1,0:T(8,128)(2,1)S(1)} %get-tuple-element.19), channel_id=1, source_target_pairs={{2,0},{4,2},{6,4},{8,6},{10,8},{12,10},{14,12},{16,14},{18,16},{20... | collective-permute-start | bytes 1966088 | tf_op jit(solution)/shard_map/ppermute | solution.py:509
  45.5 6.4 %collective-permute-done.3.refs_18_.refs_19_.refs_10_ = bf16[12,2,2,80,128]{4,3,2,1,0:T(8,128)(2,1)S(1)} collective-permute-done((bf16[12,2,2,80,128]{4,3,2,1,0:T(8,128)(2,1)S(1)}, bf16[12,2,2,80,128]{4,3,2,1,0:T(8,128)(2,1)S(1)}, u32[]{:S(2)}, u32[]{:S(2)}) %collective-permute-start.3) | collective-permute-done | bytes 983072 | tf_op jit(solution)/shard_map/ppermute | solution.py:509
  51.9 1.8 %collective-permute-done.5.refs_1_ = bf16[20,240,128]{2,1,0:T(8,128)(2,1)S(1)} collective-permute-done((bf16[20,240,128]{2,1,0:T(8,128)(2,1)S(1)}, bf16[20,240,128]{2,1,0:T(8,128)(2,1)S(1)}, u32[]{:S(2)}, u32[]{:S(2)}) %collective-permute-start.5) | collective-permute-done | bytes 1228832 | tf_op jit(solution)/shard_map/ppermute | solution.py:504
  53.8 8.6 %remote_partial.2 = (bf16[13,240,128]{2,1,0:T(8,128)(2,1)S(1)}, bf16[13,240,128]{2,1,0:T(8,128)(2,1)S(1)}) custom-call(s32[125]{0:T(128)S(1)} %concatenate.3.meta, bf16[20,240,128]{2,1,0:T(8,128)(2,1)S(1)} %collective-permute-done.4.refs_0_, bf16[20,240,128]{2,1,0:T(8,128)(2,1)S(1)} %collective-permute-done.5.refs_1_, ...), custom_call_target="tpu_custom_call" | custom-call | flops 2123366400 | bytes 12000000 | tf_op jit(solution)/shard_map/remote_partial/pallas_call | solution.py:268
  62.4 5.0 %collective-permute-start.6 = (bf16[13,240,128]{2,1,0:T(8,128)(2,1)S(1)}, bf16[13,240,128]{2,1,0:T(8,128)(2,1)S(1)}, u32[]{:S(2)}, u32[]{:S(2)}) collective-permute-start(bf16[13,240,128]{2,1,0:T(8,128)(2,1)S(1)} %get-tuple-element.25), channel_id=1, source_target_pairs={{0,32},{32,64},{64,96},{96,128},{128,160},{160,192},{192,224},{1,3... | collective-permute-start | bytes 2396168 | tf_op jit(solution)/shard_map/ppermute | solution.py:515
  67.5 1.9 %collective-permute-start.7 = (bf16[13,240,128]{2,1,0:T(8,128)(2,1)S(1)}, bf16[13,240,128]{2,1,0:T(8,128)(2,1)S(1)}, u32[]{:S(2)}, u32[]{:S(2)}) collective-permute-start(bf16[13,240,128]{2,1,0:T(8,128)(2,1)S(1)} %get-tuple-element.26), channel_id=1, source_target_pairs={{32,0},{64,32},{96,64},{128,96},{160,128},{192,160},{224,192},{33,... | collective-permute-start | bytes 2396168 | tf_op jit(solution)/shard_map/ppermute | solution.py:515
  69.4 6.1 %remote_partial.3 = (bf16[9,240,128]{2,1,0:T(8,128)(2,1)S(1)}, bf16[9,240,128]{2,1,0:T(8,128)(2,1)S(1)}) custom-call(s32[125]{0:T(128)S(1)} %concatenate.3.meta, bf16[20,240,128]{2,1,0:T(8,128)(2,1)S(1)} %collective-permute-done.4.refs_0_, bf16[20,240,128]{2,1,0:T(8,128)(2,1)S(1)} %collective-permute-done.5.refs_1_, ...), custom_call_target="tpu_custom_call" | custom-call | flops 1415577600 | bytes 8000000 | tf_op jit(solution)/shard_map/remote_partial/pallas_call | solution.py:268
  75.6 4.9 %collective-permute-start.8 = (bf16[9,240,128]{2,1,0:T(8,128)(2,1)S(1)}, bf16[9,240,128]{2,1,0:T(8,128)(2,1)S(1)}, u32[]{:S(2)}, u32[]{:S(2)}) collective-permute-start(bf16[9,240,128]{2,1,0:T(8,128)(2,1)S(1)} %get-tuple-element.27), channel_id=1, source_target_pairs={{0,32},{32,64},{64,96},{96,128},{128,160},{160,192},{192,224},{1,3... | collective-permute-start | bytes 1658888 | tf_op jit(solution)/shard_map/ppermute | solution.py:515
  80.4 1.9 %collective-permute-start.9 = (bf16[9,240,128]{2,1,0:T(8,128)(2,1)S(1)}, bf16[9,240,128]{2,1,0:T(8,128)(2,1)S(1)}, u32[]{:S(2)}, u32[]{:S(2)}) collective-permute-start(bf16[9,240,128]{2,1,0:T(8,128)(2,1)S(1)} %get-tuple-element.28), channel_id=1, source_target_pairs={{32,0},{64,32},{96,64},{128,96},{160,128},{192,160},{224,192},{33,... | collective-permute-start | bytes 1658888 | tf_op jit(solution)/shard_map/ppermute | solution.py:515
  82.3 14.8 %own_partial.1 = (bf16[20,2,3,80,128]{4,3,2,1,0:T(8,128)(2,1)S(1)}, f32[2,3,80,128]{3,2,1,0:T(8,128)S(1)}) custom-call(s32[125]{0:T(128)S(1)} %concatenate.3.meta, f32[2,3,80,128]{3,2,1,0:T(8,128)S(1)} %broadcast_in_dim.60.refs_0_.refs_8_, f32[2,3,80,128]{3,2,1,0:T(8,128)S(1)} %broadcast_in_dim.61.refs_12_.refs_1_.refs_2_, ...), custom_call_target="tpu_custom_call" | custom-call | flops 7077888000 | bytes 20000000 | tf_op jit(solution)/shard_map/own_partial/pallas_call | solution.py:361
  97.2 3.4 %collective-permute-done.9.oa.sa = bf16[9,240,128]{2,1,0:T(8,128)(2,1)S(1)} collective-permute-done((bf16[9,240,128]{2,1,0:T(8,128)(2,1)S(1)}, bf16[9,240,128]{2,1,0:T(8,128)(2,1)S(1)}, u32[]{:S(2)}, u32[]{:S(2)}) %collective-permute-start.9) | collective-permute-done | bytes 552992 | tf_op jit(solution)/shard_map/ppermute | solution.py:515
  100.5 3.2 %merge.2.refs_0_ = bf16[2,3,80,2560]{3,2,1,0:T(8,128)(2,1)} custom-call(s32[125]{0:T(128)S(1)} %concatenate.3.meta, bf16[20,2,3,80,128]{4,3,2,1,0:T(8,128)(2,1)S(1)} %get-tuple-element.21.part, f32[2,3,80,128]{3,2,1,0:T(8,128)S(1)} %get-tuple-element.22.lse, bf16[9,240,128]{2,1,0:T(8,128)(2,1)S(1)} %collective-permute-done.8.ob.sb, ...), custom_call_target="tpu_custom_call" | custom-call | flops 8000000 | bytes 3200000 | tf_op jit(solution)/shard_map/merge/pallas_call | solution.py:456
  103.8 4.3 %merge.3 = bf16[2,3,80,2560]{3,2,1,0:T(8,128)(2,1)} custom-call(s32[125]{0:T(128)S(1)} %concatenate.3.meta, bf16[20,2,3,80,128]{4,3,2,1,0:T(8,128)(2,1)S(1)} %get-tuple-element.21.part, f32[2,3,80,128]{3,2,1,0:T(8,128)S(1)} %get-tuple-element.22.lse, bf16[13,240,128]{2,1,0:T(8,128)(2,1)S(1)} %collective-permute-done.6.ob.sb, ...), custom_call_target="tpu_custom_call", output_to_operand_aliasing={{}: (7, {})} | custom-call | flops 12000000 | bytes 4800000 | tf_op jit(solution)/shard_map/merge/pallas_call | solution.py:456
  (24 shorter events, 0.3 us)
Async XLA Ops:
  2.9 6.1 %copy-start.4 = (f32[2560]{0:T(1024)S(1)}, f32[2560]{0:T(1024)}, u32[]{:S(2)}) copy-start(f32[2560]{0:T(1024)} %param.10) | copy-start | bytes 30724
  2.9 7.5 %copy-start = (bf16[2,3,80,2560]{3,2,1,0:T(8,128)(2,1)S(1)}, bf16[2,3,80,2560]{3,2,1,0:T(8,128)(2,1)}, u32[]{:S(2)}) copy-start(bf16[2,3,80,2560]{3,2,1,0:T(8,128)(2,1)} %refs_4_.9) | copy-start | bytes 7372804
  10.4 1.7 %copy-start.1 = (bf16[2,3,80,2560]{3,2,1,0:T(8,128)(2,1)S(1)}, bf16[2,3,80,2560]{3,2,1,0:T(8,128)(2,1)}, u32[]{:S(2)}) copy-start(bf16[2,3,80,2560]{3,2,1,0:T(8,128)(2,1)} %refs_6_.9) | copy-start | bytes 7372804
  12.1 5.2 %copy-start.5 = (f32[2560]{0:T(1024)S(1)}, f32[2560]{0:T(1024)}, u32[]{:S(2)}) copy-start(f32[2560]{0:T(1024)} %param.9) | copy-start | bytes 30724
  12.1 5.3 %copy-start.3 = (bf16[2,3,80,2560]{3,2,1,0:T(8,128)(2,1)S(1)}, bf16[2,3,80,2560]{3,2,1,0:T(8,128)(2,1)}, u32[]{:S(2)}) copy-start(bf16[2,3,80,2560]{3,2,1,0:T(8,128)(2,1)} %refs_3_.9) | copy-start | bytes 7372804
  13.8 28.6 %collective-permute-start.1 = (bf16[12,2,2,80,128]{4,3,2,1,0:T(8,128)(2,1)S(1)}, bf16[12,2,2,80,128]{4,3,2,1,0:T(8,128)(2,1)S(1)}, u32[]{:S(2)}, u32[]{:S(2)}) collective-permute-start(bf16[12,2,2,80,128]{4,3,2,1,0:T(8,128)(2,1)S(1)} %get-tuple-element.18), channel_id=1, source_target_pairs={{0,2},{2,4},{4,6},{6,8},{8,10},{10,12},{12,14},{14,16},{16,18},{18... | collective-permute-start | bytes 2949128 | tf_op jit(solution)/shard_map/ppermute | solution.py:508
  17.5 12.3 %copy-start.2 = (bf16[2,3,80,2560]{3,2,1,0:T(8,128)(2,1)S(1)}, bf16[2,3,80,2560]{3,2,1,0:T(8,128)(2,1)}, u32[]{:S(2)}) copy-start(bf16[2,3,80,2560]{3,2,1,0:T(8,128)(2,1)} %refs_6_.9) | copy-start | bytes 7372804
  19.3 32.6 %collective-permute-start.4 = (bf16[20,240,128]{2,1,0:T(8,128)(2,1)S(1)}, bf16[20,240,128]{2,1,0:T(8,128)(2,1)S(1)}, u32[]{:S(2)}, u32[]{:S(2)}) collective-permute-start(bf16[20,240,128]{2,1,0:T(8,128)(2,1)S(1)} %get-tuple-element.23), channel_id=1, source_target_pairs={{0,32},{32,64},{64,96},{96,128},{128,160},{160,192},{192,224},{1,3... | collective-permute-start | bytes 3686408 | tf_op jit(solution)/shard_map/ppermute | solution.py:503
  23.2 30.6 %collective-permute-start.5 = (bf16[20,240,128]{2,1,0:T(8,128)(2,1)S(1)}, bf16[20,240,128]{2,1,0:T(8,128)(2,1)S(1)}, u32[]{:S(2)}, u32[]{:S(2)}) collective-permute-start(bf16[20,240,128]{2,1,0:T(8,128)(2,1)S(1)} %get-tuple-element.24), channel_id=1, source_target_pairs={{32,0},{64,32},{96,64},{128,96},{160,128},{192,160},{224,192},{33,... | collective-permute-start | bytes 3686408 | tf_op jit(solution)/shard_map/ppermute | solution.py:504
  25.3 26.7 %collective-permute-start.3 = (bf16[12,2,2,80,128]{4,3,2,1,0:T(8,128)(2,1)S(1)}, bf16[12,2,2,80,128]{4,3,2,1,0:T(8,128)(2,1)S(1)}, u32[]{:S(2)}, u32[]{:S(2)}) collective-permute-start(bf16[12,2,2,80,128]{4,3,2,1,0:T(8,128)(2,1)S(1)} %get-tuple-element.20), channel_id=1, source_target_pairs={{2,0},{4,2},{6,4},{8,6},{10,8},{12,10},{14,12},{16,14},{18,16},{20... | collective-permute-start | bytes 2949128 | tf_op jit(solution)/shard_map/ppermute | solution.py:509
  31.1 38.3 %collective-permute-start = (bf16[8,2,2,80,128]{4,3,2,1,0:T(8,128)(2,1)S(1)}, bf16[8,2,2,80,128]{4,3,2,1,0:T(8,128)(2,1)S(1)}, u32[]{:S(2)}, u32[]{:S(2)}) collective-permute-start(bf16[8,2,2,80,128]{4,3,2,1,0:T(8,128)(2,1)S(1)} %get-tuple-element.17), channel_id=1, source_target_pairs={{0,2},{2,4},{4,6},{6,8},{8,10},{10,12},{12,14},{14,16},{16,18},{18... | collective-permute-start | bytes 1966088 | tf_op jit(solution)/shard_map/ppermute | solution.py:508
  42.4 27.0 %collective-permute-start.2 = (bf16[8,2,2,80,128]{4,3,2,1,0:T(8,128)(2,1)S(1)}, bf16[8,2,2,80,128]{4,3,2,1,0:T(8,128)(2,1)S(1)}, u32[]{:S(2)}, u32[]{:S(2)}) collective-permute-start(bf16[8,2,2,80,128]{4,3,2,1,0:T(8,128)(2,1)S(1)} %get-tuple-element.19), channel_id=1, source_target_pairs={{2,0},{4,2},{6,4},{8,6},{10,8},{12,10},{14,12},{16,14},{18,16},{20... | collective-permute-start | bytes 1966088 | tf_op jit(solution)/shard_map/ppermute | solution.py:509
  62.4 41.4 %collective-permute-start.6 = (bf16[13,240,128]{2,1,0:T(8,128)(2,1)S(1)}, bf16[13,240,128]{2,1,0:T(8,128)(2,1)S(1)}, u32[]{:S(2)}, u32[]{:S(2)}) collective-permute-start(bf16[13,240,128]{2,1,0:T(8,128)(2,1)S(1)} %get-tuple-element.25), channel_id=1, source_target_pairs={{0,32},{32,64},{64,96},{96,128},{128,160},{160,192},{192,224},{1,3... | collective-permute-start | bytes 2396168 | tf_op jit(solution)/shard_map/ppermute | solution.py:515
  67.5 36.4 %collective-permute-start.7 = (bf16[13,240,128]{2,1,0:T(8,128)(2,1)S(1)}, bf16[13,240,128]{2,1,0:T(8,128)(2,1)S(1)}, u32[]{:S(2)}, u32[]{:S(2)}) collective-permute-start(bf16[13,240,128]{2,1,0:T(8,128)(2,1)S(1)} %get-tuple-element.26), channel_id=1, source_target_pairs={{32,0},{64,32},{96,64},{128,96},{160,128},{192,160},{224,192},{33,... | collective-permute-start | bytes 2396168 | tf_op jit(solution)/shard_map/ppermute | solution.py:515
  75.6 21.6 %collective-permute-start.8 = (bf16[9,240,128]{2,1,0:T(8,128)(2,1)S(1)}, bf16[9,240,128]{2,1,0:T(8,128)(2,1)S(1)}, u32[]{:S(2)}, u32[]{:S(2)}) collective-permute-start(bf16[9,240,128]{2,1,0:T(8,128)(2,1)S(1)} %get-tuple-element.27), channel_id=1, source_target_pairs={{0,32},{32,64},{64,96},{96,128},{128,160},{160,192},{192,224},{1,3... | collective-permute-start | bytes 1658888 | tf_op jit(solution)/shard_map/ppermute | solution.py:515
  80.4 20.1 %collective-permute-start.9 = (bf16[9,240,128]{2,1,0:T(8,128)(2,1)S(1)}, bf16[9,240,128]{2,1,0:T(8,128)(2,1)S(1)}, u32[]{:S(2)}, u32[]{:S(2)}) collective-permute-start(bf16[9,240,128]{2,1,0:T(8,128)(2,1)S(1)} %get-tuple-element.28), channel_id=1, source_target_pairs={{32,0},{64,32},{96,64},{128,96},{160,128},{192,160},{224,192},{33,... | collective-permute-start | bytes 1658888 | tf_op jit(solution)/shard_map/ppermute | solution.py:515

commit v2 on v0

v2 whole, which is shorter than its diff:
```python
import functools
import math

import jax
import jax.numpy as jnp
from jax import lax
from jax.experimental import pallas as pl
from jax.experimental.pallas import tpu as pltpu
from jax.sharding import PartitionSpec as P

HD = 128
W = 80
NH = 20
FIRST = 12
EPS = 1e-06
NEG = -1e30
FAR = 100
LOG2E = math.log2(math.e)
SCALE2 = LOG2E / math.sqrt(HD)
F32 = jnp.float32
BF16 = jnp.bfloat16


def params(mib=12):
    return pltpu.CompilerParams(vmem_limit_bytes=mib * 1024 * 1024)


def cost(microseconds):
    return pl.CostEstimate(flops=0, bytes_accessed=int(microseconds * 3_000_000), transcendentals=0)


def normed(raw, inverse, gain):
    return (raw.astype(F32) * inverse * gain).astype(BF16)


def lanes(g):
    return slice(g * HD, (g + 1) * HD)


def heads_spec(start, group):
    return pl.BlockSpec((2, 3, W, group * HD), lambda s, window: (0, 0, 0, start // group + s))


def gains_spec(start, group):
    return pl.BlockSpec((1, group * HD), lambda s, window: (0, start // group + s))


def whole(shape):
    return pl.BlockSpec(shape, lambda s, window: (0,) * len(shape))


def pack_queries_kernel(group, window, raw, gain, inverse, up, down):
    for g in range(group):
        q = normed(raw[:, :, :, lanes(g)], inverse[...], gain[:, lanes(g)].reshape(1, 1, 1, HD))
        up[g] = q[1].reshape(3 * W, HD)
        down[g] = q[0].reshape(3 * W, HD)


def pack_rows_kernel(group, window, keys, values, gain, inverse, up, down):
    for g in range(group):
        k_gain = gain[:, lanes(g)].reshape(1, 1, HD)
        for out, row in ((up, 2), (down, 0)):
            out[g, 0] = normed(keys[:, row, :, lanes(g)], inverse[:, row], k_gain)
            out[g, 1] = values[:, row, :, lanes(g)]


def group_of(start, count):
    return max(n for n in (1, 2, 4, 5) if count % n == 0 and start % n == 0)


def pack_queries(window, q, gain, inverse, start, count):
    group = group_of(start, count)
    out = jax.ShapeDtypeStruct((count, 3 * W, HD), BF16)
    out_spec = pl.BlockSpec((group, 3 * W, HD), lambda s, window: (s, 0, 0))
    return pl.pallas_call(
        functools.partial(pack_queries_kernel, group),
        grid_spec=pltpu.PrefetchScalarGridSpec(
            num_scalar_prefetch=1,
            grid=(count // group,),
            in_specs=[heads_spec(start, group), gains_spec(start, group), whole((2, 3, W, HD))],
            out_specs=[out_spec, out_spec],
        ),
        out_shape=[out, out],
        compiler_params=params(),
        cost_estimate=cost(0.1 * count),
        name="pack_queries",
    )(window, q, gain, inverse)


def pack_rows(window, k, v, gain, inverse, start, count):
    group = group_of(start, count)
    out = jax.ShapeDtypeStruct((count, 2, 2, W, HD), BF16)
    out_spec = pl.BlockSpec((group, 2, 2, W, HD), lambda s, window: (s, 0, 0, 0, 0))
    return pl.pallas_call(
        functools.partial(pack_rows_kernel, group),
        grid_spec=pltpu.PrefetchScalarGridSpec(
            num_scalar_prefetch=1,
            grid=(count // group,),
            in_specs=[heads_spec(start, group)] * 2 + [gains_spec(start, group), whole((2, 3, W, HD))],
            out_specs=[out_spec, out_spec],
        ),
        out_shape=[out, out],
        compiler_params=params(),
        cost_estimate=cost(0.15 * count),
        name="pack_rows",
    )(window, k, v, gain, inverse)


def fill_lines(kx, vx, k, v, inverse, gain, low, high):
    kn = normed(k, inverse, gain.reshape(1, 1, 1, HD))
    for j in range(2):
        kx[j, 0:W] = low[0, j]
        kx[j, W : 4 * W] = kn[j].reshape(3 * W, HD)
        kx[j, 4 * W : 5 * W] = high[0, j]
        vx[j, 0:W, 0:HD] = low[1, j]
        vx[j, W : 4 * W, 0:HD] = v[j].reshape(3 * W, HD)
        vx[j, 4 * W : 5 * W, 0:HD] = high[1, j]


def line_scratch(group):
    return [pltpu.VMEM((2, 5 * W, HD), BF16)] * group + [pltpu.VMEM((2, 5 * W, 2 * HD), BF16)] * group


def inside(axis):
    at = lax.axis_index(axis)
    return at > 0, at < lax.axis_size(axis) - 1


def fill_ones(values):
    for vx in values:
        vx[:, :, HD:] = jnp.ones((2, 5 * W, HD), BF16)


def fill_gaps(gaps):
    lane = lax.broadcasted_iota(jnp.int32, (W, 3 * W), 1)
    line = (lane >= W).astype(jnp.int32) + (lane >= 2 * W).astype(jnp.int32)
    key_tile = (lane - W * line) >> 3
    query_tile = lax.broadcasted_iota(jnp.int32, (W, 3 * W), 0) >> 3
    gap = jnp.abs(key_tile - query_tile)
    below, above = inside("height")
    no_low = jnp.where(below, 0, FAR)
    no_high = jnp.where(above, 0, FAR)
    for reach in range(2):
        for i in range(3):
            low = FAR if reach == 0 else (no_low if i == 0 else 0)
            high = FAR if reach == 0 else (no_high if i == 2 else 0)
            gaps[reach, i] = gap + jnp.where(line == 0, low, 0) + jnp.where(line == 2, high, 0)


def biases(gaps, window, head):
    reach_row, reach_tile = jnp.minimum(window[head, 1], 1), window[head, 2]
    return [jnp.where(gaps[reach_row, i] <= reach_tile, 0.0, NEG).astype(F32) for i in range(3)]


def dot_t(q, k):
    return lax.dot_general(q, k, (((1,), (1,)), ((), ())), preferred_element_type=F32)


def lines_of(i):
    return slice(i * W, (i + 3) * W)


def row_max(s):
    return jnp.max(s, axis=-1, keepdims=True)


def weights_of(s, top):
    return jnp.exp2((s - top) * SCALE2).astype(BF16)


def divided(mixed):
    total = mixed[:, HD:]
    inverse = pl.reciprocal(total, approx=True)
    inverse = inverse * (2.0 - total * inverse)
    return (mixed[:, :HD] * inverse).astype(BF16)


def mark(st, at, here, top, mixed):
    st[0, at] = jnp.where(here, top, st[0, at])
    st[1, at] = jnp.where(here, mixed[:, HD:], st[1, at])


def lse_of(st):
    return st[0] * SCALE2 + jnp.log(st[1]) * LOG2E


def pieces_of(full, lane):
    high = full.astype(BF16).astype(F32)
    rest = full - high
    middle = rest.astype(BF16).astype(F32)
    low = rest - middle
    return jnp.where(lane < 32, high, jnp.where(lane < 64, middle, jnp.where(lane < 96, low, 0.0))).astype(BF16)


def both_kernel(start, group, steps, window, *refs):
    st_own, st_far = refs[-2:]
    ob, oa, own_stats = refs[-6 - 2 * group : -3 - 2 * group]
    step = pl.program_id(0)

    @pl.when(step < steps)
    def _():
        both_step(start, group, step, window, *refs)

    @pl.when(step == steps)
    def _():
        lane = lax.broadcasted_iota(jnp.int32, (3 * W, HD), 1)
        for j in range(2):
            own_stats[j] = lse_of(st_own[j])
        ob[0] = pieces_of(lse_of(st_far[0]), lane)
        oa[0] = pieces_of(lse_of(st_far[1]), lane)


def both_step(start, group, step, window, *refs):
    qinverse, kinverse, qb, qa, q, k, v, qgain, kgain, low, high, part, ob, oa, _ = refs[:15]
    kxs, vxs = refs[15 : 15 + group], refs[15 + group : 15 + 2 * group]
    gaps, st_own, st_far = refs[-3:]
    slot = start + step * group

    @pl.when(step == 0)
    def _():
        for st in (st_own, st_far):
            for j in range(2):
                st[j, 0] = jnp.zeros((3 * W, HD), F32)
                st[j, 1] = jnp.ones((3 * W, HD), F32)
        fill_ones(vxs)
        fill_gaps(gaps)

    scores = []
    for g in range(group):
        own_keys, own_values = k[:, :, :, lanes(g)], v[:, :, :, lanes(g)]
        fill_lines(kxs[g], vxs[g], own_keys, own_values, kinverse[...], kgain[:, lanes(g)], low[g], high[g])
        masks = biases(gaps, window, slot + g)
        cross = jnp.where(window[slot + g, 0] > 0, 0.0, NEG)
        qn = normed(q[:, :, :, lanes(g)], qinverse[...], qgain[:, lanes(g)].reshape(1, 1, 1, HD))
        for i in range(3):
            own = qn[:, i].reshape(2 * W, HD)
            far = masks[i] + cross
            for j, far_q in ((0, qb), (1, qa)):
                queries = jnp.concatenate([own, far_q[g, i * W : (i + 1) * W]], axis=0)
                order = [masks[i], far, masks[i]] if j == 0 else [far, masks[i], masks[i]]
                raw = dot_t(queries, kxs[g][j, lines_of(i)])
                scores.append([raw[W * n : W * (n + 1)] + order[n] for n in range(3)])
    tops, weights = [], []
    for s0, s1 in zip(scores[::2], scores[1::2]):
        first, second = (row_max(jnp.maximum(s0[n], s1[n])) for n in range(2))
        below, above = row_max(s0[2]), row_max(s1[2])
        tops.append((jnp.concatenate([first, second], axis=0), below, above))
        for s, last in ((s0, below), (s1, above)):
            parts = [weights_of(a, b) for a, b in zip(s, (first, second, last))]
            weights.append(jnp.concatenate(parts, axis=0))
    lane = lax.broadcasted_iota(jnp.int32, (W, HD), 1)
    for g in range(group):
        here = (lane & 31) == step * group + g
        for i in range(3):
            w0, w1 = weights[6 * g + 2 * i : 6 * g + 2 * i + 2]
            top, top_b, top_a = tops[3 * g + i]
            m0 = jnp.dot(w0, vxs[g][0, lines_of(i)], preferred_element_type=F32)
            m1 = jnp.dot(w1, vxs[g][1, lines_of(i)], preferred_element_type=F32)
            at = slice(i * W, (i + 1) * W)
            for n in range(2):
                own = m0[W * n : W * (n + 1)] + m1[W * n : W * (n + 1)]
                part[g, n, i] = divided(own)
                mark(st_own.at[n], at, here, top[W * n : W * (n + 1)], own)
            for n, o, far, far_top in ((0, ob, m0[2 * W :], top_b), (1, oa, m1[2 * W :], top_a)):
                o[g, at] = divided(far)
                mark(st_far.at[n], at, here, far_top, far)


def both_partial(window, qb, qa, q, k, v, qgain, kgain, qinverse, kinverse, low, high, start, count):
    group = 2
    steps = count // group

    def step_of(s):
        return jnp.minimum(s, steps - 1)

    heads = pl.BlockSpec((2, 3, W, group * HD), lambda s, window: (0, 0, 0, start // group + step_of(s)))
    gains = pl.BlockSpec((1, group * HD), lambda s, window: (0, start // group + step_of(s)))
    rows = pl.BlockSpec((group, 2, 2, W, HD), lambda s, window: (step_of(s), 0, 0, 0, 0))
    q_spec = pl.BlockSpec((group, 3 * W, HD), lambda s, window: (step_of(s), 0, 0))
    o_spec = pl.BlockSpec((group, 3 * W, HD), lambda s, window: (s, 0, 0))
    out = jax.ShapeDtypeStruct((count + 1, 3 * W, HD), BF16)
    stat = pltpu.VMEM((2, 2, 3 * W, HD), F32)
    return pl.pallas_call(
        functools.partial(both_kernel, start, group, steps),
        grid_spec=pltpu.PrefetchScalarGridSpec(
            num_scalar_prefetch=1,
            grid=(steps + 1,),
            in_specs=[whole((2, 3, W, HD))] * 2 + [q_spec] * 2 + [heads] * 3 + [gains] * 2 + [rows] * 2,
            out_specs=[
                pl.BlockSpec((group, 2, 3, W, HD), lambda s, window: (step_of(s), 0, 0, 0, 0)),
                o_spec,
                o_spec,
                whole((2, 3 * W, HD)),
            ],
            scratch_shapes=line_scratch(group) + [pltpu.VMEM((2, 3, W, 3 * W), jnp.int32), stat, stat],
        ),
        out_shape=[
            jax.ShapeDtypeStruct((count, 2, 3, W, HD), BF16),
            out,
            out,
            jax.ShapeDtypeStruct((2, 3 * W, HD), F32),
        ],
        compiler_params=params(16),
        cost_estimate=cost(1.1 * count),
        name="both_partial",
    )(window, qinverse, kinverse, qb, qa, q, k, v, qgain, kgain, low, high)


def merge_kernel(start, group, window, part, lse, ob, oa, sb, sa, *refs):
    out, shares = refs[-2:]
    lane = lax.broadcasted_iota(jnp.int32, (3 * W, HD), 1)
    neighbours = inside("frame")
    step = pl.program_id(0)

    @pl.when(step == 0)
    def _():
        for j, st in ((0, sb), (1, sa)):
            pieces = st[0].astype(F32)
            other = pieces + pltpu.roll(pieces, HD - 32, 1) + pltpu.roll(pieces, HD - 64, 1)
            other = jnp.where(neighbours[j], other, NEG)
            own = lse[j]
            top = jnp.maximum(own, other)
            own_weight = jnp.exp2(own - top)
            other_weight = jnp.exp2(other - top)
            scale = 1.0 / (own_weight + other_weight)
            shares[j, 0] = own_weight * scale
            shares[j, 1] = other_weight * scale

    for g in range(group):
        here = lane == step * group + g
        for j, o in ((0, ob), (1, oa)):
            use = (window[start + step * group + g, 0] > 0) & neighbours[j]
            own = jnp.sum(jnp.where(here, shares[j, 0], 0.0), axis=1, keepdims=True)
            other = jnp.sum(jnp.where(here, shares[j, 1], 0.0), axis=1, keepdims=True)
            own = jnp.where(use, own, 1.0)
            other = jnp.where(use, other, 0.0)
            far = jnp.where(use, o[g].astype(F32), 0.0)
            mixed = part[g, j].reshape(3 * W, HD).astype(F32) * own + far * other
            out[j, :, :, lanes(g)] = mixed.astype(BF16).reshape(3, W, HD)


def merge(window, out, part, lse, o_below, o_above, start, count):
    group = group_of(start, count)
    o_spec = pl.BlockSpec((group, 3 * W, HD), lambda s, window: (s, 0, 0))
    stat_spec = pl.BlockSpec((1, 3 * W, HD), lambda s, window: (count, 0, 0))
    return pl.pallas_call(
        functools.partial(merge_kernel, start, group),
        grid_spec=pltpu.PrefetchScalarGridSpec(
            num_scalar_prefetch=1,
            grid=(count // group,),
            in_specs=[
                pl.BlockSpec((group, 2, 3, W, HD), lambda s, window: (s, 0, 0, 0, 0)),
                whole((2, 3 * W, HD)),
                o_spec,
                o_spec,
                stat_spec,
                stat_spec,
            ]
            + ([] if out is None else [pl.BlockSpec(memory_space=pl.ANY)]),
            out_specs=heads_spec(start, group),
            scratch_shapes=[pltpu.VMEM((2, 2, 3 * W, HD), F32)],
        ),
        out_shape=jax.ShapeDtypeStruct((2, 3, W, NH * HD), BF16),
        input_output_aliases={} if out is None else {7: 0},
        compiler_params=params(),
        cost_estimate=cost(0.25 * count),
        name="merge",
    )(window, part, lse, o_below, o_above, o_below, o_above, *([] if out is None else [out]))


def shifts(axis):
    count = lax.axis_size(axis)
    forward = [(i, i + 1) for i in range(count - 1)]
    return forward, [(b, a) for a, b in forward]


def attention(window, q, k, v, q_gain, k_gain, q_inverse, k_inverse):
    up_frame, down_frame = shifts("frame")
    up_row, down_row = shifts("height")
    norms = (q_gain, k_gain, q_inverse, k_inverse)
    chunks = ((0, FIRST), (FIRST, NH - FIRST))
    queries, rows = [], []
    for start, count in chunks:
        rows_up, rows_down = pack_rows(window, k, v, k_gain, k_inverse, start, count)
        rows.append((lax.ppermute(rows_up, "height", up_row), lax.ppermute(rows_down, "height", down_row)))
        q, rows_up, rows_down = lax.optimization_barrier((q, rows_up, rows_down))
        q_up, q_down = pack_queries(window, q, q_gain, q_inverse, start, count)
        queries.append((lax.ppermute(q_up, "frame", up_frame), lax.ppermute(q_down, "frame", down_frame)))
        k, q_up, q_down = lax.optimization_barrier((k, q_up, q_down))
    parts = []
    for n, (start, count) in enumerate(chunks):
        part, ob, oa, lse = both_partial(window, *queries[n], q, k, v, *norms, *rows[n], start, count)
        below, above = lax.ppermute(oa, "frame", up_frame), lax.ppermute(ob, "frame", down_frame)
        parts.append((part, lse, below, above, start, count))
    out = None
    for part in parts:
        out = merge(window, out, *part)
    return out


def squares_of(raw):
    values = raw.astype(F32)
    return jnp.sum(values * values, axis=-1)


def body(q, k, v, q_gain, k_gain, window):
    width_total = q.shape[3] * lax.axis_size("head")
    query_sum, key_sum = lax.psum((squares_of(q), squares_of(k)), "head")

    def inverse_of(total):
        return jnp.broadcast_to(lax.rsqrt(total / width_total + EPS)[..., None], (2, 3, W, HD))

    return attention(
        window, q, k, v, q_gain[None], k_gain[None], inverse_of(query_sum), inverse_of(key_sum)
    )


def solution(mesh):
    placed = (
        P("frame", "height", None, "head"),
        P("frame", "height", None, "head"),
        P("frame", "height", None, "head"),
        P("head"),
        P("head"),
        P("head", None),
    )
    return jax.shard_map(
        body,
        mesh=mesh,
        in_specs=placed,
        out_specs=P("frame", "height", None, "head"),
        check_vma=False,
    )
```

time: 337 us -> 101 us (0.30)
  the two profiles are of different devices: /device:TPU:38 before, /device:TPU:120 now
where the time goes in v2:
time: 101 us
  starting transfers between devices  40.2 us (40%)
  Pallas kernels  31.7 us (31%)
  waiting for transfers between devices  20.2 us (20%)
  other arithmetic  3.65 us (4%)
  blocking collectives  2.5 us (2%)
  local copies, waits for them, and re-layouts  2.06 us (2%)
    pallas_call x2, Pallas kernels, both_partial(): pl.pallas_call(functools.partial(both_kernel, start, group, steps), grid_...  20 us
    ppermute x2, starting transfers between devices, attention(): lax.ppermute(oa, 'frame', up_frame)  10.3 us
    ppermute x2, starting transfers between devices, attention(): lax.ppermute(q_up, 'frame', up_frame)  10.2 us
    ppermute x2, waiting for transfers between devices, attention(): lax.ppermute(ob, 'frame', down_frame)  9.39 us
    pallas_call x2, Pallas kernels, merge(): pl.pallas_call(functools.partial(merge_kernel, start, group), grid_spec=p...  6.75 us
    ppermute x2, starting transfers between devices, attention(): lax.ppermute(rows_up, 'height', up_row)  6.53 us
    ppermute x2, starting transfers between devices, attention(): lax.ppermute(rows_down, 'height', down_row)  5.56 us
    ppermute x2, waiting for transfers between devices, attention(): lax.ppermute(rows_down, 'height', down_row)  4.79 us
  transfers between devices with their start and end apart: 12, of which 6 were waited for; matrix products, arithmetic and copies ran while one was open for 0% of the time, Pallas kernels for 27%

profile of v2, /device:TPU:120, one launch (start us, length us, event | category | flops | bytes accessed | tf_op | source)
XLA Modules:
  0.0 100.7 jit_solution(11621849251617902253)
XLA Ops:
  0.0 3.6 %multiply_reduce_fusion = (f32[2,3,80]{2,1,0:T(4,128)S(1)}, f32[2,3,80]{2,1,0:T(4,128)S(1)}) fusion(bf16[2,3,80,2560]{3,2,1,0:T(8,128)(2,1)} %refs_5_.1, bf16[2,3,80,2560]{3,2,1,0:T(8,128)(2,1)} %refs_4_.1), kind=kLoop, calls=%fused_computation | loop fusion | flops 7371840 | bytes 4919040 | tf_op jit(solution)/shard_map/reduce_sum | solution.py:403
  3.6 2.5 %all-reduce = (f32[2,3,80]{2,1,0:T(4,128)S(1)}, f32[2,3,80]{2,1,0:T(4,128)S(1)}) all-reduce(f32[2,3,80]{2,1,0:T(4,128)S(1)} %get-tuple-element.48, f32[2,3,80]{2,1,0:T(4,128)S(1)} %get-tuple-element.47), channel_id=1, replica_groups=mesh['frame'=8,'height'=16,'head'=2] {'head'}, use_global_device_ids=true, to_apply=%region_1.0 | all-reduce | flops 960 | bytes 7680 | tf_op jit(solution)/shard_map/psum | solution.py:408
  6.2 0.1 copy.15.window
  6.3 0.1 broadcast_in_dim.9.inverse.refs_1_
  6.4 1.7 %copy-done.2 = bf16[2,3,80,2560]{3,2,1,0:T(8,128)(2,1)S(1)} copy-done((bf16[2,3,80,2560]{3,2,1,0:T(8,128)(2,1)S(1)}, bf16[2,3,80,2560]{3,2,1,0:T(8,128)(2,1)}, u32[]{:S(2)}) %copy-start.2) | copy-done | bytes 2457624
  8.1 1.3 %pack_rows.2 = (bf16[12,2,2,80,128]{4,3,2,1,0:T(8,128)(2,1)S(1)}, bf16[12,2,2,80,128]{4,3,2,1,0:T(8,128)(2,1)S(1)}) custom-call(s32[20,3]{1,0:T(8,128)S(1)} %copy.15.window, bf16[2,3,80,2560]{3,2,1,0:T(8,128)(2,1)S(1)} %copy-done, bf16[2,3,80,2560]{3,2,1,0:T(8,128)(2,1)S(1)} %copy-done.2, f32[1,2560]{1,0:T(1,128)S(1)} %broadcast_in_dim.20.gain.refs_8_, ...), custom_call_target="tpu_custom_call" | custom-call | bytes 5399999 | tf_op jit(solution)/shard_map/pack_rows/pallas_call | solution.py:94
  9.5 3.1 %collective-permute-start.8 = (bf16[12,2,2,80,128]{4,3,2,1,0:T(8,128)(2,1)S(1)}, bf16[12,2,2,80,128]{4,3,2,1,0:T(8,128)(2,1)S(1)}, u32[]{:S(2)}, u32[]{:S(2)}) collective-permute-start(bf16[12,2,2,80,128]{4,3,2,1,0:T(8,128)(2,1)S(1)} %get-tuple-element.25), channel_id=1, source_target_pairs={{0,2},{2,4},{4,6},{6,8},{8,10},{10,12},{12,14},{14,16},{16,18},{18... | collective-permute-start | bytes 2949128 | tf_op jit(solution)/shard_map/ppermute | solution.py:385
  12.6 0.1 broadcast_in_dim.8.inverse.refs_0_
  12.7 1.3 %pack_queries.2 = (bf16[12,240,128]{2,1,0:T(8,128)(2,1)S(1)}, bf16[12,240,128]{2,1,0:T(8,128)(2,1)S(1)}) custom-call(s32[20,3]{1,0:T(8,128)S(1)} %copy.15.window, bf16[2,3,80,2560]{3,2,1,0:T(8,128)(2,1)S(1)} %copy-done.1, f32[1,2560]{1,0:T(1,128)S(1)} %broadcast_in_dim.21.gain.refs_7_, f32[2,3,80,128]{3,2,1,0:T(8,128)S(1)} %broadcast_in_dim.8.inverse.refs_0_), custom_call_target="tpu_custom_call" | custom-call | bytes 3600000 | tf_op jit(solution)/shard_map/pack_queries/pallas_call | solution.py:75
  14.0 5.0 %collective-permute-start.6 = (bf16[12,240,128]{2,1,0:T(8,128)(2,1)S(1)}, bf16[12,240,128]{2,1,0:T(8,128)(2,1)S(1)}, u32[]{:S(2)}, u32[]{:S(2)}) collective-permute-start(bf16[12,240,128]{2,1,0:T(8,128)(2,1)S(1)} %get-tuple-element.28), channel_id=1, source_target_pairs={{0,32},{32,64},{64,96},{96,128},{128,160},{160,192},{192,224},{1,3... | collective-permute-start | bytes 2211848 | tf_op jit(solution)/shard_map/ppermute | solution.py:388
  19.0 1.9 %collective-permute-start.7 = (bf16[12,240,128]{2,1,0:T(8,128)(2,1)S(1)}, bf16[12,240,128]{2,1,0:T(8,128)(2,1)S(1)}, u32[]{:S(2)}, u32[]{:S(2)}) collective-permute-start(bf16[12,240,128]{2,1,0:T(8,128)(2,1)S(1)} %get-tuple-element.29), channel_id=1, source_target_pairs={{32,0},{64,32},{96,64},{128,96},{160,128},{192,160},{224,192},{33,... | collective-permute-start | bytes 2211848 | tf_op jit(solution)/shard_map/ppermute | solution.py:388
  21.0 2.8 %collective-permute-start.9 = (bf16[12,2,2,80,128]{4,3,2,1,0:T(8,128)(2,1)S(1)}, bf16[12,2,2,80,128]{4,3,2,1,0:T(8,128)(2,1)S(1)}, u32[]{:S(2)}, u32[]{:S(2)}) collective-permute-start(bf16[12,2,2,80,128]{4,3,2,1,0:T(8,128)(2,1)S(1)} %get-tuple-element.26), channel_id=1, source_target_pairs={{2,0},{4,2},{6,4},{8,6},{10,8},{12,10},{14,12},{16,14},{18,16},{20... | collective-permute-start | bytes 2949128 | tf_op jit(solution)/shard_map/ppermute | solution.py:385
  23.8 1.2 %pack_rows.3 = (bf16[8,2,2,80,128]{4,3,2,1,0:T(8,128)(2,1)S(1)}, bf16[8,2,2,80,128]{4,3,2,1,0:T(8,128)(2,1)S(1)}) custom-call(s32[20,3]{1,0:T(8,128)S(1)} %copy.15.window, bf16[2,3,80,2560]{3,2,1,0:T(8,128)(2,1)S(1)} %copy-done, bf16[2,3,80,2560]{3,2,1,0:T(8,128)(2,1)S(1)} %copy-done.2, f32[1,2560]{1,0:T(1,128)S(1)} %broadcast_in_dim.20.gain.refs_8_, ...), custom_call_target="tpu_custom_call" | custom-call | bytes 3600000 | tf_op jit(solution)/shard_map/pack_rows/pallas_call | solution.py:94
  24.9 1.1 %pack_queries.3 = (bf16[8,240,128]{2,1,0:T(8,128)(2,1)S(1)}, bf16[8,240,128]{2,1,0:T(8,128)(2,1)S(1)}) custom-call(s32[20,3]{1,0:T(8,128)S(1)} %copy.15.window, bf16[2,3,80,2560]{3,2,1,0:T(8,128)(2,1)S(1)} %copy-done.1, f32[1,2560]{1,0:T(1,128)S(1)} %broadcast_in_dim.21.gain.refs_7_, f32[2,3,80,128]{3,2,1,0:T(8,128)S(1)} %broadcast_in_dim.8.inverse.refs_0_), custom_call_target="tpu_custom_call" | custom-call | bytes 2400000 | tf_op jit(solution)/shard_map/pack_queries/pallas_call | solution.py:75
  26.1 5.1 %collective-permute-start = (bf16[8,240,128]{2,1,0:T(8,128)(2,1)S(1)}, bf16[8,240,128]{2,1,0:T(8,128)(2,1)S(1)}, u32[]{:S(2)}, u32[]{:S(2)}) collective-permute-start(bf16[8,240,128]{2,1,0:T(8,128)(2,1)S(1)} %get-tuple-element.34), channel_id=1, source_target_pairs={{0,32},{32,64},{64,96},{96,128},{128,160},{160,192},{192,224},{1,3... | collective-permute-start | bytes 1474568 | tf_op jit(solution)/shard_map/ppermute | solution.py:388
  31.2 4.7 %collective-permute-done.6.refs_2_ = bf16[12,240,128]{2,1,0:T(8,128)(2,1)S(1)} collective-permute-done((bf16[12,240,128]{2,1,0:T(8,128)(2,1)S(1)}, bf16[12,240,128]{2,1,0:T(8,128)(2,1)S(1)}, u32[]{:S(2)}, u32[]{:S(2)}) %collective-permute-start.6) | collective-permute-done | bytes 737312 | tf_op jit(solution)/shard_map/ppermute | solution.py:388
  35.9 3.5 %collective-permute-start.2 = (bf16[8,2,2,80,128]{4,3,2,1,0:T(8,128)(2,1)S(1)}, bf16[8,2,2,80,128]{4,3,2,1,0:T(8,128)(2,1)S(1)}, u32[]{:S(2)}, u32[]{:S(2)}) collective-permute-start(bf16[8,2,2,80,128]{4,3,2,1,0:T(8,128)(2,1)S(1)} %get-tuple-element.31), channel_id=1, source_target_pairs={{0,2},{2,4},{4,6},{6,8},{8,10},{10,12},{12,14},{14,16},{16,18},{18... | collective-permute-start | bytes 1966088 | tf_op jit(solution)/shard_map/ppermute | solution.py:385
  39.4 0.8 collective-permute-done.7.refs_3_
  40.2 2.8 %collective-permute-start.3 = (bf16[8,2,2,80,128]{4,3,2,1,0:T(8,128)(2,1)S(1)}, bf16[8,2,2,80,128]{4,3,2,1,0:T(8,128)(2,1)S(1)}, u32[]{:S(2)}, u32[]{:S(2)}) collective-permute-start(bf16[8,2,2,80,128]{4,3,2,1,0:T(8,128)(2,1)S(1)} %get-tuple-element.32), channel_id=1, source_target_pairs={{2,0},{4,2},{6,4},{8,6},{10,8},{12,10},{14,12},{16,14},{18,16},{20... | collective-permute-start | bytes 1966088 | tf_op jit(solution)/shard_map/ppermute | solution.py:385
  42.9 1.9 %collective-permute-start.1 = (bf16[8,240,128]{2,1,0:T(8,128)(2,1)S(1)}, bf16[8,240,128]{2,1,0:T(8,128)(2,1)S(1)}, u32[]{:S(2)}, u32[]{:S(2)}) collective-permute-start(bf16[8,240,128]{2,1,0:T(8,128)(2,1)S(1)} %get-tuple-element.35), channel_id=1, source_target_pairs={{32,0},{64,32},{96,64},{128,96},{160,128},{192,160},{224,192},{33,... | collective-permute-start | bytes 1474568 | tf_op jit(solution)/shard_map/ppermute | solution.py:388
  44.9 4.8 %collective-permute-done.9.refs_10_ = bf16[12,2,2,80,128]{4,3,2,1,0:T(8,128)(2,1)S(1)} collective-permute-done((bf16[12,2,2,80,128]{4,3,2,1,0:T(8,128)(2,1)S(1)}, bf16[12,2,2,80,128]{4,3,2,1,0:T(8,128)(2,1)S(1)}, u32[]{:S(2)}, u32[]{:S(2)}) %collective-permute-start.9) | collective-permute-done | bytes 983072 | tf_op jit(solution)/shard_map/ppermute | solution.py:385
  49.7 11.7 %both_partial.3 = (bf16[12,2,3,80,128]{4,3,2,1,0:T(8,128)(2,1)S(1)}, bf16[13,240,128]{2,1,0:T(8,128)(2,1)S(1)}, bf16[13,240,128]{2,1,0:T(8,128)(2,1)S(1)}, f32[2,240,128]{2,1,0:T(8,128)S(1)}) custom-call(s32[20,3]{1,0:T(8,128)S(1)} %copy.15.window, f32[2,3,80,128]{3,2,1,0:T(8,128)S(1)} %broadcast_in_dim.8.inverse.refs_0_, ...), custom_call_target="tpu_custom_call" | custom-call | bytes 39600000 | tf_op jit(solution)/shard_map/both_partial/pallas_call | solution.py:283
  61.4 5.1 %collective-permute-start.10 = (bf16[13,240,128]{2,1,0:T(8,128)(2,1)S(1)}, bf16[13,240,128]{2,1,0:T(8,128)(2,1)S(1)}, u32[]{:S(2)}, u32[]{:S(2)}) collective-permute-start(bf16[13,240,128]{2,1,0:T(8,128)(2,1)S(1)} %get-tuple-element.43), channel_id=1, source_target_pairs={{0,32},{32,64},{64,96},{96,128},{128,160},{160,192},{192,224},{1,3... | collective-permute-start | bytes 2396168 | tf_op jit(solution)/shard_map/ppermute | solution.py:393
  66.6 1.9 %collective-permute-start.11 = (bf16[13,240,128]{2,1,0:T(8,128)(2,1)S(1)}, bf16[13,240,128]{2,1,0:T(8,128)(2,1)S(1)}, u32[]{:S(2)}, u32[]{:S(2)}) collective-permute-start(bf16[13,240,128]{2,1,0:T(8,128)(2,1)S(1)} %get-tuple-element.44), channel_id=1, source_target_pairs={{32,0},{64,32},{96,64},{128,96},{160,128},{192,160},{224,192},{33,... | collective-permute-start | bytes 2396168 | tf_op jit(solution)/shard_map/ppermute | solution.py:393
  68.5 8.3 %both_partial.2 = (bf16[8,2,3,80,128]{4,3,2,1,0:T(8,128)(2,1)S(1)}, bf16[9,240,128]{2,1,0:T(8,128)(2,1)S(1)}, bf16[9,240,128]{2,1,0:T(8,128)(2,1)S(1)}, f32[2,240,128]{2,1,0:T(8,128)S(1)}) custom-call(s32[20,3]{1,0:T(8,128)S(1)} %copy.15.window, f32[2,3,80,128]{3,2,1,0:T(8,128)S(1)} %broadcast_in_dim.8.inverse.refs_0_, ...), custom_call_target="tpu_custom_call" | custom-call | bytes 26400000 | tf_op jit(solution)/shard_map/both_partial/pallas_call | solution.py:283
  76.8 5.1 %collective-permute-start.4 = (bf16[9,240,128]{2,1,0:T(8,128)(2,1)S(1)}, bf16[9,240,128]{2,1,0:T(8,128)(2,1)S(1)}, u32[]{:S(2)}, u32[]{:S(2)}) collective-permute-start(bf16[9,240,128]{2,1,0:T(8,128)(2,1)S(1)} %get-tuple-element.39), channel_id=1, source_target_pairs={{0,32},{32,64},{64,96},{96,128},{128,160},{160,192},{192,224},{1,3... | collective-permute-start | bytes 1658888 | tf_op jit(solution)/shard_map/ppermute | solution.py:393
  82.0 1.9 %collective-permute-start.5 = (bf16[9,240,128]{2,1,0:T(8,128)(2,1)S(1)}, bf16[9,240,128]{2,1,0:T(8,128)(2,1)S(1)}, u32[]{:S(2)}, u32[]{:S(2)}) collective-permute-start(bf16[9,240,128]{2,1,0:T(8,128)(2,1)S(1)} %get-tuple-element.40), channel_id=1, source_target_pairs={{32,0},{64,32},{96,64},{128,96},{160,128},{192,160},{224,192},{33,... | collective-permute-start | bytes 1658888 | tf_op jit(solution)/shard_map/ppermute | solution.py:393
  83.9 4.0 %collective-permute-done.11.oa.sa = bf16[13,240,128]{2,1,0:T(8,128)(2,1)S(1)} collective-permute-done((bf16[13,240,128]{2,1,0:T(8,128)(2,1)S(1)}, bf16[13,240,128]{2,1,0:T(8,128)(2,1)S(1)}, u32[]{:S(2)}, u32[]{:S(2)}) %collective-permute-start.11) | collective-permute-done | bytes 798752 | tf_op jit(solution)/shard_map/ppermute | solution.py:393
  88.0 3.8 %merge.2.refs_0_ = bf16[2,3,80,2560]{3,2,1,0:T(8,128)(2,1)} custom-call(s32[20,3]{1,0:T(8,128)S(1)} %copy.15.window, bf16[12,2,3,80,128]{4,3,2,1,0:T(8,128)(2,1)S(1)} %get-tuple-element.41.part, f32[2,240,128]{2,1,0:T(8,128)S(1)} %get-tuple-element.42.lse, bf16[13,240,128]{2,1,0:T(8,128)(2,1)S(1)} %collective-permute-done.10.ob.sb, ...), custom_call_target="tpu_custom_call" | custom-call | bytes 9000000 | tf_op jit(solution)/shard_map/merge/pallas_call | solution.py:346
  91.7 0.6 collective-permute-done.4.ob.sb
  92.3 5.3 %collective-permute-done.5.oa.sa = bf16[9,240,128]{2,1,0:T(8,128)(2,1)S(1)} collective-permute-done((bf16[9,240,128]{2,1,0:T(8,128)(2,1)S(1)}, bf16[9,240,128]{2,1,0:T(8,128)(2,1)S(1)}, u32[]{:S(2)}, u32[]{:S(2)}) %collective-permute-start.5) | collective-permute-done | bytes 552992 | tf_op jit(solution)/shard_map/ppermute | solution.py:393
  97.7 3.0 %merge.3 = bf16[2,3,80,2560]{3,2,1,0:T(8,128)(2,1)} custom-call(s32[20,3]{1,0:T(8,128)S(1)} %copy.15.window, bf16[8,2,3,80,128]{4,3,2,1,0:T(8,128)(2,1)S(1)} %get-tuple-element.37.part, f32[2,240,128]{2,1,0:T(8,128)S(1)} %get-tuple-element.38.lse, bf16[9,240,128]{2,1,0:T(8,128)(2,1)S(1)} %collective-permute-done.4.ob.sb, ...), custom_call_target="tpu_custom_call", output_to_operand_aliasing={{}: (7, {})} | custom-call | bytes 6000000 | tf_op jit(solution)/shard_map/merge/pallas_call | solution.py:346
  (23 shorter events, 0.1 us)
Async XLA Ops:
  0.0 6.4 %copy-start = (bf16[2,3,80,2560]{3,2,1,0:T(8,128)(2,1)S(1)}, bf16[2,3,80,2560]{3,2,1,0:T(8,128)(2,1)}, u32[]{:S(2)}) copy-start(bf16[2,3,80,2560]{3,2,1,0:T(8,128)(2,1)} %refs_5_.1) | copy-start | bytes 7372804
  0.0 6.2 %copy-start.4 = (f32[2560]{0:T(1024)S(1)}, f32[2560]{0:T(1024)}, u32[]{:S(2)}) copy-start(f32[2560]{0:T(1024)} %param.10) | copy-start | bytes 30724
  0.0 6.2 %copy-start.6 = (s32[20,3]{0,1:T(4,128)S(1)}, s32[20,3]{0,1:T(4,128)}, u32[]{:S(2)}) copy-start(s32[20,3]{0,1:T(4,128)} %param.11) | copy-start | bytes 724
  6.4 1.7 %copy-start.2 = (bf16[2,3,80,2560]{3,2,1,0:T(8,128)(2,1)S(1)}, bf16[2,3,80,2560]{3,2,1,0:T(8,128)(2,1)}, u32[]{:S(2)}) copy-start(bf16[2,3,80,2560]{3,2,1,0:T(8,128)(2,1)} %refs_6_.3) | copy-start | bytes 7372804
  8.1 4.4 %copy-start.5 = (f32[2560]{0:T(1024)S(1)}, f32[2560]{0:T(1024)}, u32[]{:S(2)}) copy-start(f32[2560]{0:T(1024)} %param.9) | copy-start | bytes 30724
  8.1 4.6 %copy-start.1 = (bf16[2,3,80,2560]{3,2,1,0:T(8,128)(2,1)S(1)}, bf16[2,3,80,2560]{3,2,1,0:T(8,128)(2,1)}, u32[]{:S(2)}) copy-start(bf16[2,3,80,2560]{3,2,1,0:T(8,128)(2,1)} %refs_4_.1) | copy-start | bytes 7372804
  9.5 33.5 %collective-permute-start.8 = (bf16[12,2,2,80,128]{4,3,2,1,0:T(8,128)(2,1)S(1)}, bf16[12,2,2,80,128]{4,3,2,1,0:T(8,128)(2,1)S(1)}, u32[]{:S(2)}, u32[]{:S(2)}) collective-permute-start(bf16[12,2,2,80,128]{4,3,2,1,0:T(8,128)(2,1)S(1)} %get-tuple-element.25), channel_id=1, source_target_pairs={{0,2},{2,4},{4,6},{6,8},{8,10},{10,12},{12,14},{14,16},{16,18},{18... | collective-permute-start | bytes 2949128 | tf_op jit(solution)/shard_map/ppermute | solution.py:385
  14.0 21.9 %collective-permute-start.6 = (bf16[12,240,128]{2,1,0:T(8,128)(2,1)S(1)}, bf16[12,240,128]{2,1,0:T(8,128)(2,1)S(1)}, u32[]{:S(2)}, u32[]{:S(2)}) collective-permute-start(bf16[12,240,128]{2,1,0:T(8,128)(2,1)S(1)} %get-tuple-element.28), channel_id=1, source_target_pairs={{0,32},{32,64},{64,96},{96,128},{128,160},{160,192},{192,224},{1,3... | collective-permute-start | bytes 2211848 | tf_op jit(solution)/shard_map/ppermute | solution.py:388
  19.0 21.1 %collective-permute-start.7 = (bf16[12,240,128]{2,1,0:T(8,128)(2,1)S(1)}, bf16[12,240,128]{2,1,0:T(8,128)(2,1)S(1)}, u32[]{:S(2)}, u32[]{:S(2)}) collective-permute-start(bf16[12,240,128]{2,1,0:T(8,128)(2,1)S(1)} %get-tuple-element.29), channel_id=1, source_target_pairs={{32,0},{64,32},{96,64},{128,96},{160,128},{192,160},{224,192},{33,... | collective-permute-start | bytes 2211848 | tf_op jit(solution)/shard_map/ppermute | solution.py:388
  21.0 28.7 %collective-permute-start.9 = (bf16[12,2,2,80,128]{4,3,2,1,0:T(8,128)(2,1)S(1)}, bf16[12,2,2,80,128]{4,3,2,1,0:T(8,128)(2,1)S(1)}, u32[]{:S(2)}, u32[]{:S(2)}) collective-permute-start(bf16[12,2,2,80,128]{4,3,2,1,0:T(8,128)(2,1)S(1)} %get-tuple-element.26), channel_id=1, source_target_pairs={{2,0},{4,2},{6,4},{8,6},{10,8},{12,10},{14,12},{16,14},{18,16},{20... | collective-permute-start | bytes 2949128 | tf_op jit(solution)/shard_map/ppermute | solution.py:385
  24.9 24.7 %copy-start.3 = (bf16[2,3,80,2560]{3,2,1,0:T(8,128)(2,1)S(1)}, bf16[2,3,80,2560]{3,2,1,0:T(8,128)(2,1)}, u32[]{:S(2)}) copy-start(bf16[2,3,80,2560]{3,2,1,0:T(8,128)(2,1)} %refs_6_.3) | copy-start | bytes 7372804
  26.1 40.5 %collective-permute-start = (bf16[8,240,128]{2,1,0:T(8,128)(2,1)S(1)}, bf16[8,240,128]{2,1,0:T(8,128)(2,1)S(1)}, u32[]{:S(2)}, u32[]{:S(2)}) collective-permute-start(bf16[8,240,128]{2,1,0:T(8,128)(2,1)S(1)} %get-tuple-element.34), channel_id=1, source_target_pairs={{0,32},{32,64},{64,96},{96,128},{128,160},{160,192},{192,224},{1,3... | collective-permute-start | bytes 1474568 | tf_op jit(solution)/shard_map/ppermute | solution.py:388
  35.9 32.6 %collective-permute-start.2 = (bf16[8,2,2,80,128]{4,3,2,1,0:T(8,128)(2,1)S(1)}, bf16[8,2,2,80,128]{4,3,2,1,0:T(8,128)(2,1)S(1)}, u32[]{:S(2)}, u32[]{:S(2)}) collective-permute-start(bf16[8,2,2,80,128]{4,3,2,1,0:T(8,128)(2,1)S(1)} %get-tuple-element.31), channel_id=1, source_target_pairs={{0,2},{2,4},{4,6},{6,8},{8,10},{10,12},{12,14},{14,16},{16,18},{18... | collective-permute-start | bytes 1966088 | tf_op jit(solution)/shard_map/ppermute | solution.py:385
  40.2 28.4 %collective-permute-start.3 = (bf16[8,2,2,80,128]{4,3,2,1,0:T(8,128)(2,1)S(1)}, bf16[8,2,2,80,128]{4,3,2,1,0:T(8,128)(2,1)S(1)}, u32[]{:S(2)}, u32[]{:S(2)}) collective-permute-start(bf16[8,2,2,80,128]{4,3,2,1,0:T(8,128)(2,1)S(1)} %get-tuple-element.32), channel_id=1, source_target_pairs={{2,0},{4,2},{6,4},{8,6},{10,8},{12,10},{14,12},{16,14},{18,16},{20... | collective-permute-start | bytes 1966088 | tf_op jit(solution)/shard_map/ppermute | solution.py:385
  42.9 25.5 %collective-permute-start.1 = (bf16[8,240,128]{2,1,0:T(8,128)(2,1)S(1)}, bf16[8,240,128]{2,1,0:T(8,128)(2,1)S(1)}, u32[]{:S(2)}, u32[]{:S(2)}) collective-permute-start(bf16[8,240,128]{2,1,0:T(8,128)(2,1)S(1)} %get-tuple-element.35), channel_id=1, source_target_pairs={{32,0},{64,32},{96,64},{128,96},{160,128},{192,160},{224,192},{33,... | collective-permute-start | bytes 1474568 | tf_op jit(solution)/shard_map/ppermute | solution.py:388
  61.4 22.5 %collective-permute-start.10 = (bf16[13,240,128]{2,1,0:T(8,128)(2,1)S(1)}, bf16[13,240,128]{2,1,0:T(8,128)(2,1)S(1)}, u32[]{:S(2)}, u32[]{:S(2)}) collective-permute-start(bf16[13,240,128]{2,1,0:T(8,128)(2,1)S(1)} %get-tuple-element.43), channel_id=1, source_target_pairs={{0,32},{32,64},{64,96},{96,128},{128,160},{160,192},{192,224},{1,3... | collective-permute-start | bytes 2396168 | tf_op jit(solution)/shard_map/ppermute | solution.py:393
  66.6 21.4 %collective-permute-start.11 = (bf16[13,240,128]{2,1,0:T(8,128)(2,1)S(1)}, bf16[13,240,128]{2,1,0:T(8,128)(2,1)S(1)}, u32[]{:S(2)}, u32[]{:S(2)}) collective-permute-start(bf16[13,240,128]{2,1,0:T(8,128)(2,1)S(1)} %get-tuple-element.44), channel_id=1, source_target_pairs={{32,0},{64,32},{96,64},{128,96},{160,128},{192,160},{224,192},{33,... | collective-permute-start | bytes 2396168 | tf_op jit(solution)/shard_map/ppermute | solution.py:393
  76.8 15.5 %collective-permute-start.4 = (bf16[9,240,128]{2,1,0:T(8,128)(2,1)S(1)}, bf16[9,240,128]{2,1,0:T(8,128)(2,1)S(1)}, u32[]{:S(2)}, u32[]{:S(2)}) collective-permute-start(bf16[9,240,128]{2,1,0:T(8,128)(2,1)S(1)} %get-tuple-element.39), channel_id=1, source_target_pairs={{0,32},{32,64},{64,96},{96,128},{128,160},{160,192},{192,224},{1,3... | collective-permute-start | bytes 1658888 | tf_op jit(solution)/shard_map/ppermute | solution.py:393
  82.0 15.7 %collective-permute-start.5 = (bf16[9,240,128]{2,1,0:T(8,128)(2,1)S(1)}, bf16[9,240,128]{2,1,0:T(8,128)(2,1)S(1)}, u32[]{:S(2)}, u32[]{:S(2)}) collective-permute-start(bf16[9,240,128]{2,1,0:T(8,128)(2,1)S(1)} %get-tuple-element.40), channel_id=1, source_target_pairs={{32,0},{64,32},{96,64},{128,96},{160,128},{192,160},{224,192},{33,... | collective-permute-start | bytes 1658888 | tf_op jit(solution)/shard_map/ppermute | solution.py:393

commit v3 on v2

v3 whole, which is shorter than its diff:
```python
import functools
import math

import jax
import jax.numpy as jnp
from jax import lax
from jax.experimental import pallas as pl
from jax.experimental.pallas import tpu as pltpu
from jax.sharding import PartitionSpec as P

HD = 128
W = 80
NH = 20
FIRST = 10
EPS = 1e-06
NEG = -1e30
FAR = 100
LOG2E = math.log2(math.e)
SCALE2 = LOG2E / math.sqrt(HD)
F32 = jnp.float32
BF16 = jnp.bfloat16


def params(mib=12):
    return pltpu.CompilerParams(vmem_limit_bytes=mib * 1024 * 1024)


def cost(microseconds):
    return pl.CostEstimate(flops=0, bytes_accessed=int(microseconds * 3_000_000), transcendentals=0)


def normed(raw, inverse, gain):
    return (raw.astype(F32) * inverse * gain).astype(BF16)


def lanes(g):
    return slice(g * HD, (g + 1) * HD)


def heads_spec(start, group):
    return pl.BlockSpec((2, 3, W, group * HD), lambda s, window: (0, 0, 0, start // group + s))


def gains_spec(start, group):
    return pl.BlockSpec((1, group * HD), lambda s, window: (0, start // group + s))


def whole(shape):
    return pl.BlockSpec(shape, lambda s, window: (0,) * len(shape))


def pack_queries_kernel(group, window, raw, gain, inverse, first, second):
    for g in range(group):
        q = normed(raw[:, :, :, lanes(g)], inverse[...], gain[:, lanes(g)].reshape(1, 1, 1, HD))
        first[g], second[g] = sides("frame", q[0].reshape(3 * W, HD), q[1].reshape(3 * W, HD))


def pack_rows_kernel(group, window, keys, values, gain, inverse, first, second):
    for g in range(group):
        k_gain = gain[:, lanes(g)].reshape(1, 1, HD)
        for n, row_of in (
            (0, lambda row: normed(keys[:, row, :, lanes(g)], inverse[:, row], k_gain)),
            (1, lambda row: values[:, row, :, lanes(g)]),
        ):
            first[g, n], second[g, n] = sides("height", row_of(0), row_of(2))


def group_of(start, count):
    return max(n for n in (1, 2, 4, 5) if count % n == 0 and start % n == 0)


def pack_queries(window, q, gain, inverse, start, count):
    group = group_of(start, count)
    out = jax.ShapeDtypeStruct((count, 3 * W, HD), BF16)
    out_spec = pl.BlockSpec((group, 3 * W, HD), lambda s, window: (s, 0, 0))
    return pl.pallas_call(
        functools.partial(pack_queries_kernel, group),
        grid_spec=pltpu.PrefetchScalarGridSpec(
            num_scalar_prefetch=1,
            grid=(count // group,),
            in_specs=[heads_spec(start, group), gains_spec(start, group), whole((2, 3, W, HD))],
            out_specs=[out_spec, out_spec],
        ),
        out_shape=[out, out],
        compiler_params=params(),
        cost_estimate=cost(0.1 * count),
        name="pack_queries",
    )(window, q, gain, inverse)


def pack_rows(window, k, v, gain, inverse, start, count):
    group = group_of(start, count)
    out = jax.ShapeDtypeStruct((count, 2, 2, W, HD), BF16)
    out_spec = pl.BlockSpec((group, 2, 2, W, HD), lambda s, window: (s, 0, 0, 0, 0))
    return pl.pallas_call(
        functools.partial(pack_rows_kernel, group),
        grid_spec=pltpu.PrefetchScalarGridSpec(
            num_scalar_prefetch=1,
            grid=(count // group,),
            in_specs=[heads_spec(start, group)] * 2 + [gains_spec(start, group), whole((2, 3, W, HD))],
            out_specs=[out_spec, out_spec],
        ),
        out_shape=[out, out],
        compiler_params=params(),
        cost_estimate=cost(0.15 * count),
        name="pack_rows",
    )(window, k, v, gain, inverse)


def fill_lines(kx, vx, k, v, inverse, gain, first, second):
    kn = normed(k, inverse, gain.reshape(1, 1, 1, HD))
    low, high = sides("height", first[...], second[...])
    for j in range(2):
        kx[j, 0:W] = low[0, j]
        kx[j, W : 4 * W] = kn[j].reshape(3 * W, HD)
        kx[j, 4 * W : 5 * W] = high[0, j]
        vx[j, 0:W, 0:HD] = low[1, j]
        vx[j, W : 4 * W, 0:HD] = v[j].reshape(3 * W, HD)
        vx[j, 4 * W : 5 * W, 0:HD] = high[1, j]


def line_scratch(group):
    return [pltpu.VMEM((2, 5 * W, HD), BF16)] * group + [pltpu.VMEM((2, 5 * W, 2 * HD), BF16)] * group


def even(axis):
    return lax.rem(lax.axis_index(axis), 2) == 0


def sides(axis, first, second):
    return jnp.where(even(axis), second, first), jnp.where(even(axis), first, second)


def inside(axis):
    at = lax.axis_index(axis)
    return at > 0, at < lax.axis_size(axis) - 1


def fill_ones(values):
    for vx in values:
        vx[:, :, HD:] = jnp.ones((2, 5 * W, HD), BF16)


def fill_gaps(gaps):
    lane = lax.broadcasted_iota(jnp.int32, (W, 3 * W), 1)
    line = (lane >= W).astype(jnp.int32) + (lane >= 2 * W).astype(jnp.int32)
    key_tile = (lane - W * line) >> 3
    query_tile = lax.broadcasted_iota(jnp.int32, (W, 3 * W), 0) >> 3
    gap = jnp.abs(key_tile - query_tile)
    below, above = inside("height")
    no_low = jnp.where(below, 0, FAR)
    no_high = jnp.where(above, 0, FAR)
    for reach in range(2):
        for i in range(3):
            low = FAR if reach == 0 else (no_low if i == 0 else 0)
            high = FAR if reach == 0 else (no_high if i == 2 else 0)
            gaps[reach, i] = gap + jnp.where(line == 0, low, 0) + jnp.where(line == 2, high, 0)


def biases(gaps, window, head):
    reach_row, reach_tile = jnp.minimum(window[head, 1], 1), window[head, 2]
    return [jnp.where(gaps[reach_row, i] <= reach_tile, 0.0, NEG).astype(F32) for i in range(3)]


def dot_t(q, k):
    return lax.dot_general(q, k, (((1,), (1,)), ((), ())), preferred_element_type=F32)


def lines_of(i):
    return slice(i * W, (i + 3) * W)


def row_max(s):
    return jnp.max(s, axis=-1, keepdims=True)


def weights_of(s, top):
    return jnp.exp2((s - top) * SCALE2).astype(BF16)


def divided(mixed):
    total = mixed[:, HD:]
    inverse = pl.reciprocal(total, approx=True)
    inverse = inverse * (2.0 - total * inverse)
    return (mixed[:, :HD] * inverse).astype(BF16)


def mark(st, at, here, top, mixed):
    st[0, at] = jnp.where(here, top, st[0, at])
    st[1, at] = jnp.where(here, mixed[:, HD:], st[1, at])


def lse_of(st):
    return st[0] * SCALE2 + jnp.log(st[1]) * LOG2E


def pieces_of(full, lane):
    high = full.astype(BF16).astype(F32)
    rest = full - high
    middle = rest.astype(BF16).astype(F32)
    low = rest - middle
    return jnp.where(lane < 32, high, jnp.where(lane < 64, middle, jnp.where(lane < 96, low, 0.0))).astype(BF16)


def partial_kernel(far, start, group, steps, window, kinverse, k, v, kgain, low, high, *refs):
    if far:
        qb, qa, ob, oa = refs[:4]
    else:
        q, qgain, qinverse, part, own_stats = refs[:5]
    kxs, vxs = refs[-2 - 2 * group : -2 - group], refs[-2 - group : -2]
    gaps, st = refs[-2:]
    step = pl.program_id(0)

    @pl.when(step == 0)
    def _():
        for j in range(2):
            st[j, 0] = jnp.zeros((3 * W, HD), F32)
            st[j, 1] = jnp.ones((3 * W, HD), F32)
        fill_ones(vxs)
        fill_gaps(gaps)

    @pl.when(step < steps)
    def _():
        for g in range(group):
            own_keys, own_values = k[:, :, :, lanes(g)], v[:, :, :, lanes(g)]
            fill_lines(
                kxs[g], vxs[g], own_keys, own_values, kinverse[...], kgain[:, lanes(g)], low.at[g], high.at[g]
            )
        if far:
            far_step(start, group, step, window, qb, qa, ob, oa, kxs, vxs, gaps, st)
        else:
            own_step(start, group, step, window, q, qgain, qinverse, part, kxs, vxs, gaps, st)

    if far:

        @pl.when(step == steps)
        def _():
            lane = lax.broadcasted_iota(jnp.int32, (3 * W, HD), 1)
            below, above = (pieces_of(lse_of(st[j]), lane) for j in range(2))
            ob[0], oa[0] = sides("frame", below, above)

    else:

        @pl.when(step == steps - 1)
        def _():
            for j in range(2):
                own_stats[j] = lse_of(st[j])


def marked_lanes(step, group, g):
    return (lax.broadcasted_iota(jnp.int32, (W, HD), 1) & 31) == step * group + g


def far_step(start, group, step, window, qb, qa, ob, oa, kxs, vxs, gaps, st):
    scores = []
    for g in range(group):
        masks = biases(gaps, window, start + step * group + g)
        for i in range(3):
            at = slice(i * W, (i + 1) * W)
            asked = sides("frame", qb[g, at], qa[g, at])
            scores += [dot_t(asked[j], kxs[g][j, lines_of(i)]) + masks[i] for j in range(2)]
    tops = [row_max(s) for s in scores]
    weights = [weights_of(s, top) for s, top in zip(scores, tops)]
    for g in range(group):
        here = marked_lanes(step, group, g)
        for i in range(3):
            at, n = slice(i * W, (i + 1) * W), 6 * g + 2 * i
            mixed = [
                jnp.dot(weights[n + j], vxs[g][j, lines_of(i)], preferred_element_type=F32) for j in range(2)
            ]
            for j in range(2):
                mark(st.at[j], at, here, tops[n + j], mixed[j])
            ob[g, at], oa[g, at] = sides("frame", divided(mixed[0]), divided(mixed[1]))


def own_step(start, group, step, window, q, qgain, qinverse, part, kxs, vxs, gaps, st):
    scores = []
    for g in range(group):
        head = start + step * group + g
        masks = biases(gaps, window, head)
        cross = jnp.where(window[head, 0] > 0, 0.0, NEG)
        qn = normed(q[:, :, :, lanes(g)], qinverse[...], qgain[:, lanes(g)].reshape(1, 1, 1, HD))
        for i in range(3):
            own = qn[:, i].reshape(2 * W, HD)
            other = masks[i] + cross
            for j in range(2):
                raw = dot_t(own, kxs[g][j, lines_of(i)])
                order = (masks[i], other) if j == 0 else (other, masks[i])
                scores.append([raw[W * n : W * (n + 1)] + order[n] for n in range(2)])
    tops, weights = [], []
    for s0, s1 in zip(scores[::2], scores[1::2]):
        top = [row_max(jnp.maximum(s0[n], s1[n])) for n in range(2)]
        tops.append(top)
        for s in (s0, s1):
            weights.append(jnp.concatenate([weights_of(a, b) for a, b in zip(s, top)], axis=0))
    for g in range(group):
        here = marked_lanes(step, group, g)
        for i in range(3):
            at, n = slice(i * W, (i + 1) * W), 3 * g + i
            m0, m1 = (
                jnp.dot(weights[2 * n + j], vxs[g][j, lines_of(i)], preferred_element_type=F32)
                for j in range(2)
            )
            for f in range(2):
                own = m0[W * f : W * (f + 1)] + m1[W * f : W * (f + 1)]
                part[g, f, i] = divided(own)
                mark(st.at[f], at, here, tops[n][f], own)


def partial_call(far, window, k, v, kgain, kinverse, low, high, asked, start, count):
    group = 2
    steps = count // group

    def step_of(s):
        return jnp.minimum(s, steps - 1)

    heads = pl.BlockSpec((2, 3, W, group * HD), lambda s, window: (0, 0, 0, start // group + step_of(s)))
    gains = pl.BlockSpec((1, group * HD), lambda s, window: (0, start // group + step_of(s)))
    rows = pl.BlockSpec((group, 2, 2, W, HD), lambda s, window: (step_of(s), 0, 0, 0, 0))
    norms = whole((2, 3, W, HD))
    if far:
        q_spec = pl.BlockSpec((group, 3 * W, HD), lambda s, window: (step_of(s), 0, 0))
        o_spec = pl.BlockSpec((group, 3 * W, HD), lambda s, window: (s, 0, 0))
        asked_specs, out_specs = [q_spec] * 2, [o_spec] * 2
        out_shape = [jax.ShapeDtypeStruct((count + 1, 3 * W, HD), BF16)] * 2
    else:
        asked_specs = [heads, gains, norms]
        out_specs = [
            pl.BlockSpec((group, 2, 3, W, HD), lambda s, window: (s, 0, 0, 0, 0)),
            whole((2, 3 * W, HD)),
        ]
        out_shape = [
            jax.ShapeDtypeStruct((count, 2, 3, W, HD), BF16),
            jax.ShapeDtypeStruct((2, 3 * W, HD), F32),
        ]
    return pl.pallas_call(
        functools.partial(partial_kernel, far, start, group, steps),
        grid_spec=pltpu.PrefetchScalarGridSpec(
            num_scalar_prefetch=1,
            grid=(steps + 1 if far else steps,),
            in_specs=[norms, heads, heads, gains, rows, rows] + asked_specs,
            out_specs=out_specs,
            scratch_shapes=line_scratch(group)
            + [pltpu.VMEM((2, 3, W, 3 * W), jnp.int32), pltpu.VMEM((2, 2, 3 * W, HD), F32)],
        ),
        out_shape=out_shape,
        compiler_params=params(16),
        cost_estimate=cost(0.6 * count),
        name="far_partial" if far else "own_partial",
    )(window, kinverse, k, v, kgain, low, high, *asked)


def far_partial(window, queries, k, v, kgain, kinverse, rows, start, count):
    return partial_call(True, window, k, v, kgain, kinverse, *rows, queries, start, count)


def own_partial(window, q, k, v, qgain, kgain, qinverse, kinverse, rows, start, count):
    return partial_call(False, window, k, v, kgain, kinverse, *rows, (q, qgain, qinverse), start, count)


def merge_kernel(start, group, window, part, lse, ob, oa, sb, sa, *refs):
    out, shares = refs[-2:]
    lane = lax.broadcasted_iota(jnp.int32, (3 * W, HD), 1)
    neighbours = inside("frame")
    step = pl.program_id(0)

    @pl.when(step == 0)
    def _():
        for j, st in enumerate(sides("frame", sb[0], sa[0])):
            pieces = st.astype(F32)
            other = pieces + pltpu.roll(pieces, HD - 32, 1) + pltpu.roll(pieces, HD - 64, 1)
            other = jnp.where(neighbours[j], other, NEG)
            top = jnp.maximum(lse[j], other)
            own_weight = jnp.exp2(lse[j] - top)
            other_weight = jnp.exp2(other - top)
            shares[j] = other_weight / (own_weight + other_weight)

    for g in range(group):
        here = lane == step * group + g
        for j, far in enumerate(sides("frame", ob[g], oa[g])):
            share = jnp.sum(jnp.where(here, shares[j], 0.0), axis=1, keepdims=True)
            share = jnp.where(window[start + step * group + g, 0] > 0, share, 0.0)
            own = part[g, j].reshape(3 * W, HD).astype(F32)
            mixed = own + (far.astype(F32) - own) * share
            out[j, :, :, lanes(g)] = mixed.astype(BF16).reshape(3, W, HD)


def merge(window, out, part, lse, o_below, o_above, start, count):
    group = group_of(start, count)
    o_spec = pl.BlockSpec((group, 3 * W, HD), lambda s, window: (s, 0, 0))
    stat_spec = pl.BlockSpec((1, 3 * W, HD), lambda s, window: (count, 0, 0))
    return pl.pallas_call(
        functools.partial(merge_kernel, start, group),
        grid_spec=pltpu.PrefetchScalarGridSpec(
            num_scalar_prefetch=1,
            grid=(count // group,),
            in_specs=[
                pl.BlockSpec((group, 2, 3, W, HD), lambda s, window: (s, 0, 0, 0, 0)),
                whole((2, 3 * W, HD)),
                o_spec,
                o_spec,
                stat_spec,
                stat_spec,
            ]
            + ([] if out is None else [pl.BlockSpec(memory_space=pl.ANY)]),
            out_specs=heads_spec(start, group),
            scratch_shapes=[pltpu.VMEM((2, 3 * W, HD), F32)],
        ),
        out_shape=jax.ShapeDtypeStruct((2, 3, W, NH * HD), BF16),
        input_output_aliases={} if out is None else {7: 0},
        compiler_params=params(),
        cost_estimate=cost(0.25 * count),
        name="merge",
    )(window, part, lse, o_below, o_above, o_below, o_above, *([] if out is None else [out]))


def exchange(axis, first, second):
    out = []
    for start, block in enumerate((first, second)):
        pairs = [(i, i + 1) for i in range(start, lax.axis_size(axis) - 1, 2)]
        out.append(lax.ppermute(block, axis, pairs + [(b, a) for a, b in pairs]))
    return out


def attention(window, q, k, v, q_gain, k_gain, q_inverse, k_inverse):
    norms = (q_gain, k_gain, q_inverse, k_inverse)
    chunks = ((0, FIRST), (FIRST, NH - FIRST))
    queries, rows = [], []
    for start, count in chunks:
        packed = pack_queries(window, q, q_gain, q_inverse, start, count)
        k, *packed = lax.optimization_barrier((k, *packed))
        if queries:
            *packed, queries[0][0], queries[0][1] = lax.optimization_barrier((*packed, *queries[0]))
        packed_rows = pack_rows(window, k, v, k_gain, k_inverse, start, count)
        rows.append(exchange("height", *packed_rows))
        queries.append(exchange("frame", *packed))
        q, *_ = lax.optimization_barrier((q, *packed_rows))
    parts = []
    for n, (start, count) in enumerate(chunks):
        far = far_partial(window, queries[n], k, v, k_gain, k_inverse, rows[n], start, count)
        q, *queries[1] = lax.optimization_barrier((q, *queries[1]))
        part, lse = own_partial(window, q, k, v, *norms, rows[n], start, count)
        k, part = lax.optimization_barrier((k, part))
        parts.append((part, lse, *exchange("frame", *far), start, count))
    out = None
    for part in parts:
        out = merge(window, out, *part)
    return out


def squares_of(raw):
    values = raw.astype(F32)
    return jnp.sum(values * values, axis=-1)


def body(q, k, v, q_gain, k_gain, window):
    width_total = q.shape[3] * lax.axis_size("head")
    query_sum, key_sum = lax.psum((squares_of(q), squares_of(k)), "head")

    def inverse_of(total):
        return jnp.broadcast_to(lax.rsqrt(total / width_total + EPS)[..., None], (2, 3, W, HD))

    return attention(
        window, q, k, v, q_gain[None], k_gain[None], inverse_of(query_sum), inverse_of(key_sum)
    )


def solution(mesh):
    placed = (
        P("frame", "height", None, "head"),
        P("frame", "height", None, "head"),
        P("frame", "height", None, "head"),
        P("head"),
        P("head"),
        P("head", None),
    )
    return jax.shard_map(
        body,
        mesh=mesh,
        in_specs=placed,
        out_specs=P("frame", "height", None, "head"),
        check_vma=False,
    )
```

time: 101 us -> 92.1 us (0.912)
  the two profiles are of different devices: /device:TPU:120 before, /device:TPU:38 now
where the time goes in v3:
time: 92.1 us; the launch traced here: 91.8 us
  Pallas kernels  41.2 us (45%)
  starting transfers between devices  32.7 us (36%)
  waiting for transfers between devices  7.63 us (8%)
  local copies, waits for them, and re-layouts  3.75 us (4%)
  other arithmetic  3.53 us (4%)
  blocking collectives  2.63 us (3%)
    ppermute x12, starting transfers between devices, exchange(): out.append(lax.ppermute(block, axis, pairs + [(b, a) for a, b in pairs]))  32.7 us
    pallas_call x4, Pallas kernels, partial_call(): pl.pallas_call(functools.partial(partial_kernel, far, start, group, steps...  30.1 us
    ppermute x12, waiting for transfers between devices, exchange(): out.append(lax.ppermute(block, axis, pairs + [(b, a) for a, b in pairs]))  7.63 us
    pallas_call x2, Pallas kernels, merge(): pl.pallas_call(functools.partial(merge_kernel, start, group), grid_spec=p...  5.67 us
    reduce_sum x1, other arithmetic, squares_of(): return jnp.sum(values * values, axis=-1)  3.52 us
    unnamed x17, local copies, waits for them, and re-layouts  3.5 us
    pallas_call x2, Pallas kernels, pack_rows(): pl.pallas_call(functools.partial(pack_rows_kernel, group), grid_spec=pltp...  2.79 us
    pallas_call x2, Pallas kernels, pack_queries(): pl.pallas_call(functools.partial(pack_queries_kernel, group), grid_spec=p...  2.63 us
  transfers between devices with their start and end apart: 12, of which 3 were waited for; matrix products, arithmetic and copies ran while one was open for 0% of the time, Pallas kernels for 39%

profile of v3, /device:TPU:38, one launch (start us, length us, event | category | flops | bytes accessed | tf_op | source)
XLA Modules:
  0.0 91.8 jit_solution(9636940922195819345)
XLA Ops:
  0.0 3.5 %multiply_reduce_fusion = (f32[2,3,80]{2,1,0:T(4,128)S(1)}, f32[2,3,80]{2,1,0:T(4,128)S(1)}) fusion(bf16[2,3,80,2560]{3,2,1,0:T(8,128)(2,1)} %k.3, bf16[2,3,80,2560]{3,2,1,0:T(8,128)(2,1)} %refs_0_.1), kind=kLoop, calls=%fused_computation | loop fusion | flops 7371840 | bytes 4919040 | tf_op jit(solution)/shard_map/reduce_sum | solution.py:453
  3.5 2.6 %all-reduce = (f32[2,3,80]{2,1,0:T(4,128)S(1)}, f32[2,3,80]{2,1,0:T(4,128)S(1)}) all-reduce(f32[2,3,80]{2,1,0:T(4,128)S(1)} %get-tuple-element.77, f32[2,3,80]{2,1,0:T(4,128)S(1)} %get-tuple-element.76), channel_id=1, replica_groups=mesh['frame'=8,'height'=16,'head'=2] {'head'}, use_global_device_ids=true, to_apply=%region_1.0 | all-reduce | flops 960 | bytes 7680 | tf_op jit(solution)/shard_map/psum | solution.py:458
  6.3 0.1 copy.17.window
  6.4 0.1 broadcast_in_dim.9.inverse.refs_2_
  6.5 1.7 %copy-done.3 = bf16[2,3,80,2560]{3,2,1,0:T(8,128)(2,1)S(1)} copy-done((bf16[2,3,80,2560]{3,2,1,0:T(8,128)(2,1)S(1)}, bf16[2,3,80,2560]{3,2,1,0:T(8,128)(2,1)}, u32[]{:S(2)}) %copy-start.3) | copy-done | bytes 2457624
  8.2 1.3 %pack_queries.2 = (bf16[10,240,128]{2,1,0:T(8,128)(2,1)S(1)}, bf16[10,240,128]{2,1,0:T(8,128)(2,1)S(1)}) custom-call(s32[20,3]{1,0:T(8,128)S(1)} %copy.17.window, bf16[2,3,80,2560]{3,2,1,0:T(8,128)(2,1)S(1)} %copy-done.3, f32[1,2560]{1,0:T(1,128)S(1)} %broadcast_in_dim.8.gain.refs_1_, f32[2,3,80,128]{3,2,1,0:T(8,128)S(1)} %broadcast_in_dim.9.inverse.refs_2_), custom_call_target="tpu_custom_call" | custom-call | bytes 3000000 | tf_op jit(solution)/shard_map/pack_queries/pallas_call | solution.py:76
  9.5 0.1 broadcast_in_dim.21.inverse.kinverse
  9.6 1.7 %copy-done.1 = bf16[2,3,80,2560]{3,2,1,0:T(8,128)(2,1)S(1)} copy-done((bf16[2,3,80,2560]{3,2,1,0:T(8,128)(2,1)S(1)}, bf16[2,3,80,2560]{3,2,1,0:T(8,128)(2,1)}, u32[]{:S(2)}) %copy-start.1) | copy-done | bytes 2457624
  11.3 1.4 %pack_rows.2 = (bf16[10,2,2,80,128]{4,3,2,1,0:T(8,128)(2,1)S(1)}, bf16[10,2,2,80,128]{4,3,2,1,0:T(8,128)(2,1)S(1)}) custom-call(s32[20,3]{1,0:T(8,128)S(1)} %copy.17.window, bf16[2,3,80,2560]{3,2,1,0:T(8,128)(2,1)S(1)} %copy-done, bf16[2,3,80,2560]{3,2,1,0:T(8,128)(2,1)S(1)} %copy-done.1, f32[1,2560]{1,0:T(1,128)S(1)} %broadcast_in_dim.20.gain.kgain, ...), custom_call_target="tpu_custom_call" | custom-call | bytes 4500000 | tf_op jit(solution)/shard_map/pack_rows/pallas_call | solution.py:95
  12.7 1.7 %collective-permute-start = (bf16[10,2,2,80,128]{4,3,2,1,0:T(8,128)(2,1)S(1)}, bf16[10,2,2,80,128]{4,3,2,1,0:T(8,128)(2,1)S(1)}, u32[]{:S(2)}, u32[]{:S(2)}) collective-permute-start(bf16[10,2,2,80,128]{4,3,2,1,0:T(8,128)(2,1)S(1)} %get-tuple-element.43), channel_id=1, source_target_pairs={{0,2},{4,6},{8,10},{12,14},{16,18},{20,22},{24,26},{28,30},{2,0},{... | collective-permute-start | bytes 2457608 | tf_op jit(solution)/shard_map/ppermute | solution.py:421
  14.4 0.1 collective-permute-start.2
  14.5 5.6 %collective-permute-start.3 = (bf16[10,240,128]{2,1,0:T(8,128)(2,1)S(1)}, bf16[10,240,128]{2,1,0:T(8,128)(2,1)S(1)}, u32[]{:S(2)}, u32[]{:S(2)}) collective-permute-start(bf16[10,240,128]{2,1,0:T(8,128)(2,1)S(1)} %get-tuple-element.55), channel_id=1, source_target_pairs={{32,64},{96,128},{160,192},{64,32},{128,96},{192,160},{33,65},{97,... | collective-permute-start | bytes 1843208 | tf_op jit(solution)/shard_map/ppermute | solution.py:421
  20.1 4.4 %collective-permute-start.1 = (bf16[10,2,2,80,128]{4,3,2,1,0:T(8,128)(2,1)S(1)}, bf16[10,2,2,80,128]{4,3,2,1,0:T(8,128)(2,1)S(1)}, u32[]{:S(2)}, u32[]{:S(2)}) collective-permute-start(bf16[10,2,2,80,128]{4,3,2,1,0:T(8,128)(2,1)S(1)} %get-tuple-element.44), channel_id=1, source_target_pairs={{2,4},{6,8},{10,12},{14,16},{18,20},{22,24},{26,28},{4,2},{8,6},{1... | collective-permute-start | bytes 2457608 | tf_op jit(solution)/shard_map/ppermute | solution.py:421
  24.5 1.3 %pack_queries.3 = (bf16[10,240,128]{2,1,0:T(8,128)(2,1)S(1)}, bf16[10,240,128]{2,1,0:T(8,128)(2,1)S(1)}) custom-call(s32[20,3]{1,0:T(8,128)S(1)} %copy.17.window, bf16[2,3,80,2560]{3,2,1,0:T(8,128)(2,1)S(1)} %copy-done.4, f32[1,2560]{1,0:T(1,128)S(1)} %broadcast_in_dim.8.gain.refs_1_, f32[2,3,80,128]{3,2,1,0:T(8,128)S(1)} %broadcast_in_dim.9.inverse.refs_2_), custom_call_target="tpu_custom_call" | custom-call | bytes 3000000 | tf_op jit(solution)/shard_map/pack_queries/pallas_call | solution.py:76
  25.9 1.4 %pack_rows.3 = (bf16[10,2,2,80,128]{4,3,2,1,0:T(8,128)(2,1)S(1)}, bf16[10,2,2,80,128]{4,3,2,1,0:T(8,128)(2,1)S(1)}) custom-call(s32[20,3]{1,0:T(8,128)S(1)} %copy.17.window, bf16[2,3,80,2560]{3,2,1,0:T(8,128)(2,1)S(1)} %copy-done, bf16[2,3,80,2560]{3,2,1,0:T(8,128)(2,1)S(1)} %copy-done.2, f32[1,2560]{1,0:T(1,128)S(1)} %broadcast_in_dim.20.gain.kgain, ...), custom_call_target="tpu_custom_call" | custom-call | bytes 4500000 | tf_op jit(solution)/shard_map/pack_rows/pallas_call | solution.py:95
  27.3 0.5 collective-permute-start.6
  27.8 2.3 %collective-permute-done.2.refs_0_ = bf16[10,240,128]{2,1,0:T(8,128)(2,1)S(1)} collective-permute-done((bf16[10,240,128]{2,1,0:T(8,128)(2,1)S(1)}, bf16[10,240,128]{2,1,0:T(8,128)(2,1)S(1)}, u32[]{:S(2)}, u32[]{:S(2)}) %collective-permute-start.2) | collective-permute-done | bytes 614432 | tf_op jit(solution)/shard_map/ppermute | solution.py:421
  30.1 4.3 %collective-permute-start.7 = (bf16[10,2,2,80,128]{4,3,2,1,0:T(8,128)(2,1)S(1)}, bf16[10,2,2,80,128]{4,3,2,1,0:T(8,128)(2,1)S(1)}, u32[]{:S(2)}, u32[]{:S(2)}) collective-permute-start(bf16[10,2,2,80,128]{4,3,2,1,0:T(8,128)(2,1)S(1)} %get-tuple-element.50), channel_id=1, source_target_pairs={{2,4},{6,8},{10,12},{14,16},{18,20},{22,24},{26,28},{4,2},{8,6},{1... | collective-permute-start | bytes 2457608 | tf_op jit(solution)/shard_map/ppermute | solution.py:421
  34.4 0.4 collective-permute-start.4
  34.8 5.4 %collective-permute-start.5 = (bf16[10,240,128]{2,1,0:T(8,128)(2,1)S(1)}, bf16[10,240,128]{2,1,0:T(8,128)(2,1)S(1)}, u32[]{:S(2)}, u32[]{:S(2)}) collective-permute-start(bf16[10,240,128]{2,1,0:T(8,128)(2,1)S(1)} %get-tuple-element.57), channel_id=1, source_target_pairs={{32,64},{96,128},{160,192},{64,32},{128,96},{192,160},{33,65},{97,... | collective-permute-start | bytes 1843208 | tf_op jit(solution)/shard_map/ppermute | solution.py:421
  40.2 5.1 %collective-permute-done.1.high = bf16[10,2,2,80,128]{4,3,2,1,0:T(8,128)(2,1)S(1)} collective-permute-done((bf16[10,2,2,80,128]{4,3,2,1,0:T(8,128)(2,1)S(1)}, bf16[10,2,2,80,128]{4,3,2,1,0:T(8,128)(2,1)S(1)}, u32[]{:S(2)}, u32[]{:S(2)}) %collective-permute-start.1) | collective-permute-done | bytes 819232 | tf_op jit(solution)/shard_map/ppermute | solution.py:421
  45.3 7.1 %far_partial.3 = (bf16[11,240,128]{2,1,0:T(8,128)(2,1)S(1)}, bf16[11,240,128]{2,1,0:T(8,128)(2,1)S(1)}) custom-call(s32[20,3]{1,0:T(8,128)S(1)} %copy.17.window, f32[2,3,80,128]{3,2,1,0:T(8,128)S(1)} %broadcast_in_dim.21.inverse.kinverse, bf16[2,3,80,2560]{3,2,1,0:T(8,128)(2,1)S(1)} %copy-done, bf16[2,3,80,2560]{3,2,1,0:T(8,128)(2,1)S(1)} %copy-done.2, ...), custom_call_target="tpu_custom_call" | custom-call | bytes 18000000 | tf_op jit(solution)/shard_map/far_partial/pallas_call | solution.py:336
  52.5 0.1 collective-permute-start.10
  52.6 6.0 %collective-permute-start.11 = (bf16[11,240,128]{2,1,0:T(8,128)(2,1)S(1)}, bf16[11,240,128]{2,1,0:T(8,128)(2,1)S(1)}, u32[]{:S(2)}, u32[]{:S(2)}) collective-permute-start(bf16[11,240,128]{2,1,0:T(8,128)(2,1)S(1)} %get-tuple-element.73), channel_id=1, source_target_pairs={{32,64},{96,128},{160,192},{64,32},{128,96},{192,160},{33,65},{97,... | collective-permute-start | bytes 2027528 | tf_op jit(solution)/shard_map/ppermute | solution.py:421
  58.6 7.9 %own_partial.2 = (bf16[10,2,3,80,128]{4,3,2,1,0:T(8,128)(2,1)S(1)}, f32[2,240,128]{2,1,0:T(8,128)S(1)}) custom-call(s32[20,3]{1,0:T(8,128)S(1)} %copy.17.window, f32[2,3,80,128]{3,2,1,0:T(8,128)S(1)} %broadcast_in_dim.21.inverse.kinverse, bf16[2,3,80,2560]{3,2,1,0:T(8,128)(2,1)S(1)} %copy-done, bf16[2,3,80,2560]{3,2,1,0:T(8,128)(2,1)S(1)} %copy-done.2, ...), custom_call_target="tpu_custom_call" | custom-call | bytes 18000000 | tf_op jit(solution)/shard_map/own_partial/pallas_call | solution.py:336
  66.6 7.1 %far_partial.2 = (bf16[11,240,128]{2,1,0:T(8,128)(2,1)S(1)}, bf16[11,240,128]{2,1,0:T(8,128)(2,1)S(1)}) custom-call(s32[20,3]{1,0:T(8,128)S(1)} %copy.17.window, f32[2,3,80,128]{3,2,1,0:T(8,128)S(1)} %broadcast_in_dim.21.inverse.kinverse, bf16[2,3,80,2560]{3,2,1,0:T(8,128)(2,1)S(1)} %copy-done, bf16[2,3,80,2560]{3,2,1,0:T(8,128)(2,1)S(1)} %copy-done.2, ...), custom_call_target="tpu_custom_call" | custom-call | bytes 18000000 | tf_op jit(solution)/shard_map/far_partial/pallas_call | solution.py:336
  73.7 0.1 collective-permute-start.8
  73.8 4.1 %collective-permute-start.9 = (bf16[11,240,128]{2,1,0:T(8,128)(2,1)S(1)}, bf16[11,240,128]{2,1,0:T(8,128)(2,1)S(1)}, u32[]{:S(2)}, u32[]{:S(2)}) collective-permute-start(bf16[11,240,128]{2,1,0:T(8,128)(2,1)S(1)} %get-tuple-element.67), channel_id=1, source_target_pairs={{32,64},{96,128},{160,192},{64,32},{128,96},{192,160},{33,65},{97,... | collective-permute-start | bytes 2027528 | tf_op jit(solution)/shard_map/ppermute | solution.py:421
  77.9 7.9 %own_partial.3 = (bf16[10,2,3,80,128]{4,3,2,1,0:T(8,128)(2,1)S(1)}, f32[2,240,128]{2,1,0:T(8,128)S(1)}) custom-call(s32[20,3]{1,0:T(8,128)S(1)} %copy.17.window, f32[2,3,80,128]{3,2,1,0:T(8,128)S(1)} %broadcast_in_dim.21.inverse.kinverse, bf16[2,3,80,2560]{3,2,1,0:T(8,128)(2,1)S(1)} %copy-done, bf16[2,3,80,2560]{3,2,1,0:T(8,128)(2,1)S(1)} %copy-done.2, ...), custom_call_target="tpu_custom_call" | custom-call | bytes 18000000 | tf_op jit(solution)/shard_map/own_partial/pallas_call | solution.py:336
  85.9 2.8 %merge.2.refs_0_ = bf16[2,3,80,2560]{3,2,1,0:T(8,128)(2,1)} custom-call(s32[20,3]{1,0:T(8,128)S(1)} %copy.17.window, bf16[10,2,3,80,128]{4,3,2,1,0:T(8,128)(2,1)S(1)} %get-tuple-element.68.part, f32[2,240,128]{2,1,0:T(8,128)S(1)} %get-tuple-element.69.lse, bf16[11,240,128]{2,1,0:T(8,128)(2,1)S(1)} %collective-permute-done.10.ob.sb, ...), custom_call_target="tpu_custom_call" | custom-call | bytes 7500000 | tf_op jit(solution)/shard_map/merge/pallas_call | solution.py:392
  88.7 0.2 collective-permute-done.9.oa.sa
  88.9 2.8 %merge.3 = bf16[2,3,80,2560]{3,2,1,0:T(8,128)(2,1)} custom-call(s32[20,3]{1,0:T(8,128)S(1)} %copy.17.window, bf16[10,2,3,80,128]{4,3,2,1,0:T(8,128)(2,1)S(1)} %get-tuple-element.62.part, f32[2,240,128]{2,1,0:T(8,128)S(1)} %get-tuple-element.63.lse, bf16[11,240,128]{2,1,0:T(8,128)(2,1)S(1)} %collective-permute-done.8.ob.sb, ...), custom_call_target="tpu_custom_call", output_to_operand_aliasing={{}: (7, {})} | custom-call | bytes 7500000 | tf_op jit(solution)/shard_map/merge/pallas_call | solution.py:392
  (27 shorter events, 0.1 us)
Async XLA Ops:
  0.0 6.2 %copy-start.5 = (f32[2560]{0:T(1024)S(1)}, f32[2560]{0:T(1024)}, u32[]{:S(2)}) copy-start(f32[2560]{0:T(1024)} %param.10) | copy-start | bytes 30724
  0.0 6.2 %copy-start.6 = (f32[2560]{0:T(1024)S(1)}, f32[2560]{0:T(1024)}, u32[]{:S(2)}) copy-start(f32[2560]{0:T(1024)} %param.9) | copy-start | bytes 30724
  0.0 6.2 %copy-start.7 = (s32[20,3]{0,1:T(4,128)S(1)}, s32[20,3]{0,1:T(4,128)}, u32[]{:S(2)}) copy-start(s32[20,3]{0,1:T(4,128)} %param.11) | copy-start | bytes 724
  3.5 6.1 %copy-start = (bf16[2,3,80,2560]{3,2,1,0:T(8,128)(2,1)S(1)}, bf16[2,3,80,2560]{3,2,1,0:T(8,128)(2,1)}, u32[]{:S(2)}) copy-start(bf16[2,3,80,2560]{3,2,1,0:T(8,128)(2,1)} %k.3) | copy-start | bytes 7372804
  6.5 1.7 %copy-start.3 = (bf16[2,3,80,2560]{3,2,1,0:T(8,128)(2,1)S(1)}, bf16[2,3,80,2560]{3,2,1,0:T(8,128)(2,1)}, u32[]{:S(2)}) copy-start(bf16[2,3,80,2560]{3,2,1,0:T(8,128)(2,1)} %refs_0_.1) | copy-start | bytes 7372804
  9.6 1.7 %copy-start.1 = (bf16[2,3,80,2560]{3,2,1,0:T(8,128)(2,1)S(1)}, bf16[2,3,80,2560]{3,2,1,0:T(8,128)(2,1)}, u32[]{:S(2)}) copy-start(bf16[2,3,80,2560]{3,2,1,0:T(8,128)(2,1)} %v.7) | copy-start | bytes 7372804
  11.3 13.2 %copy-start.4 = (bf16[2,3,80,2560]{3,2,1,0:T(8,128)(2,1)S(1)}, bf16[2,3,80,2560]{3,2,1,0:T(8,128)(2,1)}, u32[]{:S(2)}) copy-start(bf16[2,3,80,2560]{3,2,1,0:T(8,128)(2,1)} %refs_0_.1) | copy-start | bytes 7372804
  12.7 13.1 %copy-start.2 = (bf16[2,3,80,2560]{3,2,1,0:T(8,128)(2,1)S(1)}, bf16[2,3,80,2560]{3,2,1,0:T(8,128)(2,1)}, u32[]{:S(2)}) copy-start(bf16[2,3,80,2560]{3,2,1,0:T(8,128)(2,1)} %v.7) | copy-start | bytes 7372804
  12.7 22.0 %collective-permute-start = (bf16[10,2,2,80,128]{4,3,2,1,0:T(8,128)(2,1)S(1)}, bf16[10,2,2,80,128]{4,3,2,1,0:T(8,128)(2,1)S(1)}, u32[]{:S(2)}, u32[]{:S(2)}) collective-permute-start(bf16[10,2,2,80,128]{4,3,2,1,0:T(8,128)(2,1)S(1)} %get-tuple-element.43), channel_id=1, source_target_pairs={{0,2},{4,6},{8,10},{12,14},{16,18},{20,22},{24,26},{28,30},{2,0},{... | collective-permute-start | bytes 2457608 | tf_op jit(solution)/shard_map/ppermute | solution.py:421
  14.4 15.6 %collective-permute-start.2 = (bf16[10,240,128]{2,1,0:T(8,128)(2,1)S(1)}, bf16[10,240,128]{2,1,0:T(8,128)(2,1)S(1)}, u32[]{:S(2)}, u32[]{:S(2)}) collective-permute-start(bf16[10,240,128]{2,1,0:T(8,128)(2,1)S(1)} %get-tuple-element.54), channel_id=1, source_target_pairs={{0,32},{64,96},{128,160},{192,224},{32,0},{96,64},{160,128},{224,1... | collective-permute-start | bytes 1843208 | tf_op jit(solution)/shard_map/ppermute | solution.py:421
  14.5 19.9 %collective-permute-start.3 = (bf16[10,240,128]{2,1,0:T(8,128)(2,1)S(1)}, bf16[10,240,128]{2,1,0:T(8,128)(2,1)S(1)}, u32[]{:S(2)}, u32[]{:S(2)}) collective-permute-start(bf16[10,240,128]{2,1,0:T(8,128)(2,1)S(1)} %get-tuple-element.55), channel_id=1, source_target_pairs={{32,64},{96,128},{160,192},{64,32},{128,96},{192,160},{33,65},{97,... | collective-permute-start | bytes 1843208 | tf_op jit(solution)/shard_map/ppermute | solution.py:421
  20.1 25.2 %collective-permute-start.1 = (bf16[10,2,2,80,128]{4,3,2,1,0:T(8,128)(2,1)S(1)}, bf16[10,2,2,80,128]{4,3,2,1,0:T(8,128)(2,1)S(1)}, u32[]{:S(2)}, u32[]{:S(2)}) collective-permute-start(bf16[10,2,2,80,128]{4,3,2,1,0:T(8,128)(2,1)S(1)} %get-tuple-element.44), channel_id=1, source_target_pairs={{2,4},{6,8},{10,12},{14,16},{18,20},{22,24},{26,28},{4,2},{8,6},{1... | collective-permute-start | bytes 2457608 | tf_op jit(solution)/shard_map/ppermute | solution.py:421
  27.3 39.3 %collective-permute-start.6 = (bf16[10,2,2,80,128]{4,3,2,1,0:T(8,128)(2,1)S(1)}, bf16[10,2,2,80,128]{4,3,2,1,0:T(8,128)(2,1)S(1)}, u32[]{:S(2)}, u32[]{:S(2)}) collective-permute-start(bf16[10,2,2,80,128]{4,3,2,1,0:T(8,128)(2,1)S(1)} %get-tuple-element.49), channel_id=1, source_target_pairs={{0,2},{4,6},{8,10},{12,14},{16,18},{20,22},{24,26},{28,30},{2,0},{... | collective-permute-start | bytes 2457608 | tf_op jit(solution)/shard_map/ppermute | solution.py:421
  30.1 36.5 %collective-permute-start.7 = (bf16[10,2,2,80,128]{4,3,2,1,0:T(8,128)(2,1)S(1)}, bf16[10,2,2,80,128]{4,3,2,1,0:T(8,128)(2,1)S(1)}, u32[]{:S(2)}, u32[]{:S(2)}) collective-permute-start(bf16[10,2,2,80,128]{4,3,2,1,0:T(8,128)(2,1)S(1)} %get-tuple-element.50), channel_id=1, source_target_pairs={{2,4},{6,8},{10,12},{14,16},{18,20},{22,24},{26,28},{4,2},{8,6},{1... | collective-permute-start | bytes 2457608 | tf_op jit(solution)/shard_map/ppermute | solution.py:421
  34.4 18.2 %collective-permute-start.4 = (bf16[10,240,128]{2,1,0:T(8,128)(2,1)S(1)}, bf16[10,240,128]{2,1,0:T(8,128)(2,1)S(1)}, u32[]{:S(2)}, u32[]{:S(2)}) collective-permute-start(bf16[10,240,128]{2,1,0:T(8,128)(2,1)S(1)} %get-tuple-element.56), channel_id=1, source_target_pairs={{0,32},{64,96},{128,160},{192,224},{32,0},{96,64},{160,128},{224,1... | collective-permute-start | bytes 1843208 | tf_op jit(solution)/shard_map/ppermute | solution.py:421
  34.8 23.8 %collective-permute-start.5 = (bf16[10,240,128]{2,1,0:T(8,128)(2,1)S(1)}, bf16[10,240,128]{2,1,0:T(8,128)(2,1)S(1)}, u32[]{:S(2)}, u32[]{:S(2)}) collective-permute-start(bf16[10,240,128]{2,1,0:T(8,128)(2,1)S(1)} %get-tuple-element.57), channel_id=1, source_target_pairs={{32,64},{96,128},{160,192},{64,32},{128,96},{192,160},{33,65},{97,... | collective-permute-start | bytes 1843208 | tf_op jit(solution)/shard_map/ppermute | solution.py:421
  52.5 33.4 %collective-permute-start.10 = (bf16[11,240,128]{2,1,0:T(8,128)(2,1)S(1)}, bf16[11,240,128]{2,1,0:T(8,128)(2,1)S(1)}, u32[]{:S(2)}, u32[]{:S(2)}) collective-permute-start(bf16[11,240,128]{2,1,0:T(8,128)(2,1)S(1)} %get-tuple-element.72), channel_id=1, source_target_pairs={{0,32},{64,96},{128,160},{192,224},{32,0},{96,64},{160,128},{224,1... | collective-permute-start | bytes 2027528 | tf_op jit(solution)/shard_map/ppermute | solution.py:421
  52.6 33.3 %collective-permute-start.11 = (bf16[11,240,128]{2,1,0:T(8,128)(2,1)S(1)}, bf16[11,240,128]{2,1,0:T(8,128)(2,1)S(1)}, u32[]{:S(2)}, u32[]{:S(2)}) collective-permute-start(bf16[11,240,128]{2,1,0:T(8,128)(2,1)S(1)} %get-tuple-element.73), channel_id=1, source_target_pairs={{32,64},{96,128},{160,192},{64,32},{128,96},{192,160},{33,65},{97,... | collective-permute-start | bytes 2027528 | tf_op jit(solution)/shard_map/ppermute | solution.py:421
  73.7 15.0 %collective-permute-start.8 = (bf16[11,240,128]{2,1,0:T(8,128)(2,1)S(1)}, bf16[11,240,128]{2,1,0:T(8,128)(2,1)S(1)}, u32[]{:S(2)}, u32[]{:S(2)}) collective-permute-start(bf16[11,240,128]{2,1,0:T(8,128)(2,1)S(1)} %get-tuple-element.66), channel_id=1, source_target_pairs={{0,32},{64,96},{128,160},{192,224},{32,0},{96,64},{160,128},{224,1... | collective-permute-start | bytes 2027528 | tf_op jit(solution)/shard_map/ppermute | solution.py:421
  73.8 15.1 %collective-permute-start.9 = (bf16[11,240,128]{2,1,0:T(8,128)(2,1)S(1)}, bf16[11,240,128]{2,1,0:T(8,128)(2,1)S(1)}, u32[]{:S(2)}, u32[]{:S(2)}) collective-permute-start(bf16[11,240,128]{2,1,0:T(8,128)(2,1)S(1)} %get-tuple-element.67), channel_id=1, source_target_pairs={{32,64},{96,128},{160,192},{64,32},{128,96},{192,160},{33,65},{97,... | collective-permute-start | bytes 2027528 | tf_op jit(solution)/shard_map/ppermute | solution.py:421

commit v4 on v3

--- a/solution.py
+++ b/solution.py
@@ -358,6 +358,121 @@
     return partial_call(False, window, k, v, kgain, kinverse, *rows, (q, qgain, qinverse), start, count)
 
 
+def both_kernel(start, group, steps, window, *refs):
+    st_own, st_far = refs[-2:]
+    ob, oa, own_stats = refs[-6 - 2 * group : -3 - 2 * group]
+    step = pl.program_id(0)
+
+    @pl.when(step < steps)
+    def _():
+        both_step(start, group, step, window, *refs)
+
+    @pl.when(step == steps)
+    def _():
+        lane = lax.broadcasted_iota(jnp.int32, (3 * W, HD), 1)
+        for j in range(2):
+            own_stats[j] = lse_of(st_own[j])
+        below, above = (pieces_of(lse_of(st_far[j]), lane) for j in range(2))
+        ob[0], oa[0] = sides("frame", below, above)
+
+
+def both_step(start, group, step, window, *refs):
+    qinverse, kinverse, qb, qa, q, k, v, qgain, kgain, low, high, part, ob, oa, _ = refs[:15]
+    kxs, vxs = refs[15 : 15 + group], refs[15 + group : 15 + 2 * group]
+    gaps, st_own, st_far = refs[-3:]
+    slot = start + step * group
+
+    @pl.when(step == 0)
+    def _():
+        for st in (st_own, st_far):
+            for j in range(2):
+                st[j, 0] = jnp.zeros((3 * W, HD), F32)
+                st[j, 1] = jnp.ones((3 * W, HD), F32)
+        fill_ones(vxs)
+        fill_gaps(gaps)
+
+    scores = []
+    for g in range(group):
+        own_keys, own_values = k[:, :, :, lanes(g)], v[:, :, :, lanes(g)]
+        fill_lines(kxs[g], vxs[g], own_keys, own_values, kinverse[...], kgain[:, lanes(g)], low.at[g], high.at[g])
+        masks = biases(gaps, window, slot + g)
+        cross = jnp.where(window[slot + g, 0] > 0, 0.0, NEG)
+        qn = normed(q[:, :, :, lanes(g)], qinverse[...], qgain[:, lanes(g)].reshape(1, 1, 1, HD))
+        for i in range(3):
+            own = qn[:, i].reshape(2 * W, HD)
+            far = masks[i] + cross
+            asked = sides("frame", qb[g, i * W : (i + 1) * W], qa[g, i * W : (i + 1) * W])
+            for j in range(2):
+                queries = jnp.concatenate([own, asked[j]], axis=0)
+                order = [masks[i], far, masks[i]] if j == 0 else [far, masks[i], masks[i]]
+                raw = dot_t(queries, kxs[g][j, lines_of(i)])
+                scores.append([raw[W * n : W * (n + 1)] + order[n] for n in range(3)])
+    tops, weights = [], []
+    for s0, s1 in zip(scores[::2], scores[1::2]):
+        first, second = (row_max(jnp.maximum(s0[n], s1[n])) for n in range(2))
+        below, above = row_max(s0[2]), row_max(s1[2])
+        tops.append((jnp.concatenate([first, second], axis=0), below, above))
+        for s, last in ((s0, below), (s1, above)):
+            parts = [weights_of(a, b) for a, b in zip(s, (first, second, last))]
+            weights.append(jnp.concatenate(parts, axis=0))
+    lane = lax.broadcasted_iota(jnp.int32, (W, HD), 1)
+    for g in range(group):
+        here = (lane & 31) == step * group + g
+        for i in range(3):
+            w0, w1 = weights[6 * g + 2 * i : 6 * g + 2 * i + 2]
+            top, top_b, top_a = tops[3 * g + i]
+            m0 = jnp.dot(w0, vxs[g][0, lines_of(i)], preferred_element_type=F32)
+            m1 = jnp.dot(w1, vxs[g][1, lines_of(i)], preferred_element_type=F32)
+            at = slice(i * W, (i + 1) * W)
+            for n in range(2):
+                own = m0[W * n : W * (n + 1)] + m1[W * n : W * (n + 1)]
+                part[g, n, i] = divided(own)
+                mark(st_own.at[n], at, here, top[W * n : W * (n + 1)], own)
+            for n, far in ((0, m0[2 * W :]), (1, m1[2 * W :])):
+                mark(st_far.at[n], at, here, (top_b, top_a)[n], far)
+            ob[g, at], oa[g, at] = sides("frame", divided(m0[2 * W :]), divided(m1[2 * W :]))
+
+
+def both_partial(window, qb, qa, q, k, v, qgain, kgain, qinverse, kinverse, low, high, start, count):
+    group = 2
+    steps = count // group
+
+    def step_of(s):
+        return jnp.minimum(s, steps - 1)
+
+    heads = pl.BlockSpec((2, 3, W, group * HD), lambda s, window: (0, 0, 0, start // group + step_of(s)))
+    gains = pl.BlockSpec((1, group * HD), lambda s, window: (0, start // group + step_of(s)))
+    rows = pl.BlockSpec((group, 2, 2, W, HD), lambda s, window: (step_of(s), 0, 0, 0, 0))
+    q_spec = pl.BlockSpec((group, 3 * W, HD), lambda s, window: (step_of(s), 0, 0))
+    o_spec = pl.BlockSpec((group, 3 * W, HD), lambda s, window: (s, 0, 0))
+    out = jax.ShapeDtypeStruct((count + 1, 3 * W, HD), BF16)
+    stat = pltpu.VMEM((2, 2, 3 * W, HD), F32)
+    return pl.pallas_call(
+        functools.partial(both_kernel, start, group, steps),
+        grid_spec=pltpu.PrefetchScalarGridSpec(
+            num_scalar_prefetch=1,
+            grid=(steps + 1,),
+            in_specs=[whole((2, 3, W, HD))] * 2 + [q_spec] * 2 + [heads] * 3 + [gains] * 2 + [rows] * 2,
+            out_specs=[
+                pl.BlockSpec((group, 2, 3, W, HD), lambda s, window: (step_of(s), 0, 0, 0, 0)),
+                o_spec,
+                o_spec,
+                whole((2, 3 * W, HD)),
+            ],
+            scratch_shapes=line_scratch(group) + [pltpu.VMEM((2, 3, W, 3 * W), jnp.int32), stat, stat],
+        ),
+        out_shape=[
+            jax.ShapeDtypeStruct((count, 2, 3, W, HD), BF16),
+            out,
+            out,
+            jax.ShapeDtypeStruct((2, 3 * W, HD), F32),
+        ],
+        compiler_params=params(16),
+        cost_estimate=cost(1.1 * count),
+        name="both_partial",
+    )(window, qinverse, kinverse, qb, qa, q, k, v, qgain, kgain, low, high)
+
+
 def merge_kernel(start, group, window, part, lse, ob, oa, sb, sa, *refs):
     out, shares = refs[-2:]
     lane = lax.broadcasted_iota(jnp.int32, (3 * W, HD), 1)
@@ -429,19 +544,16 @@
     for start, count in chunks:
         packed = pack_queries(window, q, q_gain, q_inverse, start, count)
         k, *packed = lax.optimization_barrier((k, *packed))
-        if queries:
-            *packed, queries[0][0], queries[0][1] = lax.optimization_barrier((*packed, *queries[0]))
         packed_rows = pack_rows(window, k, v, k_gain, k_inverse, start, count)
         rows.append(exchange("height", *packed_rows))
         queries.append(exchange("frame", *packed))
         q, *_ = lax.optimization_barrier((q, *packed_rows))
-    parts = []
-    for n, (start, count) in enumerate(chunks):
-        far = far_partial(window, queries[n], k, v, k_gain, k_inverse, rows[n], start, count)
-        q, *queries[1] = lax.optimization_barrier((q, *queries[1]))
-        part, lse = own_partial(window, q, k, v, *norms, rows[n], start, count)
-        k, part = lax.optimization_barrier((k, part))
-        parts.append((part, lse, *exchange("frame", *far), start, count))
+    (start, count), (late_start, late_count) = chunks
+    part, *far, lse = both_partial(window, *queries[0], q, k, v, *norms, *rows[0], start, count)
+    parts = [(part, lse, *exchange("frame", *far), start, count)]
+    far = far_partial(window, queries[1], k, v, k_gain, k_inverse, rows[1], late_start, late_count)
+    part, lse = own_partial(window, q, k, v, *norms, rows[1], late_start, late_count)
+    parts.append((part, lse, *exchange("frame", *far), late_start, late_count))
     out = None
     for part in parts:
         out = merge(window, out, *part)

time: 92.1 us -> 91.4 us (level)
  Pallas kernels: 41.2 us -> 36.6 us
  waiting for transfers between devices: 7.63 us -> 10.2 us
  starting transfers between devices: 32.7 us -> 34 us
    pallas_call x4 -> x2, Pallas kernels: 30.1 us -> 15 us  [partial_call(): pl.pallas_call(functools.partial(partial_kernel, far, start, group, steps...]
    pallas_call x0 -> x1, Pallas kernels: none -> 10.5 us  [both_partial(): pl.pallas_call(functools.partial(both_kernel, start, group, steps), grid_...]
    ppermute x12, waiting for transfers between devices: 7.63 us -> 10.2 us  [exchange(): out.append(lax.ppermute(block, axis, pairs + [(b, a) for a, b in pairs]))]
    ppermute x12, starting transfers between devices: 32.7 us -> 34 us  [exchange(): out.append(lax.ppermute(block, axis, pairs + [(b, a) for a, b in pairs]))]
  transfers between devices with their start and end apart: 12 -> 12, of which waited for: 3 -> 3; matrix products, arithmetic and copies ran while one was open for 0% -> 0% of each run, Pallas kernels for 39% -> 34%
where the time goes in v4:
time: 91.4 us; the launch traced here: 91 us
  Pallas kernels  36.6 us (40%)
  starting transfers between devices  34 us (37%)
  waiting for transfers between devices  10.2 us (11%)
  local copies, waits for them, and re-layouts  3.76 us (4%)
  other arithmetic  3.53 us (4%)
  blocking collectives  2.63 us (3%)
    ppermute x12, starting transfers between devices, exchange(): out.append(lax.ppermute(block, axis, pairs + [(b, a) for a, b in pairs]))  34 us
    pallas_call x2, Pallas kernels, partial_call(): pl.pallas_call(functools.partial(partial_kernel, far, start, group, steps...  15 us
    pallas_call x1, Pallas kernels, both_partial(): pl.pallas_call(functools.partial(both_kernel, start, group, steps), grid_...  10.5 us
    ppermute x12, waiting for transfers between devices, exchange(): out.append(lax.ppermute(block, axis, pairs + [(b, a) for a, b in pairs]))  10.2 us
    pallas_call x2, Pallas kernels, merge(): pl.pallas_call(functools.partial(merge_kernel, start, group), grid_spec=p...  5.68 us
    reduce_sum x1, other arithmetic, squares_of(): return jnp.sum(values * values, axis=-1)  3.52 us
    unnamed x17, local copies, waits for them, and re-layouts  3.51 us
    pallas_call x2, Pallas kernels, pack_rows(): pl.pallas_call(functools.partial(pack_rows_kernel, group), grid_spec=pltp...  2.79 us
  transfers between devices with their start and end apart: 12, of which 3 were waited for; matrix products, arithmetic and copies ran while one was open for 0% of the time, Pallas kernels for 34%

profile of v4, /device:TPU:38, one launch (start us, length us, event | category | flops | bytes accessed | tf_op | source)
XLA Modules:
  0.0 91.0 jit_solution(16528380600220872702)
XLA Ops:
  0.0 3.5 %multiply_reduce_fusion = (f32[2,3,80]{2,1,0:T(4,128)S(1)}, f32[2,3,80]{2,1,0:T(4,128)S(1)}) fusion(bf16[2,3,80,2560]{3,2,1,0:T(8,128)(2,1)} %refs_4_, bf16[2,3,80,2560]{3,2,1,0:T(8,128)(2,1)} %refs_5_), kind=kLoop, calls=%fused_computation | loop fusion | flops 7371840 | bytes 4919040 | tf_op jit(solution)/shard_map/reduce_sum | solution.py:565
  3.5 2.6 %all-reduce = (f32[2,3,80]{2,1,0:T(4,128)S(1)}, f32[2,3,80]{2,1,0:T(4,128)S(1)}) all-reduce(f32[2,3,80]{2,1,0:T(4,128)S(1)} %get-tuple-element.56, f32[2,3,80]{2,1,0:T(4,128)S(1)} %get-tuple-element.55), channel_id=1, replica_groups=mesh['frame'=8,'height'=16,'head'=2] {'head'}, use_global_device_ids=true, to_apply=%region_1.0 | all-reduce | flops 960 | bytes 7680 | tf_op jit(solution)/shard_map/psum | solution.py:570
  6.3 0.1 copy.16.window
  6.4 0.1 broadcast_in_dim.20.inverse.refs_2_.refs_0_
  6.5 0.0 copy-start.1
  6.5 1.7 %copy-done.1 = bf16[2,3,80,2560]{3,2,1,0:T(8,128)(2,1)S(1)} copy-done((bf16[2,3,80,2560]{3,2,1,0:T(8,128)(2,1)S(1)}, bf16[2,3,80,2560]{3,2,1,0:T(8,128)(2,1)}, u32[]{:S(2)}) %copy-start.1) | copy-done | bytes 2457624
  8.2 1.3 %pack_queries.2 = (bf16[10,240,128]{2,1,0:T(8,128)(2,1)S(1)}, bf16[10,240,128]{2,1,0:T(8,128)(2,1)S(1)}) custom-call(s32[20,3]{1,0:T(8,128)S(1)} %copy.16.window, bf16[2,3,80,2560]{3,2,1,0:T(8,128)(2,1)S(1)} %copy-done.1, f32[1,2560]{1,0:T(1,128)S(1)} %broadcast_in_dim.9.gain.refs_1_.refs_7_, f32[2,3,80,128]{3,2,1,0:T(8,128)S(1)} %broadcast_in_dim.20.inverse.refs_2_.refs_0_), custom_call_target="tpu_custom_call" | custom-call | bytes 3000000 | tf_op jit(solution)/shard_map/pack_queries/pallas_call | solution.py:76
  9.5 0.1 broadcast_in_dim.8.inverse.kinverse.refs_1_
  9.6 1.7 %copy-done.3 = bf16[2,3,80,2560]{3,2,1,0:T(8,128)(2,1)S(1)} copy-done((bf16[2,3,80,2560]{3,2,1,0:T(8,128)(2,1)S(1)}, bf16[2,3,80,2560]{3,2,1,0:T(8,128)(2,1)}, u32[]{:S(2)}) %copy-start.3) | copy-done | bytes 2457624
  11.3 1.4 %pack_rows.2 = (bf16[10,2,2,80,128]{4,3,2,1,0:T(8,128)(2,1)S(1)}, bf16[10,2,2,80,128]{4,3,2,1,0:T(8,128)(2,1)S(1)}) custom-call(s32[20,3]{1,0:T(8,128)S(1)} %copy.16.window, bf16[2,3,80,2560]{3,2,1,0:T(8,128)(2,1)S(1)} %copy-done, bf16[2,3,80,2560]{3,2,1,0:T(8,128)(2,1)S(1)} %copy-done.3, f32[1,2560]{1,0:T(1,128)S(1)} %broadcast_in_dim.21.gain.kgain.refs_8_, ...), custom_call_target="tpu_custom_call" | custom-call | bytes 4500000 | tf_op jit(solution)/shard_map/pack_rows/pallas_call | solution.py:95
  12.7 1.7 %collective-permute-start.8 = (bf16[10,2,2,80,128]{4,3,2,1,0:T(8,128)(2,1)S(1)}, bf16[10,2,2,80,128]{4,3,2,1,0:T(8,128)(2,1)S(1)}, u32[]{:S(2)}, u32[]{:S(2)}) collective-permute-start(bf16[10,2,2,80,128]{4,3,2,1,0:T(8,128)(2,1)S(1)} %get-tuple-element.32), channel_id=1, source_target_pairs={{0,2},{4,6},{8,10},{12,14},{16,18},{20,22},{24,26},{28,30},{2,0},{... | collective-permute-start | bytes 2457608 | tf_op jit(solution)/shard_map/ppermute | solution.py:536
  14.4 0.1 collective-permute-start.6
  14.5 5.6 %collective-permute-start.7 = (bf16[10,240,128]{2,1,0:T(8,128)(2,1)S(1)}, bf16[10,240,128]{2,1,0:T(8,128)(2,1)S(1)}, u32[]{:S(2)}, u32[]{:S(2)}) collective-permute-start(bf16[10,240,128]{2,1,0:T(8,128)(2,1)S(1)} %get-tuple-element.48), channel_id=1, source_target_pairs={{32,64},{96,128},{160,192},{64,32},{128,96},{192,160},{33,65},{97,... | collective-permute-start | bytes 1843208 | tf_op jit(solution)/shard_map/ppermute | solution.py:536
  20.1 4.4 %collective-permute-start.9 = (bf16[10,2,2,80,128]{4,3,2,1,0:T(8,128)(2,1)S(1)}, bf16[10,2,2,80,128]{4,3,2,1,0:T(8,128)(2,1)S(1)}, u32[]{:S(2)}, u32[]{:S(2)}) collective-permute-start(bf16[10,2,2,80,128]{4,3,2,1,0:T(8,128)(2,1)S(1)} %get-tuple-element.33), channel_id=1, source_target_pairs={{2,4},{6,8},{10,12},{14,16},{18,20},{22,24},{26,28},{4,2},{8,6},{1... | collective-permute-start | bytes 2457608 | tf_op jit(solution)/shard_map/ppermute | solution.py:536
  24.5 1.3 %pack_queries.3 = (bf16[10,240,128]{2,1,0:T(8,128)(2,1)S(1)}, bf16[10,240,128]{2,1,0:T(8,128)(2,1)S(1)}) custom-call(s32[20,3]{1,0:T(8,128)S(1)} %copy.16.window, bf16[2,3,80,2560]{3,2,1,0:T(8,128)(2,1)S(1)} %copy-done.1, f32[1,2560]{1,0:T(1,128)S(1)} %broadcast_in_dim.9.gain.refs_1_.refs_7_, f32[2,3,80,128]{3,2,1,0:T(8,128)S(1)} %broadcast_in_dim.20.inverse.refs_2_.refs_0_), custom_call_target="tpu_custom_call" | custom-call | bytes 3000000 | tf_op jit(solution)/shard_map/pack_queries/pallas_call | solution.py:76
  25.8 1.4 %pack_rows.3 = (bf16[10,2,2,80,128]{4,3,2,1,0:T(8,128)(2,1)S(1)}, bf16[10,2,2,80,128]{4,3,2,1,0:T(8,128)(2,1)S(1)}) custom-call(s32[20,3]{1,0:T(8,128)S(1)} %copy.16.window, bf16[2,3,80,2560]{3,2,1,0:T(8,128)(2,1)S(1)} %copy-done, bf16[2,3,80,2560]{3,2,1,0:T(8,128)(2,1)S(1)} %copy-done.4, f32[1,2560]{1,0:T(1,128)S(1)} %broadcast_in_dim.21.gain.kgain.refs_8_, ...), custom_call_target="tpu_custom_call" | custom-call | bytes 4500000 | tf_op jit(solution)/shard_map/pack_rows/pallas_call | solution.py:95
  27.3 0.5 collective-permute-start
  27.8 2.3 %collective-permute-done.6.refs_2_ = bf16[10,240,128]{2,1,0:T(8,128)(2,1)S(1)} collective-permute-done((bf16[10,240,128]{2,1,0:T(8,128)(2,1)S(1)}, bf16[10,240,128]{2,1,0:T(8,128)(2,1)S(1)}, u32[]{:S(2)}, u32[]{:S(2)}) %collective-permute-start.6) | collective-permute-done | bytes 614432 | tf_op jit(solution)/shard_map/ppermute | solution.py:536
  30.0 4.3 %collective-permute-start.1 = (bf16[10,2,2,80,128]{4,3,2,1,0:T(8,128)(2,1)S(1)}, bf16[10,2,2,80,128]{4,3,2,1,0:T(8,128)(2,1)S(1)}, u32[]{:S(2)}, u32[]{:S(2)}) collective-permute-start(bf16[10,2,2,80,128]{4,3,2,1,0:T(8,128)(2,1)S(1)} %get-tuple-element.39), channel_id=1, source_target_pairs={{2,4},{6,8},{10,12},{14,16},{18,20},{22,24},{26,28},{4,2},{8,6},{1... | collective-permute-start | bytes 2457608 | tf_op jit(solution)/shard_map/ppermute | solution.py:536
  34.4 0.4 collective-permute-start.2
  34.8 5.4 %collective-permute-start.3 = (bf16[10,240,128]{2,1,0:T(8,128)(2,1)S(1)}, bf16[10,240,128]{2,1,0:T(8,128)(2,1)S(1)}, u32[]{:S(2)}, u32[]{:S(2)}) collective-permute-start(bf16[10,240,128]{2,1,0:T(8,128)(2,1)S(1)} %get-tuple-element.44), channel_id=1, source_target_pairs={{32,64},{96,128},{160,192},{64,32},{128,96},{192,160},{33,65},{97,... | collective-permute-start | bytes 1843208 | tf_op jit(solution)/shard_map/ppermute | solution.py:536
  40.2 5.1 %collective-permute-done.9.refs_10_ = bf16[10,2,2,80,128]{4,3,2,1,0:T(8,128)(2,1)S(1)} collective-permute-done((bf16[10,2,2,80,128]{4,3,2,1,0:T(8,128)(2,1)S(1)}, bf16[10,2,2,80,128]{4,3,2,1,0:T(8,128)(2,1)S(1)}, u32[]{:S(2)}, u32[]{:S(2)}) %collective-permute-start.9) | collective-permute-done | bytes 819232 | tf_op jit(solution)/shard_map/ppermute | solution.py:536
  45.3 10.5 %both_partial.1 = (bf16[10,2,3,80,128]{4,3,2,1,0:T(8,128)(2,1)S(1)}, bf16[11,240,128]{2,1,0:T(8,128)(2,1)S(1)}, bf16[11,240,128]{2,1,0:T(8,128)(2,1)S(1)}, f32[2,240,128]{2,1,0:T(8,128)S(1)}) custom-call(s32[20,3]{1,0:T(8,128)S(1)} %copy.16.window, f32[2,3,80,128]{3,2,1,0:T(8,128)S(1)} %broadcast_in_dim.20.inverse.refs_2_.refs_0_, ...), custom_call_target="tpu_custom_call" | custom-call | bytes 33000000 | tf_op jit(solution)/shard_map/both_partial/pallas_call | solution.py:450
  55.8 0.1 collective-permute-start.10
  55.9 6.0 %collective-permute-start.11 = (bf16[11,240,128]{2,1,0:T(8,128)(2,1)S(1)}, bf16[11,240,128]{2,1,0:T(8,128)(2,1)S(1)}, u32[]{:S(2)}, u32[]{:S(2)}) collective-permute-start(bf16[11,240,128]{2,1,0:T(8,128)(2,1)S(1)} %get-tuple-element.52), channel_id=1, source_target_pairs={{32,64},{96,128},{160,192},{64,32},{128,96},{192,160},{33,65},{97,... | collective-permute-start | bytes 2027528 | tf_op jit(solution)/shard_map/ppermute | solution.py:536
  62.0 7.1 %far_partial.1 = (bf16[11,240,128]{2,1,0:T(8,128)(2,1)S(1)}, bf16[11,240,128]{2,1,0:T(8,128)(2,1)S(1)}) custom-call(s32[20,3]{1,0:T(8,128)S(1)} %copy.16.window, f32[2,3,80,128]{3,2,1,0:T(8,128)S(1)} %broadcast_in_dim.8.inverse.kinverse.refs_1_, bf16[2,3,80,2560]{3,2,1,0:T(8,128)(2,1)S(1)} %copy-done, bf16[2,3,80,2560]{3,2,1,0:T(8,128)(2,1)S(1)} %copy-done.4, ...), custom_call_target="tpu_custom_call" | custom-call | bytes 18000000 | tf_op jit(solution)/shard_map/far_partial/pallas_call | solution.py:336
  69.2 0.1 collective-permute-start.4
  69.3 5.4 %collective-permute-start.5 = (bf16[11,240,128]{2,1,0:T(8,128)(2,1)S(1)}, bf16[11,240,128]{2,1,0:T(8,128)(2,1)S(1)}, u32[]{:S(2)}, u32[]{:S(2)}) collective-permute-start(bf16[11,240,128]{2,1,0:T(8,128)(2,1)S(1)} %get-tuple-element.46), channel_id=1, source_target_pairs={{32,64},{96,128},{160,192},{64,32},{128,96},{192,160},{33,65},{97,... | collective-permute-start | bytes 2027528 | tf_op jit(solution)/shard_map/ppermute | solution.py:536
  74.6 7.9 %own_partial.1 = (bf16[10,2,3,80,128]{4,3,2,1,0:T(8,128)(2,1)S(1)}, f32[2,240,128]{2,1,0:T(8,128)S(1)}) custom-call(s32[20,3]{1,0:T(8,128)S(1)} %copy.16.window, f32[2,3,80,128]{3,2,1,0:T(8,128)S(1)} %broadcast_in_dim.8.inverse.kinverse.refs_1_, bf16[2,3,80,2560]{3,2,1,0:T(8,128)(2,1)S(1)} %copy-done, bf16[2,3,80,2560]{3,2,1,0:T(8,128)(2,1)S(1)} %copy-done.4, ...), custom_call_target="tpu_custom_call" | custom-call | bytes 18000000 | tf_op jit(solution)/shard_map/own_partial/pallas_call | solution.py:336
  82.6 2.8 %merge.2.refs_0_ = bf16[2,3,80,2560]{3,2,1,0:T(8,128)(2,1)} custom-call(s32[20,3]{1,0:T(8,128)S(1)} %copy.16.window, bf16[10,2,3,80,128]{4,3,2,1,0:T(8,128)(2,1)S(1)} %get-tuple-element.49.part, f32[2,240,128]{2,1,0:T(8,128)S(1)} %get-tuple-element.50.lse, bf16[11,240,128]{2,1,0:T(8,128)(2,1)S(1)} %collective-permute-done.10.ob.sb, ...), custom_call_target="tpu_custom_call" | custom-call | bytes 7500000 | tf_op jit(solution)/shard_map/merge/pallas_call | solution.py:507
  85.4 2.8 %collective-permute-done.5.oa.sa = bf16[11,240,128]{2,1,0:T(8,128)(2,1)S(1)} collective-permute-done((bf16[11,240,128]{2,1,0:T(8,128)(2,1)S(1)}, bf16[11,240,128]{2,1,0:T(8,128)(2,1)S(1)}, u32[]{:S(2)}, u32[]{:S(2)}) %collective-permute-start.5) | collective-permute-done | bytes 675872 | tf_op jit(solution)/shard_map/ppermute | solution.py:536
  88.2 2.8 %merge.3 = bf16[2,3,80,2560]{3,2,1,0:T(8,128)(2,1)} custom-call(s32[20,3]{1,0:T(8,128)S(1)} %copy.16.window, bf16[10,2,3,80,128]{4,3,2,1,0:T(8,128)(2,1)S(1)} %get-tuple-element.41.part, f32[2,240,128]{2,1,0:T(8,128)S(1)} %get-tuple-element.42.lse, bf16[11,240,128]{2,1,0:T(8,128)(2,1)S(1)} %collective-permute-done.4.ob.sb, ...), custom_call_target="tpu_custom_call", output_to_operand_aliasing={{}: (7, {})} | custom-call | bytes 7500000 | tf_op jit(solution)/shard_map/merge/pallas_call | solution.py:507
  (26 shorter events, 0.1 us)
Async XLA Ops:
  0.0 6.2 %copy-start.5 = (f32[2560]{0:T(1024)S(1)}, f32[2560]{0:T(1024)}, u32[]{:S(2)}) copy-start(f32[2560]{0:T(1024)} %param.10) | copy-start | bytes 30724
  0.0 6.2 %copy-start.6 = (f32[2560]{0:T(1024)S(1)}, f32[2560]{0:T(1024)}, u32[]{:S(2)}) copy-start(f32[2560]{0:T(1024)} %param.9) | copy-start | bytes 30724
  0.0 6.2 %copy-start.7 = (s32[20,3]{0,1:T(4,128)S(1)}, s32[20,3]{0,1:T(4,128)}, u32[]{:S(2)}) copy-start(s32[20,3]{0,1:T(4,128)} %param.11) | copy-start | bytes 724
  3.5 6.1 %copy-start = (bf16[2,3,80,2560]{3,2,1,0:T(8,128)(2,1)S(1)}, bf16[2,3,80,2560]{3,2,1,0:T(8,128)(2,1)}, u32[]{:S(2)}) copy-start(bf16[2,3,80,2560]{3,2,1,0:T(8,128)(2,1)} %refs_5_) | copy-start | bytes 7372804
  6.5 1.7 %copy-start.1 = (bf16[2,3,80,2560]{3,2,1,0:T(8,128)(2,1)S(1)}, bf16[2,3,80,2560]{3,2,1,0:T(8,128)(2,1)}, u32[]{:S(2)}) copy-start(bf16[2,3,80,2560]{3,2,1,0:T(8,128)(2,1)} %refs_4_) | copy-start | bytes 7372804
  9.6 1.7 %copy-start.3 = (bf16[2,3,80,2560]{3,2,1,0:T(8,128)(2,1)S(1)}, bf16[2,3,80,2560]{3,2,1,0:T(8,128)(2,1)}, u32[]{:S(2)}) copy-start(bf16[2,3,80,2560]{3,2,1,0:T(8,128)(2,1)} %refs_6_.1) | copy-start | bytes 7372804
  12.7 13.1 %copy-start.4 = (bf16[2,3,80,2560]{3,2,1,0:T(8,128)(2,1)S(1)}, bf16[2,3,80,2560]{3,2,1,0:T(8,128)(2,1)}, u32[]{:S(2)}) copy-start(bf16[2,3,80,2560]{3,2,1,0:T(8,128)(2,1)} %refs_6_.1) | copy-start | bytes 7372804
  12.7 22.0 %collective-permute-start.8 = (bf16[10,2,2,80,128]{4,3,2,1,0:T(8,128)(2,1)S(1)}, bf16[10,2,2,80,128]{4,3,2,1,0:T(8,128)(2,1)S(1)}, u32[]{:S(2)}, u32[]{:S(2)}) collective-permute-start(bf16[10,2,2,80,128]{4,3,2,1,0:T(8,128)(2,1)S(1)} %get-tuple-element.32), channel_id=1, source_target_pairs={{0,2},{4,6},{8,10},{12,14},{16,18},{20,22},{24,26},{28,30},{2,0},{... | collective-permute-start | bytes 2457608 | tf_op jit(solution)/shard_map/ppermute | solution.py:536
  14.4 15.6 %collective-permute-start.6 = (bf16[10,240,128]{2,1,0:T(8,128)(2,1)S(1)}, bf16[10,240,128]{2,1,0:T(8,128)(2,1)S(1)}, u32[]{:S(2)}, u32[]{:S(2)}) collective-permute-start(bf16[10,240,128]{2,1,0:T(8,128)(2,1)S(1)} %get-tuple-element.47), channel_id=1, source_target_pairs={{0,32},{64,96},{128,160},{192,224},{32,0},{96,64},{160,128},{224,1... | collective-permute-start | bytes 1843208 | tf_op jit(solution)/shard_map/ppermute | solution.py:536
  14.5 19.9 %collective-permute-start.7 = (bf16[10,240,128]{2,1,0:T(8,128)(2,1)S(1)}, bf16[10,240,128]{2,1,0:T(8,128)(2,1)S(1)}, u32[]{:S(2)}, u32[]{:S(2)}) collective-permute-start(bf16[10,240,128]{2,1,0:T(8,128)(2,1)S(1)} %get-tuple-element.48), channel_id=1, source_target_pairs={{32,64},{96,128},{160,192},{64,32},{128,96},{192,160},{33,65},{97,... | collective-permute-start | bytes 1843208 | tf_op jit(solution)/shard_map/ppermute | solution.py:536
  20.1 25.2 %collective-permute-start.9 = (bf16[10,2,2,80,128]{4,3,2,1,0:T(8,128)(2,1)S(1)}, bf16[10,2,2,80,128]{4,3,2,1,0:T(8,128)(2,1)S(1)}, u32[]{:S(2)}, u32[]{:S(2)}) collective-permute-start(bf16[10,2,2,80,128]{4,3,2,1,0:T(8,128)(2,1)S(1)} %get-tuple-element.33), channel_id=1, source_target_pairs={{2,4},{6,8},{10,12},{14,16},{18,20},{22,24},{26,28},{4,2},{8,6},{1... | collective-permute-start | bytes 2457608 | tf_op jit(solution)/shard_map/ppermute | solution.py:536
  25.8 19.5 %copy-start.2 = (bf16[2,3,80,2560]{3,2,1,0:T(8,128)(2,1)S(1)}, bf16[2,3,80,2560]{3,2,1,0:T(8,128)(2,1)}, u32[]{:S(2)}) copy-start(bf16[2,3,80,2560]{3,2,1,0:T(8,128)(2,1)} %refs_4_) | copy-start | bytes 7372804
  27.3 34.7 %collective-permute-start = (bf16[10,2,2,80,128]{4,3,2,1,0:T(8,128)(2,1)S(1)}, bf16[10,2,2,80,128]{4,3,2,1,0:T(8,128)(2,1)S(1)}, u32[]{:S(2)}, u32[]{:S(2)}) collective-permute-start(bf16[10,2,2,80,128]{4,3,2,1,0:T(8,128)(2,1)S(1)} %get-tuple-element.38), channel_id=1, source_target_pairs={{0,2},{4,6},{8,10},{12,14},{16,18},{20,22},{24,26},{28,30},{2,0},{... | collective-permute-start | bytes 2457608 | tf_op jit(solution)/shard_map/ppermute | solution.py:536
  30.0 31.9 %collective-permute-start.1 = (bf16[10,2,2,80,128]{4,3,2,1,0:T(8,128)(2,1)S(1)}, bf16[10,2,2,80,128]{4,3,2,1,0:T(8,128)(2,1)S(1)}, u32[]{:S(2)}, u32[]{:S(2)}) collective-permute-start(bf16[10,2,2,80,128]{4,3,2,1,0:T(8,128)(2,1)S(1)} %get-tuple-element.39), channel_id=1, source_target_pairs={{2,4},{6,8},{10,12},{14,16},{18,20},{22,24},{26,28},{4,2},{8,6},{1... | collective-permute-start | bytes 2457608 | tf_op jit(solution)/shard_map/ppermute | solution.py:536
  34.4 21.5 %collective-permute-start.2 = (bf16[10,240,128]{2,1,0:T(8,128)(2,1)S(1)}, bf16[10,240,128]{2,1,0:T(8,128)(2,1)S(1)}, u32[]{:S(2)}, u32[]{:S(2)}) collective-permute-start(bf16[10,240,128]{2,1,0:T(8,128)(2,1)S(1)} %get-tuple-element.43), channel_id=1, source_target_pairs={{0,32},{64,96},{128,160},{192,224},{32,0},{96,64},{160,128},{224,1... | collective-permute-start | bytes 1843208 | tf_op jit(solution)/shard_map/ppermute | solution.py:536
  34.8 27.2 %collective-permute-start.3 = (bf16[10,240,128]{2,1,0:T(8,128)(2,1)S(1)}, bf16[10,240,128]{2,1,0:T(8,128)(2,1)S(1)}, u32[]{:S(2)}, u32[]{:S(2)}) collective-permute-start(bf16[10,240,128]{2,1,0:T(8,128)(2,1)S(1)} %get-tuple-element.44), channel_id=1, source_target_pairs={{32,64},{96,128},{160,192},{64,32},{128,96},{192,160},{33,65},{97,... | collective-permute-start | bytes 1843208 | tf_op jit(solution)/shard_map/ppermute | solution.py:536
  55.8 26.7 %collective-permute-start.10 = (bf16[11,240,128]{2,1,0:T(8,128)(2,1)S(1)}, bf16[11,240,128]{2,1,0:T(8,128)(2,1)S(1)}, u32[]{:S(2)}, u32[]{:S(2)}) collective-permute-start(bf16[11,240,128]{2,1,0:T(8,128)(2,1)S(1)} %get-tuple-element.51), channel_id=1, source_target_pairs={{0,32},{64,96},{128,160},{192,224},{32,0},{96,64},{160,128},{224,1... | collective-permute-start | bytes 2027528 | tf_op jit(solution)/shard_map/ppermute | solution.py:536
  55.9 26.6 %collective-permute-start.11 = (bf16[11,240,128]{2,1,0:T(8,128)(2,1)S(1)}, bf16[11,240,128]{2,1,0:T(8,128)(2,1)S(1)}, u32[]{:S(2)}, u32[]{:S(2)}) collective-permute-start(bf16[11,240,128]{2,1,0:T(8,128)(2,1)S(1)} %get-tuple-element.52), channel_id=1, source_target_pairs={{32,64},{96,128},{160,192},{64,32},{128,96},{192,160},{33,65},{97,... | collective-permute-start | bytes 2027528 | tf_op jit(solution)/shard_map/ppermute | solution.py:536
  69.2 16.3 %collective-permute-start.4 = (bf16[11,240,128]{2,1,0:T(8,128)(2,1)S(1)}, bf16[11,240,128]{2,1,0:T(8,128)(2,1)S(1)}, u32[]{:S(2)}, u32[]{:S(2)}) collective-permute-start(bf16[11,240,128]{2,1,0:T(8,128)(2,1)S(1)} %get-tuple-element.45), channel_id=1, source_target_pairs={{0,32},{64,96},{128,160},{192,224},{32,0},{96,64},{160,128},{224,1... | collective-permute-start | bytes 2027528 | tf_op jit(solution)/shard_map/ppermute | solution.py:536
  69.3 18.9 %collective-permute-start.5 = (bf16[11,240,128]{2,1,0:T(8,128)(2,1)S(1)}, bf16[11,240,128]{2,1,0:T(8,128)(2,1)S(1)}, u32[]{:S(2)}, u32[]{:S(2)}) collective-permute-start(bf16[11,240,128]{2,1,0:T(8,128)(2,1)S(1)} %get-tuple-element.46), channel_id=1, source_target_pairs={{32,64},{96,128},{160,192},{64,32},{128,96},{192,160},{33,65},{97,... | collective-permute-start | bytes 2027528 | tf_op jit(solution)/shard_map/ppermute | solution.py:536

commit v5 on v4

--- a/solution.py
+++ b/solution.py
@@ -542,18 +542,23 @@
     chunks = ((0, FIRST), (FIRST, NH - FIRST))
     queries, rows = [], []
     for start, count in chunks:
+        packed_rows = pack_rows(window, k, v, k_gain, k_inverse, start, count)
+        q, *packed_rows = lax.optimization_barrier((q, *packed_rows))
         packed = pack_queries(window, q, q_gain, q_inverse, start, count)
         k, *packed = lax.optimization_barrier((k, *packed))
-        packed_rows = pack_rows(window, k, v, k_gain, k_inverse, start, count)
+        if rows:
+            packed_rows, packed, rows[0], queries[0] = lax.optimization_barrier(
+                (packed_rows, packed, rows[0], queries[0])
+            )
         rows.append(exchange("height", *packed_rows))
         queries.append(exchange("frame", *packed))
-        q, *_ = lax.optimization_barrier((q, *packed_rows))
     (start, count), (late_start, late_count) = chunks
     part, *far, lse = both_partial(window, *queries[0], q, k, v, *norms, *rows[0], start, count)
     parts = [(part, lse, *exchange("frame", *far), start, count)]
     far = far_partial(window, queries[1], k, v, k_gain, k_inverse, rows[1], late_start, late_count)
     part, lse = own_partial(window, q, k, v, *norms, rows[1], late_start, late_count)
     parts.append((part, lse, *exchange("frame", *far), late_start, late_count))
+    window, part = lax.optimization_barrier((window, part))
     out = None
     for part in parts:
         out = merge(window, out, *part)

time: 91.4 us -> 93.5 us (1.023)
  starting transfers between devices: 34 us -> 31.2 us
  waiting for transfers between devices: 10.2 us -> 12.6 us
  Pallas kernels: 36.6 us -> 38.5 us
  local copies, waits for them, and re-layouts: 3.76 us -> 5.22 us
    ppermute x12, starting transfers between devices: 34 us -> 31.2 us  [exchange(): out.append(lax.ppermute(block, axis, pairs + [(b, a) for a, b in pairs]))]
    ppermute x12, waiting for transfers between devices: 10.2 us -> 12.6 us  [exchange(): out.append(lax.ppermute(block, axis, pairs + [(b, a) for a, b in pairs]))]
    pallas_call x2, Pallas kernels: 5.68 us -> 7.57 us  [merge(): pl.pallas_call(functools.partial(merge_kernel, start, group), grid_spec=p...]
    unnamed x17 -> x27, local copies, waits for them, and re-layouts: 3.51 us -> 4.86 us
    reduce_sum x1 -> x2, other arithmetic: 3.52 us -> 2.98 us  [squares_of(): return jnp.sum(values * values, axis=-1)]
  transfers between devices with their start and end apart: 12 -> 12, of which waited for: 3 -> 3; matrix products, arithmetic and copies ran while one was open for 0% -> 0% of each run, Pallas kernels for 34% -> 36%
where the time goes in v5:
time: 93.5 us; the launch traced here: 93.1 us
  Pallas kernels  38.5 us (41%)
  starting transfers between devices  31.2 us (33%)
  waiting for transfers between devices  12.6 us (13%)
  local copies, waits for them, and re-layouts  5.22 us (6%)
  other arithmetic  3 us (3%)
  blocking collectives  2.46 us (3%)
    ppermute x12, starting transfers between devices, exchange(): out.append(lax.ppermute(block, axis, pairs + [(b, a) for a, b in pairs]))  31.2 us
    pallas_call x2, Pallas kernels, partial_call(): pl.pallas_call(functools.partial(partial_kernel, far, start, group, steps...  15 us
    ppermute x12, waiting for transfers between devices, exchange(): out.append(lax.ppermute(block, axis, pairs + [(b, a) for a, b in pairs]))  12.6 us
    pallas_call x1, Pallas kernels, both_partial(): pl.pallas_call(functools.partial(both_kernel, start, group, steps), grid_...  10.5 us
    pallas_call x2, Pallas kernels, merge(): pl.pallas_call(functools.partial(merge_kernel, start, group), grid_spec=p...  7.57 us
    unnamed x27, local copies, waits for them, and re-layouts  4.86 us
    reduce_sum x2, other arithmetic, squares_of(): return jnp.sum(values * values, axis=-1)  2.98 us
    pallas_call x2, Pallas kernels, pack_rows(): pl.pallas_call(functools.partial(pack_rows_kernel, group), grid_spec=pltp...  2.79 us
  transfers between devices with their start and end apart: 12, of which 3 were waited for; matrix products, arithmetic and copies ran while one was open for 0% of the time, Pallas kernels for 36%

profile of v5, /device:TPU:38, one launch (start us, length us, event | category | flops | bytes accessed | tf_op | source)
XLA Modules:
  0.0 93.1 jit_solution(12112311633016155713)
XLA Ops:
  0.0 2.4 %multiply_reduce_fusion = f32[2,3,80]{2,1,0:T(4,128)S(1)} fusion(bf16[2,3,80,2560]{3,2,1,0:T(8,128)(2,1)} %refs_4_), kind=kLoop, calls=%fused_computation | loop fusion | flops 3685920 | bytes 2459520 | tf_op jit(solution)/shard_map/reduce_sum | solution.py:570
  2.4 0.6 multiply_reduce_fusion.1
  3.0 0.1 copy.12.window
  3.1 2.5 %all-reduce = (f32[2,3,80]{2,1,0:T(4,128)S(1)}, f32[2,3,80]{2,1,0:T(4,128)S(1)}) all-reduce(f32[2,3,80]{2,1,0:T(4,128)S(1)} %multiply_reduce_fusion.1, f32[2,3,80]{2,1,0:T(4,128)S(1)} %multiply_reduce_fusion), channel_id=1, replica_groups=mesh['frame'=8,'height'=16,'head'=2] {'head'}, use_global_device_ids=true, to_apply=%region_1.0 | all-reduce | flops 960 | bytes 7680 | tf_op jit(solution)/shard_map/psum | solution.py:575
  5.6 0.1 broadcast_in_dim.8.inverse.kinverse.refs_1_
  5.7 1.7 %copy-done.2 = bf16[2,3,80,2560]{3,2,1,0:T(8,128)(2,1)S(1)} copy-done((bf16[2,3,80,2560]{3,2,1,0:T(8,128)(2,1)S(1)}, bf16[2,3,80,2560]{3,2,1,0:T(8,128)(2,1)}, u32[]{:S(2)}) %copy-start.2) | copy-done | bytes 2457624
  7.4 1.4 %pack_rows.2 = (bf16[10,2,2,80,128]{4,3,2,1,0:T(8,128)(2,1)S(1)}, bf16[10,2,2,80,128]{4,3,2,1,0:T(8,128)(2,1)S(1)}) custom-call(s32[20,3]{1,0:T(8,128)S(1)} %copy.12.window, bf16[2,3,80,2560]{3,2,1,0:T(8,128)(2,1)S(1)} %copy-done, bf16[2,3,80,2560]{3,2,1,0:T(8,128)(2,1)S(1)} %copy-done.2, f32[1,2560]{1,0:T(1,128)S(1)} %broadcast_in_dim.9.gain.kgain.refs_8_, ...), custom_call_target="tpu_custom_call" | custom-call | bytes 4500000 | tf_op jit(solution)/shard_map/pack_rows/pallas_call | solution.py:95
  8.8 1.7 %collective-permute-start = (bf16[10,2,2,80,128]{4,3,2,1,0:T(8,128)(2,1)S(1)}, bf16[10,2,2,80,128]{4,3,2,1,0:T(8,128)(2,1)S(1)}, u32[]{:S(2)}, u32[]{:S(2)}) collective-permute-start(bf16[10,2,2,80,128]{4,3,2,1,0:T(8,128)(2,1)S(1)} %get-tuple-element.58), channel_id=1, source_target_pairs={{0,2},{4,6},{8,10},{12,14},{16,18},{20,22},{24,26},{28,30},{2,0},{... | collective-permute-start | bytes 2457608 | tf_op jit(solution)/shard_map/ppermute | solution.py:536
  10.5 4.3 %collective-permute-start.1 = (bf16[10,2,2,80,128]{4,3,2,1,0:T(8,128)(2,1)S(1)}, bf16[10,2,2,80,128]{4,3,2,1,0:T(8,128)(2,1)S(1)}, u32[]{:S(2)}, u32[]{:S(2)}) collective-permute-start(bf16[10,2,2,80,128]{4,3,2,1,0:T(8,128)(2,1)S(1)} %get-tuple-element.59), channel_id=1, source_target_pairs={{2,4},{6,8},{10,12},{14,16},{18,20},{22,24},{26,28},{4,2},{8,6},{1... | collective-permute-start | bytes 2457608 | tf_op jit(solution)/shard_map/ppermute | solution.py:536
  14.9 0.1 broadcast_in_dim.21.inverse.refs_2_.refs_0_
  15.0 1.3 %pack_queries.2 = (bf16[10,240,128]{2,1,0:T(8,128)(2,1)S(1)}, bf16[10,240,128]{2,1,0:T(8,128)(2,1)S(1)}) custom-call(s32[20,3]{1,0:T(8,128)S(1)} %copy.12.window, bf16[2,3,80,2560]{3,2,1,0:T(8,128)(2,1)S(1)} %copy-done.1, f32[1,2560]{1,0:T(1,128)S(1)} %broadcast_in_dim.20.gain.refs_1_.refs_7_, f32[2,3,80,128]{3,2,1,0:T(8,128)S(1)} %broadcast_in_dim.21.inverse.refs_2_.refs_0_), custom_call_target="tpu_custom_call" | custom-call | bytes 3000000 | tf_op jit(solution)/shard_map/pack_queries/pallas_call | solution.py:76
  16.3 0.2 collective-permute-start.2
  16.5 5.6 %collective-permute-start.3 = (bf16[10,240,128]{2,1,0:T(8,128)(2,1)S(1)}, bf16[10,240,128]{2,1,0:T(8,128)(2,1)S(1)}, u32[]{:S(2)}, u32[]{:S(2)}) collective-permute-start(bf16[10,240,128]{2,1,0:T(8,128)(2,1)S(1)} %get-tuple-element.61), channel_id=1, source_target_pairs={{32,64},{96,128},{160,192},{64,32},{128,96},{192,160},{33,65},{97,... | collective-permute-start | bytes 1843208 | tf_op jit(solution)/shard_map/ppermute | solution.py:536
  22.2 1.4 %pack_rows.3 = (bf16[10,2,2,80,128]{4,3,2,1,0:T(8,128)(2,1)S(1)}, bf16[10,2,2,80,128]{4,3,2,1,0:T(8,128)(2,1)S(1)}) custom-call(s32[20,3]{1,0:T(8,128)S(1)} %copy.12.window, bf16[2,3,80,2560]{3,2,1,0:T(8,128)(2,1)S(1)} %copy-done, bf16[2,3,80,2560]{3,2,1,0:T(8,128)(2,1)S(1)} %copy-done.2, f32[1,2560]{1,0:T(1,128)S(1)} %broadcast_in_dim.9.gain.kgain.refs_8_, ...), custom_call_target="tpu_custom_call" | custom-call | bytes 4500000 | tf_op jit(solution)/shard_map/pack_rows/pallas_call | solution.py:95
  23.6 1.3 %pack_queries.3 = (bf16[10,240,128]{2,1,0:T(8,128)(2,1)S(1)}, bf16[10,240,128]{2,1,0:T(8,128)(2,1)S(1)}) custom-call(s32[20,3]{1,0:T(8,128)S(1)} %copy.12.window, bf16[2,3,80,2560]{3,2,1,0:T(8,128)(2,1)S(1)} %copy-done.1, f32[1,2560]{1,0:T(1,128)S(1)} %broadcast_in_dim.20.gain.refs_1_.refs_7_, f32[2,3,80,128]{3,2,1,0:T(8,128)S(1)} %broadcast_in_dim.21.inverse.refs_2_.refs_0_), custom_call_target="tpu_custom_call" | custom-call | bytes 3000000 | tf_op jit(solution)/shard_map/pack_queries/pallas_call | solution.py:76
  24.9 6.9 %collective-permute-done.2.refs_2_ = bf16[10,240,128]{2,1,0:T(8,128)(2,1)S(1)} collective-permute-done((bf16[10,240,128]{2,1,0:T(8,128)(2,1)S(1)}, bf16[10,240,128]{2,1,0:T(8,128)(2,1)S(1)}, u32[]{:S(2)}, u32[]{:S(2)}) %collective-permute-start.2) | collective-permute-done | bytes 614432 | tf_op jit(solution)/shard_map/ppermute | solution.py:536
  31.8 3.7 %collective-permute-done.3.refs_3_ = bf16[10,240,128]{2,1,0:T(8,128)(2,1)S(1)} collective-permute-done((bf16[10,240,128]{2,1,0:T(8,128)(2,1)S(1)}, bf16[10,240,128]{2,1,0:T(8,128)(2,1)S(1)}, u32[]{:S(2)}, u32[]{:S(2)}) %collective-permute-start.3) | collective-permute-done | bytes 614432 | tf_op jit(solution)/shard_map/ppermute | solution.py:536
  35.5 0.4 collective-permute-start.4
  35.9 3.2 %collective-permute-start.5 = (bf16[10,2,2,80,128]{4,3,2,1,0:T(8,128)(2,1)S(1)}, bf16[10,2,2,80,128]{4,3,2,1,0:T(8,128)(2,1)S(1)}, u32[]{:S(2)}, u32[]{:S(2)}) collective-permute-start(bf16[10,2,2,80,128]{4,3,2,1,0:T(8,128)(2,1)S(1)} %get-tuple-element.63), channel_id=1, source_target_pairs={{2,4},{6,8},{10,12},{14,16},{18,20},{22,24},{26,28},{4,2},{8,6},{1... | collective-permute-start | bytes 2457608 | tf_op jit(solution)/shard_map/ppermute | solution.py:536
  39.2 6.0 %collective-permute-start.7 = (bf16[10,240,128]{2,1,0:T(8,128)(2,1)S(1)}, bf16[10,240,128]{2,1,0:T(8,128)(2,1)S(1)}, u32[]{:S(2)}, u32[]{:S(2)}) collective-permute-start(bf16[10,240,128]{2,1,0:T(8,128)(2,1)S(1)} %get-tuple-element.68), channel_id=1, source_target_pairs={{32,64},{96,128},{160,192},{64,32},{128,96},{192,160},{33,65},{97,... | collective-permute-start | bytes 1843208 | tf_op jit(solution)/shard_map/ppermute | solution.py:536
  45.3 10.5 %both_partial.1 = (bf16[10,2,3,80,128]{4,3,2,1,0:T(8,128)(2,1)S(1)}, bf16[11,240,128]{2,1,0:T(8,128)(2,1)}, bf16[11,240,128]{2,1,0:T(8,128)(2,1)}, f32[2,240,128]{2,1,0:T(8,128)S(1)}) custom-call(s32[20,3]{1,0:T(8,128)S(1)} %copy.12.window, f32[2,3,80,128]{3,2,1,0:T(8,128)S(1)} %broadcast_in_dim.21.inverse.refs_2_.refs_0_, ...), custom_call_target="tpu_custom_call" | custom-call | bytes 33000000 | tf_op jit(solution)/shard_map/both_partial/pallas_call | solution.py:450
  55.7 5.5 %collective-permute-start.11 = (bf16[11,240,128]{2,1,0:T(8,128)(2,1)}, bf16[11,240,128]{2,1,0:T(8,128)(2,1)}, u32[]{:S(2)}, u32[]{:S(2)}) collective-permute-start(bf16[11,240,128]{2,1,0:T(8,128)(2,1)} %get-tuple-element.78), channel_id=1, source_target_pairs={{32,64},{96,128},{160,192},{64,32},{128,96},{192,160},{33,65},{97,... | collective-permute-start | bytes 2027528 | tf_op jit(solution)/shard_map/ppermute | solution.py:536
  61.3 7.1 %far_partial.1 = (bf16[11,240,128]{2,1,0:T(8,128)(2,1)}, bf16[11,240,128]{2,1,0:T(8,128)(2,1)}) custom-call(s32[20,3]{1,0:T(8,128)S(1)} %copy.12.window, f32[2,3,80,128]{3,2,1,0:T(8,128)S(1)} %broadcast_in_dim.8.inverse.kinverse.refs_1_, bf16[2,3,80,2560]{3,2,1,0:T(8,128)(2,1)S(1)} %copy-done, bf16[2,3,80,2560]{3,2,1,0:T(8,128)(2,1)S(1)} %copy-done.3, ...), custom_call_target="tpu_custom_call" | custom-call | bytes 18000000 | tf_op jit(solution)/shard_map/far_partial/pallas_call | solution.py:336
  68.4 4.1 %collective-permute-start.9 = (bf16[11,240,128]{2,1,0:T(8,128)(2,1)}, bf16[11,240,128]{2,1,0:T(8,128)(2,1)}, u32[]{:S(2)}, u32[]{:S(2)}) collective-permute-start(bf16[11,240,128]{2,1,0:T(8,128)(2,1)} %get-tuple-element.70), channel_id=1, source_target_pairs={{32,64},{96,128},{160,192},{64,32},{128,96},{192,160},{33,65},{97,... | collective-permute-start | bytes 2027528 | tf_op jit(solution)/shard_map/ppermute | solution.py:536
  72.5 7.9 %own_partial.1 = (bf16[10,2,3,80,128]{4,3,2,1,0:T(8,128)(2,1)S(1)}, f32[2,240,128]{2,1,0:T(8,128)S(1)}) custom-call(s32[20,3]{1,0:T(8,128)S(1)} %copy.12.window, f32[2,3,80,128]{3,2,1,0:T(8,128)S(1)} %broadcast_in_dim.8.inverse.kinverse.refs_1_, bf16[2,3,80,2560]{3,2,1,0:T(8,128)(2,1)S(1)} %copy-done, bf16[2,3,80,2560]{3,2,1,0:T(8,128)(2,1)S(1)} %copy-done.3, ...), custom_call_target="tpu_custom_call" | custom-call | bytes 18000000 | tf_op jit(solution)/shard_map/own_partial/pallas_call | solution.py:336
  80.4 1.0 %copy-done.6 = bf16[10,2,3,80,128]{4,3,2,1,0:T(8,128)(2,1)} copy-done((bf16[10,2,3,80,128]{4,3,2,1,0:T(8,128)(2,1)}, bf16[10,2,3,80,128]{4,3,2,1,0:T(8,128)(2,1)S(1)}, u32[]{:S(2)}) %copy-start.6) | copy-done | bytes 1228824
  81.5 0.7 copy-done.8
  82.2 0.1 copy.16.window
  82.3 1.3 %copy-done.5 = bf16[10,2,3,80,128]{4,3,2,1,0:T(8,128)(2,1)S(1)} copy-done((bf16[10,2,3,80,128]{4,3,2,1,0:T(8,128)(2,1)S(1)}, bf16[10,2,3,80,128]{4,3,2,1,0:T(8,128)(2,1)}, u32[]{:S(2)}) %copy-start.5) | copy-done | bytes 1228824
  83.6 3.7 %merge.2.refs_0_ = bf16[2,3,80,2560]{3,2,1,0:T(8,128)(2,1)} custom-call(s32[20,3]{1,0:T(8,128)S(1)} %copy.16.window, bf16[10,2,3,80,128]{4,3,2,1,0:T(8,128)(2,1)S(1)} %copy-done.5, f32[2,240,128]{2,1,0:T(8,128)S(1)} %get-tuple-element.76.lse, bf16[11,240,128]{2,1,0:T(8,128)(2,1)S(1)} %collective-permute-done.10.ob.sb, ...), custom_call_target="tpu_custom_call" | custom-call | bytes 7500000 | tf_op jit(solution)/shard_map/merge/pallas_call | solution.py:507
  87.3 2.0 %collective-permute-done.9.oa.sa = bf16[11,240,128]{2,1,0:T(8,128)(2,1)} collective-permute-done((bf16[11,240,128]{2,1,0:T(8,128)(2,1)}, bf16[11,240,128]{2,1,0:T(8,128)(2,1)}, u32[]{:S(2)}, u32[]{:S(2)}) %collective-permute-start.9) | collective-permute-done | bytes 675872 | tf_op jit(solution)/shard_map/ppermute | solution.py:536
  89.3 3.8 %merge.3 = bf16[2,3,80,2560]{3,2,1,0:T(8,128)(2,1)} custom-call(s32[20,3]{1,0:T(8,128)S(1)} %copy.16.window, bf16[10,2,3,80,128]{4,3,2,1,0:T(8,128)(2,1)S(1)} %copy-done.7, f32[2,240,128]{2,1,0:T(8,128)S(1)} %copy-done.9, bf16[11,240,128]{2,1,0:T(8,128)(2,1)} %collective-permute-done.8.ob.sb, ...), custom_call_target="tpu_custom_call", output_to_operand_aliasing={{}: (7, {})} | custom-call | bytes 7500000 | tf_op jit(solution)/shard_map/merge/pallas_call | solution.py:507
  (37 shorter events, 0.2 us)
Async XLA Ops:
  0.0 2.4 %copy-start = (bf16[2,3,80,2560]{3,2,1,0:T(8,128)(2,1)S(1)}, bf16[2,3,80,2560]{3,2,1,0:T(8,128)(2,1)}, u32[]{:S(2)}) copy-start(bf16[2,3,80,2560]{3,2,1,0:T(8,128)(2,1)} %refs_5_) | copy-start | bytes 7372804
  0.0 3.0 %copy-start.10 = (f32[2560]{0:T(1024)S(1)}, f32[2560]{0:T(1024)}, u32[]{:S(2)}) copy-start(f32[2560]{0:T(1024)} %param.10) | copy-start | bytes 30724
  0.0 3.0 %copy-start.12 = (s32[20,3]{0,1:T(4,128)S(1)}, s32[20,3]{0,1:T(4,128)}, u32[]{:S(2)}) copy-start(s32[20,3]{0,1:T(4,128)} %param.11) | copy-start | bytes 724
  5.7 1.7 %copy-start.2 = (bf16[2,3,80,2560]{3,2,1,0:T(8,128)(2,1)S(1)}, bf16[2,3,80,2560]{3,2,1,0:T(8,128)(2,1)}, u32[]{:S(2)}) copy-start(bf16[2,3,80,2560]{3,2,1,0:T(8,128)(2,1)} %refs_6_.1) | copy-start | bytes 7372804
  7.4 7.4 %copy-start.11 = (f32[2560]{0:T(1024)S(1)}, f32[2560]{0:T(1024)}, u32[]{:S(2)}) copy-start(f32[2560]{0:T(1024)} %param.9) | copy-start | bytes 30724
  7.4 7.6 %copy-start.1 = (bf16[2,3,80,2560]{3,2,1,0:T(8,128)(2,1)S(1)}, bf16[2,3,80,2560]{3,2,1,0:T(8,128)(2,1)}, u32[]{:S(2)}) copy-start(bf16[2,3,80,2560]{3,2,1,0:T(8,128)(2,1)} %refs_4_) | copy-start | bytes 7372804
  8.8 26.7 %collective-permute-start = (bf16[10,2,2,80,128]{4,3,2,1,0:T(8,128)(2,1)S(1)}, bf16[10,2,2,80,128]{4,3,2,1,0:T(8,128)(2,1)S(1)}, u32[]{:S(2)}, u32[]{:S(2)}) collective-permute-start(bf16[10,2,2,80,128]{4,3,2,1,0:T(8,128)(2,1)S(1)} %get-tuple-element.58), channel_id=1, source_target_pairs={{0,2},{4,6},{8,10},{12,14},{16,18},{20,22},{24,26},{28,30},{2,0},{... | collective-permute-start | bytes 2457608 | tf_op jit(solution)/shard_map/ppermute | solution.py:536
  10.5 25.0 %collective-permute-start.1 = (bf16[10,2,2,80,128]{4,3,2,1,0:T(8,128)(2,1)S(1)}, bf16[10,2,2,80,128]{4,3,2,1,0:T(8,128)(2,1)S(1)}, u32[]{:S(2)}, u32[]{:S(2)}) collective-permute-start(bf16[10,2,2,80,128]{4,3,2,1,0:T(8,128)(2,1)S(1)} %get-tuple-element.59), channel_id=1, source_target_pairs={{2,4},{6,8},{10,12},{14,16},{18,20},{22,24},{26,28},{4,2},{8,6},{1... | collective-permute-start | bytes 2457608 | tf_op jit(solution)/shard_map/ppermute | solution.py:536
  16.3 15.5 %collective-permute-start.2 = (bf16[10,240,128]{2,1,0:T(8,128)(2,1)S(1)}, bf16[10,240,128]{2,1,0:T(8,128)(2,1)S(1)}, u32[]{:S(2)}, u32[]{:S(2)}) collective-permute-start(bf16[10,240,128]{2,1,0:T(8,128)(2,1)S(1)} %get-tuple-element.60), channel_id=1, source_target_pairs={{0,32},{64,96},{128,160},{192,224},{32,0},{96,64},{160,128},{224,1... | collective-permute-start | bytes 1843208 | tf_op jit(solution)/shard_map/ppermute | solution.py:536
  16.5 19.0 %collective-permute-start.3 = (bf16[10,240,128]{2,1,0:T(8,128)(2,1)S(1)}, bf16[10,240,128]{2,1,0:T(8,128)(2,1)S(1)}, u32[]{:S(2)}, u32[]{:S(2)}) collective-permute-start(bf16[10,240,128]{2,1,0:T(8,128)(2,1)S(1)} %get-tuple-element.61), channel_id=1, source_target_pairs={{32,64},{96,128},{160,192},{64,32},{128,96},{192,160},{33,65},{97,... | collective-permute-start | bytes 1843208 | tf_op jit(solution)/shard_map/ppermute | solution.py:536
  23.6 21.7 %copy-start.3 = (bf16[2,3,80,2560]{3,2,1,0:T(8,128)(2,1)S(1)}, bf16[2,3,80,2560]{3,2,1,0:T(8,128)(2,1)}, u32[]{:S(2)}) copy-start(bf16[2,3,80,2560]{3,2,1,0:T(8,128)(2,1)} %refs_6_.1) | copy-start | bytes 7372804
  35.5 25.8 %collective-permute-start.4 = (bf16[10,2,2,80,128]{4,3,2,1,0:T(8,128)(2,1)S(1)}, bf16[10,2,2,80,128]{4,3,2,1,0:T(8,128)(2,1)S(1)}, u32[]{:S(2)}, u32[]{:S(2)}) collective-permute-start(bf16[10,2,2,80,128]{4,3,2,1,0:T(8,128)(2,1)S(1)} %get-tuple-element.62), channel_id=1, source_target_pairs={{0,2},{4,6},{8,10},{12,14},{16,18},{20,22},{24,26},{28,30},{2,0},{... | collective-permute-start | bytes 2457608 | tf_op jit(solution)/shard_map/ppermute | solution.py:536
  35.9 25.3 %collective-permute-start.5 = (bf16[10,2,2,80,128]{4,3,2,1,0:T(8,128)(2,1)S(1)}, bf16[10,2,2,80,128]{4,3,2,1,0:T(8,128)(2,1)S(1)}, u32[]{:S(2)}, u32[]{:S(2)}) collective-permute-start(bf16[10,2,2,80,128]{4,3,2,1,0:T(8,128)(2,1)S(1)} %get-tuple-element.63), channel_id=1, source_target_pairs={{2,4},{6,8},{10,12},{14,16},{18,20},{22,24},{26,28},{4,2},{8,6},{1... | collective-permute-start | bytes 2457608 | tf_op jit(solution)/shard_map/ppermute | solution.py:536
  39.1 16.6 %collective-permute-start.6 = (bf16[10,240,128]{2,1,0:T(8,128)(2,1)S(1)}, bf16[10,240,128]{2,1,0:T(8,128)(2,1)S(1)}, u32[]{:S(2)}, u32[]{:S(2)}) collective-permute-start(bf16[10,240,128]{2,1,0:T(8,128)(2,1)S(1)} %get-tuple-element.67), channel_id=1, source_target_pairs={{0,32},{64,96},{128,160},{192,224},{32,0},{96,64},{160,128},{224,1... | collective-permute-start | bytes 1843208 | tf_op jit(solution)/shard_map/ppermute | solution.py:536
  39.2 22.0 %collective-permute-start.7 = (bf16[10,240,128]{2,1,0:T(8,128)(2,1)S(1)}, bf16[10,240,128]{2,1,0:T(8,128)(2,1)S(1)}, u32[]{:S(2)}, u32[]{:S(2)}) collective-permute-start(bf16[10,240,128]{2,1,0:T(8,128)(2,1)S(1)} %get-tuple-element.68), channel_id=1, source_target_pairs={{32,64},{96,128},{160,192},{64,32},{128,96},{192,160},{33,65},{97,... | collective-permute-start | bytes 1843208 | tf_op jit(solution)/shard_map/ppermute | solution.py:536
  55.7 12.7 %copy-start.4 = (bf16[10,2,3,80,128]{4,3,2,1,0:T(8,128)(2,1)}, bf16[10,2,3,80,128]{4,3,2,1,0:T(8,128)(2,1)S(1)}, u32[]{:S(2)}) copy-start(bf16[10,2,3,80,128]{4,3,2,1,0:T(8,128)(2,1)S(1)} %get-tuple-element.75.part) | copy-start | bytes 3686404
  55.7 26.5 %collective-permute-start.10 = (bf16[11,240,128]{2,1,0:T(8,128)(2,1)}, bf16[11,240,128]{2,1,0:T(8,128)(2,1)S(1)}, u32[]{:S(2)}, u32[]{:S(2)}) collective-permute-start(bf16[11,240,128]{2,1,0:T(8,128)(2,1)} %get-tuple-element.77), channel_id=1, source_target_pairs={{0,32},{64,96},{128,160},{192,224},{32,0},{96,64},{160,128},{224,1... | collective-permute-start | bytes 2027528 | tf_op jit(solution)/shard_map/ppermute | solution.py:536
  55.7 26.5 %collective-permute-start.11 = (bf16[11,240,128]{2,1,0:T(8,128)(2,1)}, bf16[11,240,128]{2,1,0:T(8,128)(2,1)}, u32[]{:S(2)}, u32[]{:S(2)}) collective-permute-start(bf16[11,240,128]{2,1,0:T(8,128)(2,1)} %get-tuple-element.78), channel_id=1, source_target_pairs={{32,64},{96,128},{160,192},{64,32},{128,96},{192,160},{33,65},{97,... | collective-permute-start | bytes 2027528 | tf_op jit(solution)/shard_map/ppermute | solution.py:536
  68.4 18.9 %collective-permute-start.8 = (bf16[11,240,128]{2,1,0:T(8,128)(2,1)}, bf16[11,240,128]{2,1,0:T(8,128)(2,1)}, u32[]{:S(2)}, u32[]{:S(2)}) collective-permute-start(bf16[11,240,128]{2,1,0:T(8,128)(2,1)} %get-tuple-element.69), channel_id=1, source_target_pairs={{0,32},{64,96},{128,160},{192,224},{32,0},{96,64},{160,128},{224,1... | collective-permute-start | bytes 2027528 | tf_op jit(solution)/shard_map/ppermute | solution.py:536
  68.4 20.9 %collective-permute-start.9 = (bf16[11,240,128]{2,1,0:T(8,128)(2,1)}, bf16[11,240,128]{2,1,0:T(8,128)(2,1)}, u32[]{:S(2)}, u32[]{:S(2)}) collective-permute-start(bf16[11,240,128]{2,1,0:T(8,128)(2,1)} %get-tuple-element.70), channel_id=1, source_target_pairs={{32,64},{96,128},{160,192},{64,32},{128,96},{192,160},{33,65},{97,... | collective-permute-start | bytes 2027528 | tf_op jit(solution)/shard_map/ppermute | solution.py:536
  80.4 1.1 %copy-start.6 = (bf16[10,2,3,80,128]{4,3,2,1,0:T(8,128)(2,1)}, bf16[10,2,3,80,128]{4,3,2,1,0:T(8,128)(2,1)S(1)}, u32[]{:S(2)}) copy-start(bf16[10,2,3,80,128]{4,3,2,1,0:T(8,128)(2,1)S(1)} %get-tuple-element.64.part) | copy-start | bytes 3686404
  81.5 0.7 copy-start.8
  82.3 1.3 %copy-start.5 = (bf16[10,2,3,80,128]{4,3,2,1,0:T(8,128)(2,1)S(1)}, bf16[10,2,3,80,128]{4,3,2,1,0:T(8,128)(2,1)}, u32[]{:S(2)}) copy-start(bf16[10,2,3,80,128]{4,3,2,1,0:T(8,128)(2,1)} %copy-done.4) | copy-start | bytes 3686404
  83.5 5.7 %copy-start.7 = (bf16[10,2,3,80,128]{4,3,2,1,0:T(8,128)(2,1)S(1)}, bf16[10,2,3,80,128]{4,3,2,1,0:T(8,128)(2,1)}, u32[]{:S(2)}) copy-start(bf16[10,2,3,80,128]{4,3,2,1,0:T(8,128)(2,1)} %copy-done.6) | copy-start | bytes 3686404
  83.6 5.7 %copy-start.9 = (f32[2,240,128]{2,1,0:T(8,128)S(1)}, f32[2,240,128]{2,1,0:T(8,128)}, u32[]{:S(2)}) copy-start(f32[2,240,128]{2,1,0:T(8,128)} %copy-done.8) | copy-start | bytes 737284

commit v6 on v4

--- a/solution.py
+++ b/solution.py
@@ -12,6 +12,7 @@
 W = 80
 NH = 20
 FIRST = 10
+PIECE = 10
 EPS = 1e-06
 NEG = -1e30
 FAR = 100
@@ -194,12 +195,22 @@
     return st[0] * SCALE2 + jnp.log(st[1]) * LOG2E
 
 
-def pieces_of(full, lane):
+def pieces_of(full):
+    lane = lax.broadcasted_iota(jnp.int32, (3 * W, HD), 1)
     high = full.astype(BF16).astype(F32)
     rest = full - high
     middle = rest.astype(BF16).astype(F32)
-    low = rest - middle
-    return jnp.where(lane < 32, high, jnp.where(lane < 64, middle, jnp.where(lane < 96, low, 0.0))).astype(BF16)
+    within = lane & 31
+    pieces = jnp.where(within < PIECE, high, jnp.where(within < 2 * PIECE, middle, rest - middle))
+    lane = lane[:W]
+    folded = jnp.where(lane < 32, pieces[:W], jnp.where(lane < 64, pieces[W : 2 * W], pieces[2 * W :]))
+    return folded.astype(BF16)
+
+
+def joined(pieces):
+    lines = pieces.astype(F32)
+    lines = jnp.concatenate([lines, pltpu.roll(lines, HD - 32, 1), pltpu.roll(lines, HD - 64, 1)], axis=0)
+    return lines + pltpu.roll(lines, HD - PIECE, 1) + pltpu.roll(lines, HD - 2 * PIECE, 1)
 
 
 def partial_kernel(far, start, group, steps, window, kinverse, k, v, kgain, low, high, *refs):
@@ -235,8 +246,7 @@
 
         @pl.when(step == steps)
         def _():
-            lane = lax.broadcasted_iota(jnp.int32, (3 * W, HD), 1)
-            below, above = (pieces_of(lse_of(st[j]), lane) for j in range(2))
+            below, above = (pieces_of(lse_of(st[j])) for j in range(2))
             ob[0], oa[0] = sides("frame", below, above)
 
     else:
@@ -248,7 +258,9 @@
 
 
 def marked_lanes(step, group, g):
-    return (lax.broadcasted_iota(jnp.int32, (W, HD), 1) & 31) == step * group + g
+    within = lax.broadcasted_iota(jnp.int32, (W, HD), 1) & 31
+    slot = step * group + g
+    return (within == slot) | (within == slot + PIECE) | (within == slot + 2 * PIECE)
 
 
 def far_step(start, group, step, window, qb, qa, ob, oa, kxs, vxs, gaps, st):
@@ -270,7 +282,7 @@
             ]
             for j in range(2):
                 mark(st.at[j], at, here, tops[n + j], mixed[j])
-            ob[g, at], oa[g, at] = sides("frame", divided(mixed[0]), divided(mixed[1]))
+            ob[3 * g + i], oa[3 * g + i] = sides("frame", divided(mixed[0]), divided(mixed[1]))
 
 
 def own_step(start, group, step, window, q, qgain, qinverse, part, kxs, vxs, gaps, st):
@@ -320,9 +332,9 @@
     norms = whole((2, 3, W, HD))
     if far:
         q_spec = pl.BlockSpec((group, 3 * W, HD), lambda s, window: (step_of(s), 0, 0))
-        o_spec = pl.BlockSpec((group, 3 * W, HD), lambda s, window: (s, 0, 0))
+        o_spec = pl.BlockSpec((3 * group, W, HD), lambda s, window: (s, 0, 0))
         asked_specs, out_specs = [q_spec] * 2, [o_spec] * 2
-        out_shape = [jax.ShapeDtypeStruct((count + 1, 3 * W, HD), BF16)] * 2
+        out_shape = [jax.ShapeDtypeStruct((3 * count + 1, W, HD), BF16)] * 2
     else:
         asked_specs = [heads, gains, norms]
         out_specs = [
@@ -369,10 +381,9 @@
 
     @pl.when(step == steps)
     def _():
-        lane = lax.broadcasted_iota(jnp.int32, (3 * W, HD), 1)
         for j in range(2):
             own_stats[j] = lse_of(st_own[j])
-        below, above = (pieces_of(lse_of(st_far[j]), lane) for j in range(2))
+        below, above = (pieces_of(lse_of(st_far[j])) for j in range(2))
         ob[0], oa[0] = sides("frame", below, above)
 
 
@@ -415,9 +426,8 @@
         for s, last in ((s0, below), (s1, above)):
             parts = [weights_of(a, b) for a, b in zip(s, (first, second, last))]
             weights.append(jnp.concatenate(parts, axis=0))
-    lane = lax.broadcasted_iota(jnp.int32, (W, HD), 1)
-    for g in range(group):
-        here = (lane & 31) == step * group + g
+    for g in range(group):
+        here = marked_lanes(step, group, g)
         for i in range(3):
             w0, w1 = weights[6 * g + 2 * i : 6 * g + 2 * i + 2]
             top, top_b, top_a = tops[3 * g + i]
@@ -430,7 +440,7 @@
                 mark(st_own.at[n], at, here, top[W * n : W * (n + 1)], own)
             for n, far in ((0, m0[2 * W :]), (1, m1[2 * W :])):
                 mark(st_far.at[n], at, here, (top_b, top_a)[n], far)
-            ob[g, at], oa[g, at] = sides("frame", divided(m0[2 * W :]), divided(m1[2 * W :]))
+            ob[3 * g + i], oa[3 * g + i] = sides("frame", divided(m0[2 * W :]), divided(m1[2 * W :]))
 
 
 def both_partial(window, qb, qa, q, k, v, qgain, kgain, qinverse, kinverse, low, high, start, count):
@@ -444,8 +454,8 @@
     gains = pl.BlockSpec((1, group * HD), lambda s, window: (0, start // group + step_of(s)))
     rows = pl.BlockSpec((group, 2, 2, W, HD), lambda s, window: (step_of(s), 0, 0, 0, 0))
     q_spec = pl.BlockSpec((group, 3 * W, HD), lambda s, window: (step_of(s), 0, 0))
-    o_spec = pl.BlockSpec((group, 3 * W, HD), lambda s, window: (s, 0, 0))
-    out = jax.ShapeDtypeStruct((count + 1, 3 * W, HD), BF16)
+    o_spec = pl.BlockSpec((3 * group, W, HD), lambda s, window: (s, 0, 0))
+    out = jax.ShapeDtypeStruct((3 * count + 1, W, HD), BF16)
     stat = pltpu.VMEM((2, 2, 3 * W, HD), F32)
     return pl.pallas_call(
         functools.partial(both_kernel, start, group, steps),
@@ -482,9 +492,7 @@
     @pl.when(step == 0)
     def _():
         for j, st in enumerate(sides("frame", sb[0], sa[0])):
-            pieces = st.astype(F32)
-            other = pieces + pltpu.roll(pieces, HD - 32, 1) + pltpu.roll(pieces, HD - 64, 1)
-            other = jnp.where(neighbours[j], other, NEG)
+            other = jnp.where(neighbours[j], joined(st), NEG)
             top = jnp.maximum(lse[j], other)
             own_weight = jnp.exp2(lse[j] - top)
             other_weight = jnp.exp2(other - top)
@@ -492,18 +500,18 @@
 
     for g in range(group):
         here = lane == step * group + g
-        for j, far in enumerate(sides("frame", ob[g], oa[g])):
+        for j, far in enumerate(sides("frame", ob[3 * g : 3 * g + 3], oa[3 * g : 3 * g + 3])):
             share = jnp.sum(jnp.where(here, shares[j], 0.0), axis=1, keepdims=True)
             share = jnp.where(window[start + step * group + g, 0] > 0, share, 0.0)
             own = part[g, j].reshape(3 * W, HD).astype(F32)
-            mixed = own + (far.astype(F32) - own) * share
+            mixed = own + (far.reshape(3 * W, HD).astype(F32) - own) * share
             out[j, :, :, lanes(g)] = mixed.astype(BF16).reshape(3, W, HD)
 
 
 def merge(window, out, part, lse, o_below, o_above, start, count):
     group = group_of(start, count)
-    o_spec = pl.BlockSpec((group, 3 * W, HD), lambda s, window: (s, 0, 0))
-    stat_spec = pl.BlockSpec((1, 3 * W, HD), lambda s, window: (count, 0, 0))
+    o_spec = pl.BlockSpec((3 * group, W, HD), lambda s, window: (s, 0, 0))
+    stat_spec = pl.BlockSpec((1, W, HD), lambda s, window: (3 * count, 0, 0))
     return pl.pallas_call(
         functools.partial(merge_kernel, start, group),
         grid_spec=pltpu.PrefetchScalarGridSpec(

time: 91.4 us -> 89.9 us (0.984)
  waiting for transfers between devices: 10.2 us -> 9.06 us
    ppermute x12, waiting for transfers between devices: 10.2 us -> 9.06 us  [exchange(): out.append(lax.ppermute(block, axis, pairs + [(b, a) for a, b in pairs]))]
where the time goes in v6:
time: 89.9 us; the launch traced here: 89.6 us
  Pallas kernels  36.1 us (40%)
  starting transfers between devices  34.2 us (38%)
  waiting for transfers between devices  9.06 us (10%)
  local copies, waits for them, and re-layouts  3.76 us (4%)
  other arithmetic  3.53 us (4%)
  blocking collectives  2.63 us (3%)
    ppermute x12, starting transfers between devices, exchange(): out.append(lax.ppermute(block, axis, pairs + [(b, a) for a, b in pairs]))  34.2 us
    pallas_call x2, Pallas kernels, partial_call(): pl.pallas_call(functools.partial(partial_kernel, far, start, group, steps...  14.7 us
    pallas_call x1, Pallas kernels, both_partial(): pl.pallas_call(functools.partial(both_kernel, start, group, steps), grid_...  10.3 us
    ppermute x12, waiting for transfers between devices, exchange(): out.append(lax.ppermute(block, axis, pairs + [(b, a) for a, b in pairs]))  9.06 us
    pallas_call x2, Pallas kernels, merge(): pl.pallas_call(functools.partial(merge_kernel, start, group), grid_spec=p...  5.68 us
    reduce_sum x1, other arithmetic, squares_of(): return jnp.sum(values * values, axis=-1)  3.52 us
    unnamed x17, local copies, waits for them, and re-layouts  3.51 us
    pallas_call x2, Pallas kernels, pack_rows(): pl.pallas_call(functools.partial(pack_rows_kernel, group), grid_spec=pltp...  2.79 us
  transfers between devices with their start and end apart: 12, of which 3 were waited for; matrix products, arithmetic and copies ran while one was open for 0% of the time, Pallas kernels for 34%

profile of v6, /device:TPU:38, one launch (start us, length us, event | category | flops | bytes accessed | tf_op | source)
XLA Modules:
  0.0 89.6 jit_solution(7646691034089314935)
XLA Ops:
  0.0 3.5 %multiply_reduce_fusion = (f32[2,3,80]{2,1,0:T(4,128)S(1)}, f32[2,3,80]{2,1,0:T(4,128)S(1)}) fusion(bf16[2,3,80,2560]{3,2,1,0:T(8,128)(2,1)} %refs_4_, bf16[2,3,80,2560]{3,2,1,0:T(8,128)(2,1)} %refs_5_), kind=kLoop, calls=%fused_computation | loop fusion | flops 7371840 | bytes 4919040 | tf_op jit(solution)/shard_map/reduce_sum | solution.py:573
  3.5 2.6 %all-reduce = (f32[2,3,80]{2,1,0:T(4,128)S(1)}, f32[2,3,80]{2,1,0:T(4,128)S(1)}) all-reduce(f32[2,3,80]{2,1,0:T(4,128)S(1)} %get-tuple-element.56, f32[2,3,80]{2,1,0:T(4,128)S(1)} %get-tuple-element.55), channel_id=1, replica_groups=mesh['frame'=8,'height'=16,'head'=2] {'head'}, use_global_device_ids=true, to_apply=%region_1.0 | all-reduce | flops 960 | bytes 7680 | tf_op jit(solution)/shard_map/psum | solution.py:578
  6.3 0.1 copy.16.window
  6.4 0.1 broadcast_in_dim.20.inverse.refs_2_.refs_0_
  6.5 0.0 copy-start.1
  6.5 1.7 %copy-done.1 = bf16[2,3,80,2560]{3,2,1,0:T(8,128)(2,1)S(1)} copy-done((bf16[2,3,80,2560]{3,2,1,0:T(8,128)(2,1)S(1)}, bf16[2,3,80,2560]{3,2,1,0:T(8,128)(2,1)}, u32[]{:S(2)}) %copy-start.1) | copy-done | bytes 2457624
  8.2 1.3 %pack_queries.2 = (bf16[10,240,128]{2,1,0:T(8,128)(2,1)S(1)}, bf16[10,240,128]{2,1,0:T(8,128)(2,1)S(1)}) custom-call(s32[20,3]{1,0:T(8,128)S(1)} %copy.16.window, bf16[2,3,80,2560]{3,2,1,0:T(8,128)(2,1)S(1)} %copy-done.1, f32[1,2560]{1,0:T(1,128)S(1)} %broadcast_in_dim.9.gain.refs_1_.refs_7_, f32[2,3,80,128]{3,2,1,0:T(8,128)S(1)} %broadcast_in_dim.20.inverse.refs_2_.refs_0_), custom_call_target="tpu_custom_call" | custom-call | bytes 3000000 | tf_op jit(solution)/shard_map/pack_queries/pallas_call | solution.py:77
  9.5 0.1 broadcast_in_dim.8.inverse.kinverse.refs_1_
  9.6 1.7 %copy-done.3 = bf16[2,3,80,2560]{3,2,1,0:T(8,128)(2,1)S(1)} copy-done((bf16[2,3,80,2560]{3,2,1,0:T(8,128)(2,1)S(1)}, bf16[2,3,80,2560]{3,2,1,0:T(8,128)(2,1)}, u32[]{:S(2)}) %copy-start.3) | copy-done | bytes 2457624
  11.3 1.4 %pack_rows.2 = (bf16[10,2,2,80,128]{4,3,2,1,0:T(8,128)(2,1)S(1)}, bf16[10,2,2,80,128]{4,3,2,1,0:T(8,128)(2,1)S(1)}) custom-call(s32[20,3]{1,0:T(8,128)S(1)} %copy.16.window, bf16[2,3,80,2560]{3,2,1,0:T(8,128)(2,1)S(1)} %copy-done, bf16[2,3,80,2560]{3,2,1,0:T(8,128)(2,1)S(1)} %copy-done.3, f32[1,2560]{1,0:T(1,128)S(1)} %broadcast_in_dim.21.gain.kgain.refs_8_, ...), custom_call_target="tpu_custom_call" | custom-call | bytes 4500000 | tf_op jit(solution)/shard_map/pack_rows/pallas_call | solution.py:96
  12.7 1.7 %collective-permute-start.8 = (bf16[10,2,2,80,128]{4,3,2,1,0:T(8,128)(2,1)S(1)}, bf16[10,2,2,80,128]{4,3,2,1,0:T(8,128)(2,1)S(1)}, u32[]{:S(2)}, u32[]{:S(2)}) collective-permute-start(bf16[10,2,2,80,128]{4,3,2,1,0:T(8,128)(2,1)S(1)} %get-tuple-element.32), channel_id=1, source_target_pairs={{0,2},{4,6},{8,10},{12,14},{16,18},{20,22},{24,26},{28,30},{2,0},{... | collective-permute-start | bytes 2457608 | tf_op jit(solution)/shard_map/ppermute | solution.py:544
  14.4 0.1 collective-permute-start.6
  14.5 5.6 %collective-permute-start.7 = (bf16[10,240,128]{2,1,0:T(8,128)(2,1)S(1)}, bf16[10,240,128]{2,1,0:T(8,128)(2,1)S(1)}, u32[]{:S(2)}, u32[]{:S(2)}) collective-permute-start(bf16[10,240,128]{2,1,0:T(8,128)(2,1)S(1)} %get-tuple-element.48), channel_id=1, source_target_pairs={{32,64},{96,128},{160,192},{64,32},{128,96},{192,160},{33,65},{97,... | collective-permute-start | bytes 1843208 | tf_op jit(solution)/shard_map/ppermute | solution.py:544
  20.1 4.4 %collective-permute-start.9 = (bf16[10,2,2,80,128]{4,3,2,1,0:T(8,128)(2,1)S(1)}, bf16[10,2,2,80,128]{4,3,2,1,0:T(8,128)(2,1)S(1)}, u32[]{:S(2)}, u32[]{:S(2)}) collective-permute-start(bf16[10,2,2,80,128]{4,3,2,1,0:T(8,128)(2,1)S(1)} %get-tuple-element.33), channel_id=1, source_target_pairs={{2,4},{6,8},{10,12},{14,16},{18,20},{22,24},{26,28},{4,2},{8,6},{1... | collective-permute-start | bytes 2457608 | tf_op jit(solution)/shard_map/ppermute | solution.py:544
  24.5 1.3 %pack_queries.3 = (bf16[10,240,128]{2,1,0:T(8,128)(2,1)S(1)}, bf16[10,240,128]{2,1,0:T(8,128)(2,1)S(1)}) custom-call(s32[20,3]{1,0:T(8,128)S(1)} %copy.16.window, bf16[2,3,80,2560]{3,2,1,0:T(8,128)(2,1)S(1)} %copy-done.1, f32[1,2560]{1,0:T(1,128)S(1)} %broadcast_in_dim.9.gain.refs_1_.refs_7_, f32[2,3,80,128]{3,2,1,0:T(8,128)S(1)} %broadcast_in_dim.20.inverse.refs_2_.refs_0_), custom_call_target="tpu_custom_call" | custom-call | bytes 3000000 | tf_op jit(solution)/shard_map/pack_queries/pallas_call | solution.py:77
  25.8 1.4 %pack_rows.3 = (bf16[10,2,2,80,128]{4,3,2,1,0:T(8,128)(2,1)S(1)}, bf16[10,2,2,80,128]{4,3,2,1,0:T(8,128)(2,1)S(1)}) custom-call(s32[20,3]{1,0:T(8,128)S(1)} %copy.16.window, bf16[2,3,80,2560]{3,2,1,0:T(8,128)(2,1)S(1)} %copy-done, bf16[2,3,80,2560]{3,2,1,0:T(8,128)(2,1)S(1)} %copy-done.4, f32[1,2560]{1,0:T(1,128)S(1)} %broadcast_in_dim.21.gain.kgain.refs_8_, ...), custom_call_target="tpu_custom_call" | custom-call | bytes 4500000 | tf_op jit(solution)/shard_map/pack_rows/pallas_call | solution.py:96
  27.3 0.5 collective-permute-start
  27.8 2.3 %collective-permute-done.6.refs_2_ = bf16[10,240,128]{2,1,0:T(8,128)(2,1)S(1)} collective-permute-done((bf16[10,240,128]{2,1,0:T(8,128)(2,1)S(1)}, bf16[10,240,128]{2,1,0:T(8,128)(2,1)S(1)}, u32[]{:S(2)}, u32[]{:S(2)}) %collective-permute-start.6) | collective-permute-done | bytes 614432 | tf_op jit(solution)/shard_map/ppermute | solution.py:544
  30.0 4.3 %collective-permute-start.1 = (bf16[10,2,2,80,128]{4,3,2,1,0:T(8,128)(2,1)S(1)}, bf16[10,2,2,80,128]{4,3,2,1,0:T(8,128)(2,1)S(1)}, u32[]{:S(2)}, u32[]{:S(2)}) collective-permute-start(bf16[10,2,2,80,128]{4,3,2,1,0:T(8,128)(2,1)S(1)} %get-tuple-element.39), channel_id=1, source_target_pairs={{2,4},{6,8},{10,12},{14,16},{18,20},{22,24},{26,28},{4,2},{8,6},{1... | collective-permute-start | bytes 2457608 | tf_op jit(solution)/shard_map/ppermute | solution.py:544
  34.4 0.4 collective-permute-start.2
  34.8 5.4 %collective-permute-start.3 = (bf16[10,240,128]{2,1,0:T(8,128)(2,1)S(1)}, bf16[10,240,128]{2,1,0:T(8,128)(2,1)S(1)}, u32[]{:S(2)}, u32[]{:S(2)}) collective-permute-start(bf16[10,240,128]{2,1,0:T(8,128)(2,1)S(1)} %get-tuple-element.44), channel_id=1, source_target_pairs={{32,64},{96,128},{160,192},{64,32},{128,96},{192,160},{33,65},{97,... | collective-permute-start | bytes 1843208 | tf_op jit(solution)/shard_map/ppermute | solution.py:544
  40.2 5.1 %collective-permute-done.9.refs_10_ = bf16[10,2,2,80,128]{4,3,2,1,0:T(8,128)(2,1)S(1)} collective-permute-done((bf16[10,2,2,80,128]{4,3,2,1,0:T(8,128)(2,1)S(1)}, bf16[10,2,2,80,128]{4,3,2,1,0:T(8,128)(2,1)S(1)}, u32[]{:S(2)}, u32[]{:S(2)}) %collective-permute-start.9) | collective-permute-done | bytes 819232 | tf_op jit(solution)/shard_map/ppermute | solution.py:544
  45.3 10.3 %both_partial.1 = (bf16[10,2,3,80,128]{4,3,2,1,0:T(8,128)(2,1)S(1)}, bf16[31,80,128]{2,1,0:T(8,128)(2,1)S(1)}, bf16[31,80,128]{2,1,0:T(8,128)(2,1)S(1)}, f32[2,240,128]{2,1,0:T(8,128)S(1)}) custom-call(s32[20,3]{1,0:T(8,128)S(1)} %copy.16.window, f32[2,3,80,128]{3,2,1,0:T(8,128)S(1)} %broadcast_in_dim.20.inverse.refs_2_.refs_0_, ...), custom_call_target="tpu_custom_call" | custom-call | bytes 33000000 | tf_op jit(solution)/shard_map/both_partial/pallas_call | solution.py:460
  55.6 0.1 collective-permute-start.10
  55.7 6.0 %collective-permute-start.11 = (bf16[31,80,128]{2,1,0:T(8,128)(2,1)S(1)}, bf16[31,80,128]{2,1,0:T(8,128)(2,1)S(1)}, u32[]{:S(2)}, u32[]{:S(2)}) collective-permute-start(bf16[31,80,128]{2,1,0:T(8,128)(2,1)S(1)} %get-tuple-element.52), channel_id=1, source_target_pairs={{32,64},{96,128},{160,192},{64,32},{128,96},{192,160},{33,65},{97,... | collective-permute-start | bytes 1904648 | tf_op jit(solution)/shard_map/ppermute | solution.py:544
  61.8 6.9 %far_partial.1 = (bf16[31,80,128]{2,1,0:T(8,128)(2,1)S(1)}, bf16[31,80,128]{2,1,0:T(8,128)(2,1)S(1)}) custom-call(s32[20,3]{1,0:T(8,128)S(1)} %copy.16.window, f32[2,3,80,128]{3,2,1,0:T(8,128)S(1)} %broadcast_in_dim.8.inverse.kinverse.refs_1_, bf16[2,3,80,2560]{3,2,1,0:T(8,128)(2,1)S(1)} %copy-done, bf16[2,3,80,2560]{3,2,1,0:T(8,128)(2,1)S(1)} %copy-done.4, ...), custom_call_target="tpu_custom_call" | custom-call | bytes 18000000 | tf_op jit(solution)/shard_map/far_partial/pallas_call | solution.py:348
  68.7 0.1 collective-permute-start.4
  68.8 5.6 %collective-permute-start.5 = (bf16[31,80,128]{2,1,0:T(8,128)(2,1)S(1)}, bf16[31,80,128]{2,1,0:T(8,128)(2,1)S(1)}, u32[]{:S(2)}, u32[]{:S(2)}) collective-permute-start(bf16[31,80,128]{2,1,0:T(8,128)(2,1)S(1)} %get-tuple-element.46), channel_id=1, source_target_pairs={{32,64},{96,128},{160,192},{64,32},{128,96},{192,160},{33,65},{97,... | collective-permute-start | bytes 1904648 | tf_op jit(solution)/shard_map/ppermute | solution.py:544
  74.4 7.9 %own_partial.1 = (bf16[10,2,3,80,128]{4,3,2,1,0:T(8,128)(2,1)S(1)}, f32[2,240,128]{2,1,0:T(8,128)S(1)}) custom-call(s32[20,3]{1,0:T(8,128)S(1)} %copy.16.window, f32[2,3,80,128]{3,2,1,0:T(8,128)S(1)} %broadcast_in_dim.8.inverse.kinverse.refs_1_, bf16[2,3,80,2560]{3,2,1,0:T(8,128)(2,1)S(1)} %copy-done, bf16[2,3,80,2560]{3,2,1,0:T(8,128)(2,1)S(1)} %copy-done.4, ...), custom_call_target="tpu_custom_call" | custom-call | bytes 18000000 | tf_op jit(solution)/shard_map/own_partial/pallas_call | solution.py:348
  82.3 2.8 %merge.2.refs_0_ = bf16[2,3,80,2560]{3,2,1,0:T(8,128)(2,1)} custom-call(s32[20,3]{1,0:T(8,128)S(1)} %copy.16.window, bf16[10,2,3,80,128]{4,3,2,1,0:T(8,128)(2,1)S(1)} %get-tuple-element.49.part, f32[2,240,128]{2,1,0:T(8,128)S(1)} %get-tuple-element.50.lse, bf16[31,80,128]{2,1,0:T(8,128)(2,1)S(1)} %collective-permute-done.10.ob.sb, ...), custom_call_target="tpu_custom_call" | custom-call | bytes 7500000 | tf_op jit(solution)/shard_map/merge/pallas_call | solution.py:515
  85.1 1.7 %collective-permute-done.5.oa.sa = bf16[31,80,128]{2,1,0:T(8,128)(2,1)S(1)} collective-permute-done((bf16[31,80,128]{2,1,0:T(8,128)(2,1)S(1)}, bf16[31,80,128]{2,1,0:T(8,128)(2,1)S(1)}, u32[]{:S(2)}, u32[]{:S(2)}) %collective-permute-start.5) | collective-permute-done | bytes 634912 | tf_op jit(solution)/shard_map/ppermute | solution.py:544
  86.8 2.9 %merge.3 = bf16[2,3,80,2560]{3,2,1,0:T(8,128)(2,1)} custom-call(s32[20,3]{1,0:T(8,128)S(1)} %copy.16.window, bf16[10,2,3,80,128]{4,3,2,1,0:T(8,128)(2,1)S(1)} %get-tuple-element.41.part, f32[2,240,128]{2,1,0:T(8,128)S(1)} %get-tuple-element.42.lse, bf16[31,80,128]{2,1,0:T(8,128)(2,1)S(1)} %collective-permute-done.4.ob.sb, ...), custom_call_target="tpu_custom_call", output_to_operand_aliasing={{}: (7, {})} | custom-call | bytes 7500000 | tf_op jit(solution)/shard_map/merge/pallas_call | solution.py:515
  (26 shorter events, 0.1 us)
Async XLA Ops:
  0.0 6.2 %copy-start.5 = (f32[2560]{0:T(1024)S(1)}, f32[2560]{0:T(1024)}, u32[]{:S(2)}) copy-start(f32[2560]{0:T(1024)} %param.10) | copy-start | bytes 30724
  0.0 6.2 %copy-start.6 = (f32[2560]{0:T(1024)S(1)}, f32[2560]{0:T(1024)}, u32[]{:S(2)}) copy-start(f32[2560]{0:T(1024)} %param.9) | copy-start | bytes 30724
  0.0 6.2 %copy-start.7 = (s32[20,3]{0,1:T(4,128)S(1)}, s32[20,3]{0,1:T(4,128)}, u32[]{:S(2)}) copy-start(s32[20,3]{0,1:T(4,128)} %param.11) | copy-start | bytes 724
  3.5 6.1 %copy-start = (bf16[2,3,80,2560]{3,2,1,0:T(8,128)(2,1)S(1)}, bf16[2,3,80,2560]{3,2,1,0:T(8,128)(2,1)}, u32[]{:S(2)}) copy-start(bf16[2,3,80,2560]{3,2,1,0:T(8,128)(2,1)} %refs_5_) | copy-start | bytes 7372804
  6.5 1.7 %copy-start.1 = (bf16[2,3,80,2560]{3,2,1,0:T(8,128)(2,1)S(1)}, bf16[2,3,80,2560]{3,2,1,0:T(8,128)(2,1)}, u32[]{:S(2)}) copy-start(bf16[2,3,80,2560]{3,2,1,0:T(8,128)(2,1)} %refs_4_) | copy-start | bytes 7372804
  9.6 1.7 %copy-start.3 = (bf16[2,3,80,2560]{3,2,1,0:T(8,128)(2,1)S(1)}, bf16[2,3,80,2560]{3,2,1,0:T(8,128)(2,1)}, u32[]{:S(2)}) copy-start(bf16[2,3,80,2560]{3,2,1,0:T(8,128)(2,1)} %refs_6_.1) | copy-start | bytes 7372804
  12.7 13.1 %copy-start.4 = (bf16[2,3,80,2560]{3,2,1,0:T(8,128)(2,1)S(1)}, bf16[2,3,80,2560]{3,2,1,0:T(8,128)(2,1)}, u32[]{:S(2)}) copy-start(bf16[2,3,80,2560]{3,2,1,0:T(8,128)(2,1)} %refs_6_.1) | copy-start | bytes 7372804
  12.7 22.0 %collective-permute-start.8 = (bf16[10,2,2,80,128]{4,3,2,1,0:T(8,128)(2,1)S(1)}, bf16[10,2,2,80,128]{4,3,2,1,0:T(8,128)(2,1)S(1)}, u32[]{:S(2)}, u32[]{:S(2)}) collective-permute-start(bf16[10,2,2,80,128]{4,3,2,1,0:T(8,128)(2,1)S(1)} %get-tuple-element.32), channel_id=1, source_target_pairs={{0,2},{4,6},{8,10},{12,14},{16,18},{20,22},{24,26},{28,30},{2,0},{... | collective-permute-start | bytes 2457608 | tf_op jit(solution)/shard_map/ppermute | solution.py:544
  14.4 15.6 %collective-permute-start.6 = (bf16[10,240,128]{2,1,0:T(8,128)(2,1)S(1)}, bf16[10,240,128]{2,1,0:T(8,128)(2,1)S(1)}, u32[]{:S(2)}, u32[]{:S(2)}) collective-permute-start(bf16[10,240,128]{2,1,0:T(8,128)(2,1)S(1)} %get-tuple-element.47), channel_id=1, source_target_pairs={{0,32},{64,96},{128,160},{192,224},{32,0},{96,64},{160,128},{224,1... | collective-permute-start | bytes 1843208 | tf_op jit(solution)/shard_map/ppermute | solution.py:544
  14.5 19.9 %collective-permute-start.7 = (bf16[10,240,128]{2,1,0:T(8,128)(2,1)S(1)}, bf16[10,240,128]{2,1,0:T(8,128)(2,1)S(1)}, u32[]{:S(2)}, u32[]{:S(2)}) collective-permute-start(bf16[10,240,128]{2,1,0:T(8,128)(2,1)S(1)} %get-tuple-element.48), channel_id=1, source_target_pairs={{32,64},{96,128},{160,192},{64,32},{128,96},{192,160},{33,65},{97,... | collective-permute-start | bytes 1843208 | tf_op jit(solution)/shard_map/ppermute | solution.py:544
  20.1 25.2 %collective-permute-start.9 = (bf16[10,2,2,80,128]{4,3,2,1,0:T(8,128)(2,1)S(1)}, bf16[10,2,2,80,128]{4,3,2,1,0:T(8,128)(2,1)S(1)}, u32[]{:S(2)}, u32[]{:S(2)}) collective-permute-start(bf16[10,2,2,80,128]{4,3,2,1,0:T(8,128)(2,1)S(1)} %get-tuple-element.33), channel_id=1, source_target_pairs={{2,4},{6,8},{10,12},{14,16},{18,20},{22,24},{26,28},{4,2},{8,6},{1... | collective-permute-start | bytes 2457608 | tf_op jit(solution)/shard_map/ppermute | solution.py:544
  25.8 19.5 %copy-start.2 = (bf16[2,3,80,2560]{3,2,1,0:T(8,128)(2,1)S(1)}, bf16[2,3,80,2560]{3,2,1,0:T(8,128)(2,1)}, u32[]{:S(2)}) copy-start(bf16[2,3,80,2560]{3,2,1,0:T(8,128)(2,1)} %refs_4_) | copy-start | bytes 7372804
  27.3 34.5 %collective-permute-start = (bf16[10,2,2,80,128]{4,3,2,1,0:T(8,128)(2,1)S(1)}, bf16[10,2,2,80,128]{4,3,2,1,0:T(8,128)(2,1)S(1)}, u32[]{:S(2)}, u32[]{:S(2)}) collective-permute-start(bf16[10,2,2,80,128]{4,3,2,1,0:T(8,128)(2,1)S(1)} %get-tuple-element.38), channel_id=1, source_target_pairs={{0,2},{4,6},{8,10},{12,14},{16,18},{20,22},{24,26},{28,30},{2,0},{... | collective-permute-start | bytes 2457608 | tf_op jit(solution)/shard_map/ppermute | solution.py:544
  30.0 31.7 %collective-permute-start.1 = (bf16[10,2,2,80,128]{4,3,2,1,0:T(8,128)(2,1)S(1)}, bf16[10,2,2,80,128]{4,3,2,1,0:T(8,128)(2,1)S(1)}, u32[]{:S(2)}, u32[]{:S(2)}) collective-permute-start(bf16[10,2,2,80,128]{4,3,2,1,0:T(8,128)(2,1)S(1)} %get-tuple-element.39), channel_id=1, source_target_pairs={{2,4},{6,8},{10,12},{14,16},{18,20},{22,24},{26,28},{4,2},{8,6},{1... | collective-permute-start | bytes 2457608 | tf_op jit(solution)/shard_map/ppermute | solution.py:544
  34.4 21.3 %collective-permute-start.2 = (bf16[10,240,128]{2,1,0:T(8,128)(2,1)S(1)}, bf16[10,240,128]{2,1,0:T(8,128)(2,1)S(1)}, u32[]{:S(2)}, u32[]{:S(2)}) collective-permute-start(bf16[10,240,128]{2,1,0:T(8,128)(2,1)S(1)} %get-tuple-element.43), channel_id=1, source_target_pairs={{0,32},{64,96},{128,160},{192,224},{32,0},{96,64},{160,128},{224,1... | collective-permute-start | bytes 1843208 | tf_op jit(solution)/shard_map/ppermute | solution.py:544
  34.8 27.0 %collective-permute-start.3 = (bf16[10,240,128]{2,1,0:T(8,128)(2,1)S(1)}, bf16[10,240,128]{2,1,0:T(8,128)(2,1)S(1)}, u32[]{:S(2)}, u32[]{:S(2)}) collective-permute-start(bf16[10,240,128]{2,1,0:T(8,128)(2,1)S(1)} %get-tuple-element.44), channel_id=1, source_target_pairs={{32,64},{96,128},{160,192},{64,32},{128,96},{192,160},{33,65},{97,... | collective-permute-start | bytes 1843208 | tf_op jit(solution)/shard_map/ppermute | solution.py:544
  55.6 26.6 %collective-permute-start.10 = (bf16[31,80,128]{2,1,0:T(8,128)(2,1)S(1)}, bf16[31,80,128]{2,1,0:T(8,128)(2,1)S(1)}, u32[]{:S(2)}, u32[]{:S(2)}) collective-permute-start(bf16[31,80,128]{2,1,0:T(8,128)(2,1)S(1)} %get-tuple-element.51), channel_id=1, source_target_pairs={{0,32},{64,96},{128,160},{192,224},{32,0},{96,64},{160,128},{224,1... | collective-permute-start | bytes 1904648 | tf_op jit(solution)/shard_map/ppermute | solution.py:544
  55.7 26.5 %collective-permute-start.11 = (bf16[31,80,128]{2,1,0:T(8,128)(2,1)S(1)}, bf16[31,80,128]{2,1,0:T(8,128)(2,1)S(1)}, u32[]{:S(2)}, u32[]{:S(2)}) collective-permute-start(bf16[31,80,128]{2,1,0:T(8,128)(2,1)S(1)} %get-tuple-element.52), channel_id=1, source_target_pairs={{32,64},{96,128},{160,192},{64,32},{128,96},{192,160},{33,65},{97,... | collective-permute-start | bytes 1904648 | tf_op jit(solution)/shard_map/ppermute | solution.py:544
  68.7 16.4 %collective-permute-start.4 = (bf16[31,80,128]{2,1,0:T(8,128)(2,1)S(1)}, bf16[31,80,128]{2,1,0:T(8,128)(2,1)S(1)}, u32[]{:S(2)}, u32[]{:S(2)}) collective-permute-start(bf16[31,80,128]{2,1,0:T(8,128)(2,1)S(1)} %get-tuple-element.45), channel_id=1, source_target_pairs={{0,32},{64,96},{128,160},{192,224},{32,0},{96,64},{160,128},{224,1... | collective-permute-start | bytes 1904648 | tf_op jit(solution)/shard_map/ppermute | solution.py:544
  68.8 18.0 %collective-permute-start.5 = (bf16[31,80,128]{2,1,0:T(8,128)(2,1)S(1)}, bf16[31,80,128]{2,1,0:T(8,128)(2,1)S(1)}, u32[]{:S(2)}, u32[]{:S(2)}) collective-permute-start(bf16[31,80,128]{2,1,0:T(8,128)(2,1)S(1)} %get-tuple-element.46), channel_id=1, source_target_pairs={{32,64},{96,128},{160,192},{64,32},{128,96},{192,160},{33,65},{97,... | collective-permute-start | bytes 1904648 | tf_op jit(solution)/shard_map/ppermute | solution.py:544

commit v7 on v6

--- a/solution.py
+++ b/solution.py
@@ -550,12 +550,12 @@
     chunks = ((0, FIRST), (FIRST, NH - FIRST))
     queries, rows = [], []
     for start, count in chunks:
-        packed = pack_queries(window, q, q_gain, q_inverse, start, count)
-        k, *packed = lax.optimization_barrier((k, *packed))
         packed_rows = pack_rows(window, k, v, k_gain, k_inverse, start, count)
         rows.append(exchange("height", *packed_rows))
+        q, *_ = lax.optimization_barrier((q, *packed_rows))
+        packed = pack_queries(window, q, q_gain, q_inverse, start, count)
         queries.append(exchange("frame", *packed))
-        q, *_ = lax.optimization_barrier((q, *packed_rows))
+        k, *_ = lax.optimization_barrier((k, *packed))
     (start, count), (late_start, late_count) = chunks
     part, *far, lse = both_partial(window, *queries[0], q, k, v, *norms, *rows[0], start, count)
     parts = [(part, lse, *exchange("frame", *far), start, count)]

time: 89.9 us -> 88.2 us (0.981)
  local copies, waits for them, and re-layouts: 3.76 us -> 2.06 us
    unnamed x17 -> x15, local copies, waits for them, and re-layouts: 3.51 us -> 1.81 us
  transfers between devices with their start and end apart: 12 -> 12, of which waited for: 3 -> 3; matrix products, arithmetic and copies ran while one was open for 0% -> 0% of each run, Pallas kernels for 34% -> 36%
where the time goes in v7:
time: 88.2 us; the launch traced here: 87.9 us
  Pallas kernels  36.2 us (41%)
  starting transfers between devices  34.3 us (39%)
  waiting for transfers between devices  9.04 us (10%)
  other arithmetic  3.65 us (4%)
  blocking collectives  2.5 us (3%)
  local copies, waits for them, and re-layouts  2.06 us (2%)
    ppermute x12, starting transfers between devices, exchange(): out.append(lax.ppermute(block, axis, pairs + [(b, a) for a, b in pairs]))  34.3 us
    pallas_call x2, Pallas kernels, partial_call(): pl.pallas_call(functools.partial(partial_kernel, far, start, group, steps...  14.7 us
    pallas_call x1, Pallas kernels, both_partial(): pl.pallas_call(functools.partial(both_kernel, start, group, steps), grid_...  10.3 us
    ppermute x12, waiting for transfers between devices, exchange(): out.append(lax.ppermute(block, axis, pairs + [(b, a) for a, b in pairs]))  9.04 us
    pallas_call x2, Pallas kernels, merge(): pl.pallas_call(functools.partial(merge_kernel, start, group), grid_spec=p...  5.69 us
    reduce_sum x1, other arithmetic, squares_of(): return jnp.sum(values * values, axis=-1)  3.64 us
    pallas_call x2, Pallas kernels, pack_rows(): pl.pallas_call(functools.partial(pack_rows_kernel, group), grid_spec=pltp...  2.79 us
    pallas_call x2, Pallas kernels, pack_queries(): pl.pallas_call(functools.partial(pack_queries_kernel, group), grid_spec=p...  2.63 us
  transfers between devices with their start and end apart: 12, of which 3 were waited for; matrix products, arithmetic and copies ran while one was open for 0% of the time, Pallas kernels for 36%

profile of v7, /device:TPU:38, one launch (start us, length us, event | category | flops | bytes accessed | tf_op | source)
XLA Modules:
  0.0 87.9 jit_solution(705170483031755613)
XLA Ops:
  0.0 3.6 %multiply_reduce_fusion = (f32[2,3,80]{2,1,0:T(4,128)S(1)}, f32[2,3,80]{2,1,0:T(4,128)S(1)}) fusion(bf16[2,3,80,2560]{3,2,1,0:T(8,128)(2,1)} %refs_4_, bf16[2,3,80,2560]{3,2,1,0:T(8,128)(2,1)} %refs_5_), kind=kLoop, calls=%fused_computation | loop fusion | flops 7371840 | bytes 4919040 | tf_op jit(solution)/shard_map/reduce_sum | solution.py:573
  3.6 2.5 %all-reduce = (f32[2,3,80]{2,1,0:T(4,128)S(1)}, f32[2,3,80]{2,1,0:T(4,128)S(1)}) all-reduce(f32[2,3,80]{2,1,0:T(4,128)S(1)} %get-tuple-element.48, f32[2,3,80]{2,1,0:T(4,128)S(1)} %get-tuple-element.47), channel_id=1, replica_groups=mesh['frame'=8,'height'=16,'head'=2] {'head'}, use_global_device_ids=true, to_apply=%region_1.0 | all-reduce | flops 960 | bytes 7680 | tf_op jit(solution)/shard_map/psum | solution.py:578
  6.2 0.1 copy.16.window
  6.3 0.1 broadcast_in_dim.8.inverse.kinverse.refs_1_
  6.4 0.0 copy-start.2
  6.4 1.7 %copy-done.2 = bf16[2,3,80,2560]{3,2,1,0:T(8,128)(2,1)S(1)} copy-done((bf16[2,3,80,2560]{3,2,1,0:T(8,128)(2,1)S(1)}, bf16[2,3,80,2560]{3,2,1,0:T(8,128)(2,1)}, u32[]{:S(2)}) %copy-start.2) | copy-done | bytes 2457624
  8.1 1.4 %pack_rows.2 = (bf16[10,2,2,80,128]{4,3,2,1,0:T(8,128)(2,1)S(1)}, bf16[10,2,2,80,128]{4,3,2,1,0:T(8,128)(2,1)S(1)}) custom-call(s32[20,3]{1,0:T(8,128)S(1)} %copy.16.window, bf16[2,3,80,2560]{3,2,1,0:T(8,128)(2,1)S(1)} %copy-done, bf16[2,3,80,2560]{3,2,1,0:T(8,128)(2,1)S(1)} %copy-done.2, f32[1,2560]{1,0:T(1,128)S(1)} %broadcast_in_dim.9.gain.kgain.refs_8_, ...), custom_call_target="tpu_custom_call" | custom-call | bytes 4500000 | tf_op jit(solution)/shard_map/pack_rows/pallas_call | solution.py:96
  9.5 1.7 %collective-permute-start.8 = (bf16[10,2,2,80,128]{4,3,2,1,0:T(8,128)(2,1)S(1)}, bf16[10,2,2,80,128]{4,3,2,1,0:T(8,128)(2,1)S(1)}, u32[]{:S(2)}, u32[]{:S(2)}) collective-permute-start(bf16[10,2,2,80,128]{4,3,2,1,0:T(8,128)(2,1)S(1)} %get-tuple-element.25), channel_id=1, source_target_pairs={{0,2},{4,6},{8,10},{12,14},{16,18},{20,22},{24,26},{28,30},{2,0},{... | collective-permute-start | bytes 2457608 | tf_op jit(solution)/shard_map/ppermute | solution.py:544
  11.2 0.1 broadcast_in_dim.21.inverse.refs_2_.refs_0_
  11.3 1.3 %pack_queries.2 = (bf16[10,240,128]{2,1,0:T(8,128)(2,1)S(1)}, bf16[10,240,128]{2,1,0:T(8,128)(2,1)S(1)}) custom-call(s32[20,3]{1,0:T(8,128)S(1)} %copy.16.window, bf16[2,3,80,2560]{3,2,1,0:T(8,128)(2,1)S(1)} %copy-done.1, f32[1,2560]{1,0:T(1,128)S(1)} %broadcast_in_dim.20.gain.refs_1_.refs_7_, f32[2,3,80,128]{3,2,1,0:T(8,128)S(1)} %broadcast_in_dim.21.inverse.refs_2_.refs_0_), custom_call_target="tpu_custom_call" | custom-call | bytes 3000000 | tf_op jit(solution)/shard_map/pack_queries/pallas_call | solution.py:77
  12.7 0.2 collective-permute-start.6
  12.9 5.6 %collective-permute-start.7 = (bf16[10,240,128]{2,1,0:T(8,128)(2,1)S(1)}, bf16[10,240,128]{2,1,0:T(8,128)(2,1)S(1)}, u32[]{:S(2)}, u32[]{:S(2)}) collective-permute-start(bf16[10,240,128]{2,1,0:T(8,128)(2,1)S(1)} %get-tuple-element.29), channel_id=1, source_target_pairs={{32,64},{96,128},{160,192},{64,32},{128,96},{192,160},{33,65},{97,... | collective-permute-start | bytes 1843208 | tf_op jit(solution)/shard_map/ppermute | solution.py:544
  18.5 4.4 %collective-permute-start.9 = (bf16[10,2,2,80,128]{4,3,2,1,0:T(8,128)(2,1)S(1)}, bf16[10,2,2,80,128]{4,3,2,1,0:T(8,128)(2,1)S(1)}, u32[]{:S(2)}, u32[]{:S(2)}) collective-permute-start(bf16[10,2,2,80,128]{4,3,2,1,0:T(8,128)(2,1)S(1)} %get-tuple-element.26), channel_id=1, source_target_pairs={{2,4},{6,8},{10,12},{14,16},{18,20},{22,24},{26,28},{4,2},{8,6},{1... | collective-permute-start | bytes 2457608 | tf_op jit(solution)/shard_map/ppermute | solution.py:544
  22.8 1.4 %pack_rows.3 = (bf16[10,2,2,80,128]{4,3,2,1,0:T(8,128)(2,1)S(1)}, bf16[10,2,2,80,128]{4,3,2,1,0:T(8,128)(2,1)S(1)}) custom-call(s32[20,3]{1,0:T(8,128)S(1)} %copy.16.window, bf16[2,3,80,2560]{3,2,1,0:T(8,128)(2,1)S(1)} %copy-done, bf16[2,3,80,2560]{3,2,1,0:T(8,128)(2,1)S(1)} %copy-done.2, f32[1,2560]{1,0:T(1,128)S(1)} %broadcast_in_dim.9.gain.kgain.refs_8_, ...), custom_call_target="tpu_custom_call" | custom-call | bytes 4500000 | tf_op jit(solution)/shard_map/pack_rows/pallas_call | solution.py:96
  24.3 0.0 copy-start.3
  24.3 0.5 collective-permute-start
  24.8 3.6 %collective-permute-done.6.refs_2_ = bf16[10,240,128]{2,1,0:T(8,128)(2,1)S(1)} collective-permute-done((bf16[10,240,128]{2,1,0:T(8,128)(2,1)S(1)}, bf16[10,240,128]{2,1,0:T(8,128)(2,1)S(1)}, u32[]{:S(2)}, u32[]{:S(2)}) %collective-permute-start.6) | collective-permute-done | bytes 614432 | tf_op jit(solution)/shard_map/ppermute | solution.py:544
  28.4 4.3 %collective-permute-start.1 = (bf16[10,2,2,80,128]{4,3,2,1,0:T(8,128)(2,1)S(1)}, bf16[10,2,2,80,128]{4,3,2,1,0:T(8,128)(2,1)S(1)}, u32[]{:S(2)}, u32[]{:S(2)}) collective-permute-start(bf16[10,2,2,80,128]{4,3,2,1,0:T(8,128)(2,1)S(1)} %get-tuple-element.32), channel_id=1, source_target_pairs={{2,4},{6,8},{10,12},{14,16},{18,20},{22,24},{26,28},{4,2},{8,6},{1... | collective-permute-start | bytes 2457608 | tf_op jit(solution)/shard_map/ppermute | solution.py:544
  32.7 1.3 %pack_queries.3 = (bf16[10,240,128]{2,1,0:T(8,128)(2,1)S(1)}, bf16[10,240,128]{2,1,0:T(8,128)(2,1)S(1)}) custom-call(s32[20,3]{1,0:T(8,128)S(1)} %copy.16.window, bf16[2,3,80,2560]{3,2,1,0:T(8,128)(2,1)S(1)} %copy-done.1, f32[1,2560]{1,0:T(1,128)S(1)} %broadcast_in_dim.20.gain.refs_1_.refs_7_, f32[2,3,80,128]{3,2,1,0:T(8,128)S(1)} %broadcast_in_dim.21.inverse.refs_2_.refs_0_), custom_call_target="tpu_custom_call" | custom-call | bytes 3000000 | tf_op jit(solution)/shard_map/pack_queries/pallas_call | solution.py:77
  34.1 0.4 collective-permute-start.2
  34.5 5.4 %collective-permute-start.3 = (bf16[10,240,128]{2,1,0:T(8,128)(2,1)S(1)}, bf16[10,240,128]{2,1,0:T(8,128)(2,1)S(1)}, u32[]{:S(2)}, u32[]{:S(2)}) collective-permute-start(bf16[10,240,128]{2,1,0:T(8,128)(2,1)S(1)} %get-tuple-element.35), channel_id=1, source_target_pairs={{32,64},{96,128},{160,192},{64,32},{128,96},{192,160},{33,65},{97,... | collective-permute-start | bytes 1843208 | tf_op jit(solution)/shard_map/ppermute | solution.py:544
  39.9 3.8 %collective-permute-done.9.refs_10_ = bf16[10,2,2,80,128]{4,3,2,1,0:T(8,128)(2,1)S(1)} collective-permute-done((bf16[10,2,2,80,128]{4,3,2,1,0:T(8,128)(2,1)S(1)}, bf16[10,2,2,80,128]{4,3,2,1,0:T(8,128)(2,1)S(1)}, u32[]{:S(2)}, u32[]{:S(2)}) %collective-permute-start.9) | collective-permute-done | bytes 819232 | tf_op jit(solution)/shard_map/ppermute | solution.py:544
  43.7 10.3 %both_partial.1 = (bf16[10,2,3,80,128]{4,3,2,1,0:T(8,128)(2,1)S(1)}, bf16[31,80,128]{2,1,0:T(8,128)(2,1)S(1)}, bf16[31,80,128]{2,1,0:T(8,128)(2,1)S(1)}, f32[2,240,128]{2,1,0:T(8,128)S(1)}) custom-call(s32[20,3]{1,0:T(8,128)S(1)} %copy.16.window, f32[2,3,80,128]{3,2,1,0:T(8,128)S(1)} %broadcast_in_dim.21.inverse.refs_2_.refs_0_, ...), custom_call_target="tpu_custom_call" | custom-call | bytes 33000000 | tf_op jit(solution)/shard_map/both_partial/pallas_call | solution.py:460
  54.0 0.1 collective-permute-start.10
  54.1 6.0 %collective-permute-start.11 = (bf16[31,80,128]{2,1,0:T(8,128)(2,1)S(1)}, bf16[31,80,128]{2,1,0:T(8,128)(2,1)S(1)}, u32[]{:S(2)}, u32[]{:S(2)}) collective-permute-start(bf16[31,80,128]{2,1,0:T(8,128)(2,1)S(1)} %get-tuple-element.44), channel_id=1, source_target_pairs={{32,64},{96,128},{160,192},{64,32},{128,96},{192,160},{33,65},{97,... | collective-permute-start | bytes 1904648 | tf_op jit(solution)/shard_map/ppermute | solution.py:544
  60.2 6.9 %far_partial.1 = (bf16[31,80,128]{2,1,0:T(8,128)(2,1)S(1)}, bf16[31,80,128]{2,1,0:T(8,128)(2,1)S(1)}) custom-call(s32[20,3]{1,0:T(8,128)S(1)} %copy.16.window, f32[2,3,80,128]{3,2,1,0:T(8,128)S(1)} %broadcast_in_dim.8.inverse.kinverse.refs_1_, bf16[2,3,80,2560]{3,2,1,0:T(8,128)(2,1)S(1)} %copy-done, bf16[2,3,80,2560]{3,2,1,0:T(8,128)(2,1)S(1)} %copy-done.3, ...), custom_call_target="tpu_custom_call" | custom-call | bytes 18000000 | tf_op jit(solution)/shard_map/far_partial/pallas_call | solution.py:348
  67.0 0.1 collective-permute-start.4
  67.1 5.6 %collective-permute-start.5 = (bf16[31,80,128]{2,1,0:T(8,128)(2,1)S(1)}, bf16[31,80,128]{2,1,0:T(8,128)(2,1)S(1)}, u32[]{:S(2)}, u32[]{:S(2)}) collective-permute-start(bf16[31,80,128]{2,1,0:T(8,128)(2,1)S(1)} %get-tuple-element.40), channel_id=1, source_target_pairs={{32,64},{96,128},{160,192},{64,32},{128,96},{192,160},{33,65},{97,... | collective-permute-start | bytes 1904648 | tf_op jit(solution)/shard_map/ppermute | solution.py:544
  72.7 7.9 %own_partial.1 = (bf16[10,2,3,80,128]{4,3,2,1,0:T(8,128)(2,1)S(1)}, f32[2,240,128]{2,1,0:T(8,128)S(1)}) custom-call(s32[20,3]{1,0:T(8,128)S(1)} %copy.16.window, f32[2,3,80,128]{3,2,1,0:T(8,128)S(1)} %broadcast_in_dim.8.inverse.kinverse.refs_1_, bf16[2,3,80,2560]{3,2,1,0:T(8,128)(2,1)S(1)} %copy-done, bf16[2,3,80,2560]{3,2,1,0:T(8,128)(2,1)S(1)} %copy-done.3, ...), custom_call_target="tpu_custom_call" | custom-call | bytes 18000000 | tf_op jit(solution)/shard_map/own_partial/pallas_call | solution.py:348
  80.6 2.8 %merge.2.refs_0_ = bf16[2,3,80,2560]{3,2,1,0:T(8,128)(2,1)} custom-call(s32[20,3]{1,0:T(8,128)S(1)} %copy.16.window, bf16[10,2,3,80,128]{4,3,2,1,0:T(8,128)(2,1)S(1)} %get-tuple-element.41.part, f32[2,240,128]{2,1,0:T(8,128)S(1)} %get-tuple-element.42.lse, bf16[31,80,128]{2,1,0:T(8,128)(2,1)S(1)} %collective-permute-done.10.ob.sb, ...), custom_call_target="tpu_custom_call" | custom-call | bytes 7500000 | tf_op jit(solution)/shard_map/merge/pallas_call | solution.py:515
  83.5 1.6 %collective-permute-done.5.oa.sa = bf16[31,80,128]{2,1,0:T(8,128)(2,1)S(1)} collective-permute-done((bf16[31,80,128]{2,1,0:T(8,128)(2,1)S(1)}, bf16[31,80,128]{2,1,0:T(8,128)(2,1)S(1)}, u32[]{:S(2)}, u32[]{:S(2)}) %collective-permute-start.5) | collective-permute-done | bytes 634912 | tf_op jit(solution)/shard_map/ppermute | solution.py:544
  85.1 2.8 %merge.3 = bf16[2,3,80,2560]{3,2,1,0:T(8,128)(2,1)} custom-call(s32[20,3]{1,0:T(8,128)S(1)} %copy.16.window, bf16[10,2,3,80,128]{4,3,2,1,0:T(8,128)(2,1)S(1)} %get-tuple-element.37.part, f32[2,240,128]{2,1,0:T(8,128)S(1)} %get-tuple-element.38.lse, bf16[31,80,128]{2,1,0:T(8,128)(2,1)S(1)} %collective-permute-done.4.ob.sb, ...), custom_call_target="tpu_custom_call", output_to_operand_aliasing={{}: (7, {})} | custom-call | bytes 7500000 | tf_op jit(solution)/shard_map/merge/pallas_call | solution.py:515
  (24 shorter events, 0.1 us)
Async XLA Ops:
  0.0 6.4 %copy-start = (bf16[2,3,80,2560]{3,2,1,0:T(8,128)(2,1)S(1)}, bf16[2,3,80,2560]{3,2,1,0:T(8,128)(2,1)}, u32[]{:S(2)}) copy-start(bf16[2,3,80,2560]{3,2,1,0:T(8,128)(2,1)} %refs_5_) | copy-start | bytes 7372804
  0.0 6.2 %copy-start.4 = (f32[2560]{0:T(1024)S(1)}, f32[2560]{0:T(1024)}, u32[]{:S(2)}) copy-start(f32[2560]{0:T(1024)} %param.10) | copy-start | bytes 30724
  0.0 6.2 %copy-start.6 = (s32[20,3]{0,1:T(4,128)S(1)}, s32[20,3]{0,1:T(4,128)}, u32[]{:S(2)}) copy-start(s32[20,3]{0,1:T(4,128)} %param.11) | copy-start | bytes 724
  6.4 1.7 %copy-start.2 = (bf16[2,3,80,2560]{3,2,1,0:T(8,128)(2,1)S(1)}, bf16[2,3,80,2560]{3,2,1,0:T(8,128)(2,1)}, u32[]{:S(2)}) copy-start(bf16[2,3,80,2560]{3,2,1,0:T(8,128)(2,1)} %refs_6_.1) | copy-start | bytes 7372804
  8.1 3.1 %copy-start.5 = (f32[2560]{0:T(1024)S(1)}, f32[2560]{0:T(1024)}, u32[]{:S(2)}) copy-start(f32[2560]{0:T(1024)} %param.9) | copy-start | bytes 30724
  8.1 3.2 %copy-start.1 = (bf16[2,3,80,2560]{3,2,1,0:T(8,128)(2,1)S(1)}, bf16[2,3,80,2560]{3,2,1,0:T(8,128)(2,1)}, u32[]{:S(2)}) copy-start(bf16[2,3,80,2560]{3,2,1,0:T(8,128)(2,1)} %refs_4_) | copy-start | bytes 7372804
  9.5 24.9 %collective-permute-start.8 = (bf16[10,2,2,80,128]{4,3,2,1,0:T(8,128)(2,1)S(1)}, bf16[10,2,2,80,128]{4,3,2,1,0:T(8,128)(2,1)S(1)}, u32[]{:S(2)}, u32[]{:S(2)}) collective-permute-start(bf16[10,2,2,80,128]{4,3,2,1,0:T(8,128)(2,1)S(1)} %get-tuple-element.25), channel_id=1, source_target_pairs={{0,2},{4,6},{8,10},{12,14},{16,18},{20,22},{24,26},{28,30},{2,0},{... | collective-permute-start | bytes 2457608 | tf_op jit(solution)/shard_map/ppermute | solution.py:544
  12.7 15.7 %collective-permute-start.6 = (bf16[10,240,128]{2,1,0:T(8,128)(2,1)S(1)}, bf16[10,240,128]{2,1,0:T(8,128)(2,1)S(1)}, u32[]{:S(2)}, u32[]{:S(2)}) collective-permute-start(bf16[10,240,128]{2,1,0:T(8,128)(2,1)S(1)} %get-tuple-element.28), channel_id=1, source_target_pairs={{0,32},{64,96},{128,160},{192,224},{32,0},{96,64},{160,128},{224,1... | collective-permute-start | bytes 1843208 | tf_op jit(solution)/shard_map/ppermute | solution.py:544
  12.9 21.2 %collective-permute-start.7 = (bf16[10,240,128]{2,1,0:T(8,128)(2,1)S(1)}, bf16[10,240,128]{2,1,0:T(8,128)(2,1)S(1)}, u32[]{:S(2)}, u32[]{:S(2)}) collective-permute-start(bf16[10,240,128]{2,1,0:T(8,128)(2,1)S(1)} %get-tuple-element.29), channel_id=1, source_target_pairs={{32,64},{96,128},{160,192},{64,32},{128,96},{192,160},{33,65},{97,... | collective-permute-start | bytes 1843208 | tf_op jit(solution)/shard_map/ppermute | solution.py:544
  18.5 25.2 %collective-permute-start.9 = (bf16[10,2,2,80,128]{4,3,2,1,0:T(8,128)(2,1)S(1)}, bf16[10,2,2,80,128]{4,3,2,1,0:T(8,128)(2,1)S(1)}, u32[]{:S(2)}, u32[]{:S(2)}) collective-permute-start(bf16[10,2,2,80,128]{4,3,2,1,0:T(8,128)(2,1)S(1)} %get-tuple-element.26), channel_id=1, source_target_pairs={{2,4},{6,8},{10,12},{14,16},{18,20},{22,24},{26,28},{4,2},{8,6},{1... | collective-permute-start | bytes 2457608 | tf_op jit(solution)/shard_map/ppermute | solution.py:544
  24.3 19.4 %copy-start.3 = (bf16[2,3,80,2560]{3,2,1,0:T(8,128)(2,1)S(1)}, bf16[2,3,80,2560]{3,2,1,0:T(8,128)(2,1)}, u32[]{:S(2)}) copy-start(bf16[2,3,80,2560]{3,2,1,0:T(8,128)(2,1)} %refs_6_.1) | copy-start | bytes 7372804
  24.3 35.9 %collective-permute-start = (bf16[10,2,2,80,128]{4,3,2,1,0:T(8,128)(2,1)S(1)}, bf16[10,2,2,80,128]{4,3,2,1,0:T(8,128)(2,1)S(1)}, u32[]{:S(2)}, u32[]{:S(2)}) collective-permute-start(bf16[10,2,2,80,128]{4,3,2,1,0:T(8,128)(2,1)S(1)} %get-tuple-element.31), channel_id=1, source_target_pairs={{0,2},{4,6},{8,10},{12,14},{16,18},{20,22},{24,26},{28,30},{2,0},{... | collective-permute-start | bytes 2457608 | tf_op jit(solution)/shard_map/ppermute | solution.py:544
  28.4 31.8 %collective-permute-start.1 = (bf16[10,2,2,80,128]{4,3,2,1,0:T(8,128)(2,1)S(1)}, bf16[10,2,2,80,128]{4,3,2,1,0:T(8,128)(2,1)S(1)}, u32[]{:S(2)}, u32[]{:S(2)}) collective-permute-start(bf16[10,2,2,80,128]{4,3,2,1,0:T(8,128)(2,1)S(1)} %get-tuple-element.32), channel_id=1, source_target_pairs={{2,4},{6,8},{10,12},{14,16},{18,20},{22,24},{26,28},{4,2},{8,6},{1... | collective-permute-start | bytes 2457608 | tf_op jit(solution)/shard_map/ppermute | solution.py:544
  34.1 20.0 %collective-permute-start.2 = (bf16[10,240,128]{2,1,0:T(8,128)(2,1)S(1)}, bf16[10,240,128]{2,1,0:T(8,128)(2,1)S(1)}, u32[]{:S(2)}, u32[]{:S(2)}) collective-permute-start(bf16[10,240,128]{2,1,0:T(8,128)(2,1)S(1)} %get-tuple-element.34), channel_id=1, source_target_pairs={{0,32},{64,96},{128,160},{192,224},{32,0},{96,64},{160,128},{224,1... | collective-permute-start | bytes 1843208 | tf_op jit(solution)/shard_map/ppermute | solution.py:544
  34.5 25.7 %collective-permute-start.3 = (bf16[10,240,128]{2,1,0:T(8,128)(2,1)S(1)}, bf16[10,240,128]{2,1,0:T(8,128)(2,1)S(1)}, u32[]{:S(2)}, u32[]{:S(2)}) collective-permute-start(bf16[10,240,128]{2,1,0:T(8,128)(2,1)S(1)} %get-tuple-element.35), channel_id=1, source_target_pairs={{32,64},{96,128},{160,192},{64,32},{128,96},{192,160},{33,65},{97,... | collective-permute-start | bytes 1843208 | tf_op jit(solution)/shard_map/ppermute | solution.py:544
  54.0 26.6 %collective-permute-start.10 = (bf16[31,80,128]{2,1,0:T(8,128)(2,1)S(1)}, bf16[31,80,128]{2,1,0:T(8,128)(2,1)S(1)}, u32[]{:S(2)}, u32[]{:S(2)}) collective-permute-start(bf16[31,80,128]{2,1,0:T(8,128)(2,1)S(1)} %get-tuple-element.43), channel_id=1, source_target_pairs={{0,32},{64,96},{128,160},{192,224},{32,0},{96,64},{160,128},{224,1... | collective-permute-start | bytes 1904648 | tf_op jit(solution)/shard_map/ppermute | solution.py:544
  54.1 26.5 %collective-permute-start.11 = (bf16[31,80,128]{2,1,0:T(8,128)(2,1)S(1)}, bf16[31,80,128]{2,1,0:T(8,128)(2,1)S(1)}, u32[]{:S(2)}, u32[]{:S(2)}) collective-permute-start(bf16[31,80,128]{2,1,0:T(8,128)(2,1)S(1)} %get-tuple-element.44), channel_id=1, source_target_pairs={{32,64},{96,128},{160,192},{64,32},{128,96},{192,160},{33,65},{97,... | collective-permute-start | bytes 1904648 | tf_op jit(solution)/shard_map/ppermute | solution.py:544
  67.0 16.4 %collective-permute-start.4 = (bf16[31,80,128]{2,1,0:T(8,128)(2,1)S(1)}, bf16[31,80,128]{2,1,0:T(8,128)(2,1)S(1)}, u32[]{:S(2)}, u32[]{:S(2)}) collective-permute-start(bf16[31,80,128]{2,1,0:T(8,128)(2,1)S(1)} %get-tuple-element.39), channel_id=1, source_target_pairs={{0,32},{64,96},{128,160},{192,224},{32,0},{96,64},{160,128},{224,1... | collective-permute-start | bytes 1904648 | tf_op jit(solution)/shard_map/ppermute | solution.py:544
  67.1 18.0 %collective-permute-start.5 = (bf16[31,80,128]{2,1,0:T(8,128)(2,1)S(1)}, bf16[31,80,128]{2,1,0:T(8,128)(2,1)S(1)}, u32[]{:S(2)}, u32[]{:S(2)}) collective-permute-start(bf16[31,80,128]{2,1,0:T(8,128)(2,1)S(1)} %get-tuple-element.40), channel_id=1, source_target_pairs={{32,64},{96,128},{160,192},{64,32},{128,96},{192,160},{33,65},{97,... | collective-permute-start | bytes 1904648 | tf_op jit(solution)/shard_map/ppermute | solution.py:544
